TPU v7x, 256 devices: a whole 4x4x8 slice. The times are simulated.
256 devices in a mesh: gx: 8 (over x, y_lo), gy: 32 (over y_hi, z, core).
Axes of the slice: x: 4, y: 4 (y_hi: 2, y_lo: 2; y = y_hi * 2 + y_lo), z: 8, core: 2. Of those that a mesh axis runs over, the one named last changes fastest.
Arguments:
- positions: float32 [3, 8, 32, 2940], P(None, 'gx', 'gy'), may hold values from 0 to 480, as said below
- species: int32 [8, 32, 2940], P('gx', 'gy'), may hold values from 0 to 4
- mig_rows: int32 [8, 32, 8, 64], P('gx', 'gy'), may hold values from 0 to 2940, as said below
- ghost_rows: int32 [8, 32, 8, 1260], P('gx', 'gy'), may hold values from 0 to 3452, as said below
- edge_center: int32 [8, 32, 512], P('gx', 'gy'), may hold values from 0 to 2939, as said below
- edge_neighbor: int32 [8, 32, 512], P('gx', 'gy'), may hold values from 0 to 13531, as said below
- edge_blocks: int32 [8, 32], P('gx', 'gy'), may hold values from 1 to 4, as said below
- w_radial: float32 [8, 256], replicated, may hold values from -2 to 2
- w_kind_center: float32 [4, 256], replicated, may hold values from -4 to 4
- w_kind_neigh: float32 [4, 256], replicated, may hold values from -4 to 4
- w_two: bfloat16 [256, 256], replicated, may hold values from -0.375 to 0.375
- w_edge: bfloat16 [2, 256, 192], replicated, may hold values from -1.5 to 1.5
- w_env: bfloat16 [2, 256, 192], replicated, may hold values from -1.5 to 1.5
- w_update: bfloat16 [2, 448, 256], replicated, may hold values from -0.25 to 0.25
- w_out: bfloat16 [256], replicated, may hold values from -0.375 to 0.375
Outputs:
- owned_positions: float32 [3, 8, 32, 3452], P(None, 'gx', 'gy')
- forces: float32 [3, 8, 32, 3452], P(None, 'gx', 'gy')
- atom_energy: float32 [8, 32, 3452], P('gx', 'gy')
Inputs may be any that keep to these rules, and one draw needn't show every extreme that they name: `mig_rows`: each domain's lists name its own slots, each at most once over all eight directions; the value 2940 marks an empty entry and is in every list; no list points off the grid. `ghost_rows`: slots after migration, distinct within a direction; the value 3452 marks an empty entry. `edge_center`: slots of the domain's atoms before migration. `edge_neighbor`: never equal to the edge's center; a slot of the extended list. `edge_blocks`: edges of blocks at or beyond this count are padding; some domain has all 4 blocks live. `positions`: x lies in the domain's column of width 15, y in its row of width 15, z between 0 and 15 * 60 / 7.
All inputs are finite; a program needn't handle non-finite values.
Results may differ from a plain program's by a relative error of at most 0.015.
Values sent between devices are 32-bit elements; how exact they have to be, the bound alone decides.
No kernel may reach another device: no remote copies, remote signals or barrier semaphores. Data moves between devices by JAX's collectives and lax.ppermute only.
A program may use at most 64 MiB of HBM per device.

v0:
```python
import math

import jax
import jax.numpy as jnp
from jax import lax
from jax.sharding import PartitionSpec as P

DEGREE_OF = (0, 1, 1, 1, 2, 2, 2, 2, 2)
CUTOFF = 6.0
SOFTENING = 0.01
BASIS_WIDTH = 0.8
ENV_SCALE = 0.3


def extended_2(cells, sides, width):
    for axis, dim in sides:
        count = lax.axis_size(axis)
        ends = count - 1
        head = lax.slice_in_dim(cells, 0, width, axis=dim)
        tail = lax.slice_in_dim(cells, cells.shape[dim] - width, cells.shape[dim], axis=dim)
        cells = jnp.concatenate(
            [
                lax.ppermute(tail, axis, [(i, (i + 1) % count) for i in range(ends)]),
                cells,
                lax.ppermute(head, axis, [((i + 1) % count, i) for i in range(ends)]),
            ],
            axis=dim,
        )
    return cells


def harmonics(unit):
    ux, uy, uz = (unit[0], unit[1], unit[2])
    square = ux * ux + uy * uy + uz * uz
    root3 = math.sqrt(3.0)
    root15 = math.sqrt(15.0)
    cols = [
        jnp.ones_like(ux),
        root3 * ux,
        root3 * uy,
        root3 * uz,
        root15 * ux * uy,
        root15 * uy * uz,
        root15 * ux * uz,
        0.5 * math.sqrt(5.0) * (3.0 * uz * uz - square),
        0.5 * root15 * (ux * ux - uy * uy),
    ]
    return jnp.stack(cols, 1)


def local_energy(
    ext_pos,
    ext_kind,
    center,
    neighbor,
    live_blocks,
    n_own,
    w_radial,
    w_kind_center,
    w_kind_neigh,
    w_two,
    w_edge,
    w_env,
    w_update,
    w_out,
):
    edges = center.shape[0]
    chans = w_edge.shape[2] // 3
    nspec = w_kind_center.shape[0]
    nrad = w_radial.shape[0]
    delta = ext_pos[:, neighbor] - ext_pos[:, center]
    radius = jnp.sqrt(jnp.sum(delta * delta, 0) + SOFTENING)
    kind_c = ext_kind[center]
    kind_n = ext_kind[neighbor]
    block_live = jnp.arange(edges, dtype=jnp.int32) // 128 < live_blocks
    live = (
        block_live.astype(jnp.float32)
        * (kind_c > 0.5).astype(jnp.float32)
        * (kind_n > 0.5).astype(jnp.float32)
    )
    envelope = live * jnp.square(jnp.maximum(0.0, 1.0 - radius * radius / (CUTOFF * CUTOFF)))
    sph = harmonics(delta / CUTOFF)
    centers_mu = jnp.arange(nrad, dtype=jnp.float32) * (CUTOFF / (nrad - 1))
    radial = jnp.exp(-jnp.square((radius[:, None] - centers_mu[None, :]) / BASIS_WIDTH))
    ids = jnp.arange(1, nspec + 1, dtype=jnp.float32)
    onehot_c = (kind_c[:, None] == ids[None, :]).astype(jnp.float32)
    onehot_n = (kind_n[:, None] == ids[None, :]).astype(jnp.float32)
    high = lax.Precision.HIGHEST
    shared_center = (center[:, None] == center[None, :]).astype(jnp.float32)
    pre = (
        jnp.dot(radial, w_radial, precision=high)
        + jnp.dot(onehot_c, w_kind_center, precision=high)
        + jnp.dot(onehot_n, w_kind_neigh, precision=high)
    )
    hidden = jax.nn.silu(pre).astype(jnp.bfloat16)
    latent = (
        jax.nn.silu(jnp.dot(hidden, w_two, preferred_element_type=jnp.float32)) * envelope[:, None]
    )
    for layer in range(w_edge.shape[0]):
        latent_b = latent.astype(jnp.bfloat16)
        edge_mix = jnp.dot(latent_b, w_edge[layer], preferred_element_type=jnp.float32)
        env_mix = jnp.dot(latent_b, w_env[layer], preferred_element_type=jnp.float32)
        terms = jnp.concatenate(
            [
                env_mix[:, DEGREE_OF[comp] * chans : (DEGREE_OF[comp] + 1) * chans]
                * sph[:, comp : comp + 1]
                for comp in range(9)
            ],
            1,
        )
        env_at = jnp.dot(shared_center, terms, precision=high) * ENV_SCALE
        groups = []
        for degree, (first, last) in enumerate(((0, 1), (1, 4), (4, 9))):
            weight_l = edge_mix[:, degree * chans : (degree + 1) * chans]
            acc = jnp.zeros((edges, chans), jnp.float32)
            for comp in range(first, last):
                acc = (
                    acc
                    + weight_l
                    * sph[:, comp : comp + 1]
                    * env_at[:, comp * chans : (comp + 1) * chans]
                )
            groups.append(acc)
        invariants = jnp.concatenate(groups, 1).astype(jnp.bfloat16)
        joined = jnp.concatenate([latent_b, invariants], 1)
        update = jnp.dot(joined, w_update[layer], preferred_element_type=jnp.float32)
        latent = latent + jax.nn.silu(update) * envelope[:, None]
    edge_energy = envelope * jnp.dot(
        latent.astype(jnp.bfloat16), w_out, preferred_element_type=jnp.float32
    )
    owner_table = (jnp.arange(n_own, dtype=jnp.int32)[:, None] == center[None, :]).astype(
        jnp.float32
    )
    atoms = jnp.dot(owner_table, edge_energy, precision=high)
    return (jnp.sum(edge_energy), atoms)


def to_cells(blocks):
    empty = jnp.zeros_like(blocks[:, :1])
    flat = jnp.concatenate([blocks[:, :4], empty, blocks[:, 4:]], 1)
    return flat.reshape(blocks.shape[0], 3, 3, blocks.shape[2])


def from_cells(grown):
    picked = grown[:, ::2, ::2].reshape(grown.shape[0], 9, grown.shape[3])
    kept = jnp.concatenate([picked[:, :4], picked[:, 5:]], 1)
    return kept.reshape(grown.shape[0], 8 * grown.shape[3])


def per_device(
    positions,
    species,
    mig_rows,
    ghost_rows,
    edge_center,
    edge_neighbor,
    edge_blocks,
    w_radial,
    w_kind_center,
    w_kind_neigh,
    w_two,
    w_edge,
    w_env,
    w_update,
    w_out,
):
    slots = positions.shape[3]
    payload = jnp.concatenate([positions[:, 0, 0], species[0, 0].astype(jnp.float32)[None]], 0)
    padded = jnp.concatenate([payload, jnp.zeros((4, 1), jnp.float32)], 1)
    leaving = mig_rows[0, 0]
    sent = padded[:, leaving.reshape(-1)].reshape(4, 8, leaving.shape[1])
    grown = extended_2(to_cells(sent), (("gx", 1), ("gy", 2)), 1)
    keep = jnp.ones((slots + 1,), jnp.float32).at[leaving.reshape(-1)].set(0.0)
    owned = jnp.concatenate([payload * keep[None, :slots], from_cells(grown)], 1)
    n_own = owned.shape[1]
    owned_pad = jnp.concatenate([owned, jnp.zeros((4, 1), jnp.float32)], 1)
    copies = ghost_rows[0, 0]
    gcells = to_cells(owned_pad[:, copies.reshape(-1)].reshape(4, 8, copies.shape[1]))
    ghost_grown = extended_2(gcells, (("gx", 1), ("gy", 2)), 1)
    extended = jnp.concatenate([owned, from_cells(ghost_grown)], 1)

    def energy_of(coords):
        return local_energy(
            coords,
            extended[3],
            edge_center[0, 0],
            edge_neighbor[0, 0],
            edge_blocks[0, 0],
            n_own,
            w_radial,
            w_kind_center,
            w_kind_neigh,
            w_two,
            w_edge,
            w_env,
            w_update,
            w_out,
        )

    total, pullback, atoms = jax.vjp(energy_of, extended[:3], has_aux=True)
    grads = pullback(jnp.ones_like(total))[0]
    own_grad = grads[:, :n_own]
    pcells = to_cells(grads[:, n_own:].reshape(3, 8, copies.shape[1]))
    back_grown = extended_2(pcells, (("gx", 1), ("gy", 2)), 1)
    summed = jnp.concatenate([own_grad, jnp.zeros((3, 1), jnp.float32)], 1)
    summed = summed.at[:, copies.reshape(-1)].add(from_cells(back_grown))
    forces = -summed[:, :n_own]
    return (owned[:3][:, None, None, :], forces[:, None, None, :], atoms[None, None, :])


def solution(mesh):
    placed = (
        P(None, "gx", "gy", None),
        P("gx", "gy", None),
        P("gx", "gy", None, None),
        P("gx", "gy", None, None),
        P("gx", "gy", None),
        P("gx", "gy", None),
        P("gx", "gy"),
        P(),
        P(),
        P(),
        P(),
        P(),
        P(),
        P(),
        P(),
    )
    return jax.shard_map(
        per_device,
        mesh=mesh,
        in_specs=placed,
        out_specs=(P(None, "gx", "gy", None), P(None, "gx", "gy", None), P("gx", "gy", None)),
        check_vma=False,
    )
```

profile of v0, /device:TPU:26, one launch (start us, length us, event | category | flops | bytes accessed | tf_op | source)
XLA Modules:
  0.0 250.2 jit_solution(7501796010285533724)
XLA Ops:
  3.0 2.5 scatter_custom_fusion
  7.6 2.7 %collective-permute-start.1 = (f32[4,1,3,64]{3,0,2,1:T(4,128)S(1)}, f32[4,1,3,64]{3,0,2,1:T(4,128)S(1)}, u32[]{:S(2)}, u32[]{:S(2)}) collective-permute-start(f32[4,1,3,64]{3,0,2,1:T(4,128)S(1)} %get-tuple-element.157), channel_id=1, source_target_pairs={{32,0},{64,32},{96,64},{128,96},{160,128},{192,160},{224,192},{33,... | collective-permute-start | bytes 9224 | tf_op jit(solution)/shard_map/ppermute | solution.py:25
  10.2 4.1 %collective-permute-start = (f32[4,1,3,64]{3,0,2,1:T(4,128)S(1)}, f32[4,1,3,64]{3,0,2,1:T(4,128)S(1)}, u32[]{:S(2)}, u32[]{:S(2)}) collective-permute-start(f32[4,1,3,64]{3,0,2,1:T(4,128)S(1)} %get-tuple-element.156), channel_id=1, source_target_pairs={{0,32},{32,64},{64,96},{96,128},{128,160},{160,192},{192,224},{1,3... | collective-permute-start | bytes 9224 | tf_op jit(solution)/shard_map/ppermute | solution.py:23
  15.9 7.3 %collective-permute-start.3 = (f32[4,5,1,64]{3,0,2,1:T(4,128)S(1)}, f32[4,5,1,64]{3,0,2,1:T(4,128)S(1)}, u32[]{:S(2)}, u32[]{:S(2)}) collective-permute-start(f32[4,5,1,64]{3,0,2,1:T(4,128)S(1)} %get-tuple-element.153), channel_id=1, source_target_pairs={{1,0},{2,1},{3,2},{4,3},{5,4},{6,5},{7,6},{8,7},{9,8},{10,9},{11,1... | collective-permute-start | bytes 15368 | tf_op jit(solution)/shard_map/ppermute | solution.py:25
  27.0 4.9 %collective-permute-done.2 = f32[4,5,1,64]{3,0,2,1:T(4,128)S(1)} collective-permute-done((f32[4,5,1,64]{3,0,2,1:T(4,128)S(1)}, f32[4,5,1,64]{3,0,2,1:T(4,128)S(1)}, u32[]{:S(2)}, u32[]{:S(2)}) %collective-permute-start.2) | collective-permute-done | bytes 5152 | tf_op jit(solution)/shard_map/ppermute | solution.py:23
  32.7 19.6 %gather_fusion.1 = f32[10080,4]{1,0:T(8,128)} fusion(f32[4,3453]{0,1:T(8,128)S(1)} %copy.289, s32[10240]{0:T(1024)S(1)} %pad_clamp_fusion), kind=kCustom, calls=%fused_computation.1 | custom fusion | bytes 362880 | tf_op jit(solution)/shard_map/gather | solution.py:178
  52.2 3.5 %copy.290 = f32[4,10080]{1,0:T(4,128)S(1)} copy(f32[4,10080]{0,1:T(8,128)} %bitcast.199) | data formatting | bytes 322560 | tf_op jit(solution)/shard_map/gather | solution.py:178
  56.2 2.4 collective-permute-start.5
  58.6 4.3 %collective-permute-start.4 = (f32[4,1,3,1260]{3,0,2,1:T(4,128)S(1)}, f32[4,1,3,1260]{3,0,2,1:T(4,128)S(1)}, u32[]{:S(2)}, u32[]{:S(2)}) collective-permute-start(f32[4,1,3,1260]{3,0,2,1:T(4,128)S(1)} %get-tuple-element.144), channel_id=1, source_target_pairs={{0,32},{32,64},{64,96},{96,128},{128,160},{160,192},{192,224},{1,3... | collective-permute-start | bytes 181448 | tf_op jit(solution)/shard_map/ppermute | solution.py:23
  66.8 2.6 %collective-permute-start.6 = (f32[4,5,1,1260]{3,0,2,1:T(4,128)S(1)}, f32[4,5,1,1260]{3,0,2,1:T(4,128)S(1)}, u32[]{:S(2)}, u32[]{:S(2)}) collective-permute-start(f32[4,5,1,1260]{3,0,2,1:T(4,128)S(1)} %get-tuple-element.134), channel_id=1, source_target_pairs={{0,1},{1,2},{2,3},{3,4},{4,5},{5,6},{6,7},{7,8},{8,9},{9,10},{10,1... | collective-permute-start | bytes 302408 | tf_op jit(solution)/shard_map/ppermute | solution.py:23
  70.1 6.3 %collective-permute-done.6 = f32[4,5,1,1260]{3,0,2,1:T(4,128)S(1)} collective-permute-done((f32[4,5,1,1260]{3,0,2,1:T(4,128)S(1)}, f32[4,5,1,1260]{3,0,2,1:T(4,128)S(1)}, u32[]{:S(2)}, u32[]{:S(2)}) %collective-permute-start.6) | collective-permute-done | bytes 100832 | tf_op jit(solution)/shard_map/ppermute | solution.py:23
  77.2 4.5 %copy.374 = f32[3,13532]{0,1:T(8,128)} copy(f32[3,13532]{1,0:T(4,128)S(1)} %bitcast.206) | data formatting | bytes 324768
  81.7 4.0 %gather_fusion.2 = f32[512,3]{1,0:T(8,128)S(1)} fusion(f32[3,13532]{0,1:T(8,128)} %copy.374, s32[1024]{0:T(1024)S(1)} %pad_clamp_fusion.2), kind=kCustom, calls=%fused_computation.2 | custom fusion | bytes 14336 | tf_op jit(solution)/shard_map/jvp()/gather | solution.py:71
  85.7 4.0 %gather_fusion.3 = f32[512,3]{1,0:T(8,128)S(1)} fusion(f32[3,13532]{0,1:T(8,128)} %copy.374, s32[1024]{0:T(1024)S(1)} %pad_clamp_fusion.1), kind=kCustom, calls=%fused_computation.3 | custom fusion | bytes 14336 | tf_op jit(solution)/shard_map/jvp()/gather | solution.py:71
  89.7 3.1 %gather_fusion.4 = f32[512]{0:T(512)S(1)} fusion(f32[13532]{0:T(1024)S(1)} %slice_reduce_fusion, s32[1024]{0:T(1024)S(1)} %pad_clamp_fusion.1), kind=kCustom, calls=%fused_computation.4 | custom fusion | bytes 6144 | tf_op jit(solution)/shard_map/jvp()/gather | solution.py:73
  92.9 3.1 %gather_fusion.5 = f32[512]{0:T(512)S(1)} fusion(f32[13532]{0:T(1024)S(1)} %slice_reduce_fusion, s32[1024]{0:T(1024)S(1)} %pad_clamp_fusion.2), kind=kCustom, calls=%fused_computation.5 | custom fusion | bytes 6144 | tf_op jit(solution)/shard_map/jvp()/gather | solution.py:74
  102.6 2.9 %fusion.14 = f32[512,576]{1,0:T(8,128)S(1)} fusion(f32[512,576]{1,0:T(8,128)} %concatenate.94, s32[512]{0:T(512)} %bitcast.226), kind=kOutput, calls=%fused_computation.26 | convolution fusion | flops 1812496384 | bytes 2361344 | tf_op jit(solution)/shard_map/jvp()/dot_general | solution.py:111
  111.8 2.9 %concatenate.96 = f32[512,576]{1,0:T(8,128)} concatenate(f32[512,64]{1,0:T(8,128)} %get-tuple-element.121, f32[512,64]{1,0:T(8,128)} %get-tuple-element.120, f32[512,64]{1,0:T(8,128)} %get-tuple-element.115, f32[512,64]{1,0:T(8,128)} %get-tuple-element.116, f32[512,64]{1,0:T(8,128)} %get-tuple-element.122, f32[512,64]{1,0:T(8,128)} %get-tuple-element.119, ...), dimensions={1} | concatenate | bytes 2359296 | tf_op jit(solution)/shard_map/jvp()/concatenate | solution.py:103
  114.8 2.9 %fusion.17 = f32[512,576]{1,0:T(8,128)S(1)} fusion(f32[512,576]{1,0:T(8,128)} %concatenate.96, s32[512]{0:T(512)} %bitcast.227), kind=kOutput, calls=%fused_computation.27 | convolution fusion | flops 1812496384 | bytes 2361344 | tf_op jit(solution)/shard_map/jvp()/dot_general | solution.py:111
  133.3 2.3 fusion.5
  142.1 9.4 %scatter_custom_fusion.1 = f32[3,13532]{0,1:T(8,128)} fusion(s32[1024]{0:T(1024)} %bitcast.276, f32[1024,3]{1,0:T(8,128)S(1)} %copy.345, f32[]{:T(128)} %constant.31.clone.1), kind=kCustom, calls=%fused_computation.13 | custom fusion | flops 3072 | bytes 162896 | tf_op jit(solution)/shard_map/transpose(jvp())/add_any | solution.py:71
  151.5 4.2 %slice.376 = f32[3,10080]{0,1:T(8,128)} slice(f32[3,13532]{0,1:T(8,128)} %scatter_custom_fusion.1), slice={[0:3], [3452:13532]} | slice | bytes 241920 | tf_op jit(solution)/shard_map/slice | solution.py:203
  155.7 3.5 %copy.346 = f32[3,10080]{1,0:T(4,128)S(1)} copy(f32[3,10080]{0,1:T(8,128)} %slice.376) | data formatting | bytes 241920 | tf_op jit(solution)/shard_map/slice | solution.py:203
  159.6 4.2 %collective-permute-start.9 = (f32[3,1,3,1260]{3,0,2,1:T(4,128)S(1)}, f32[3,1,3,1260]{3,0,2,1:T(4,128)S(1)}, u32[]{:S(2)}, u32[]{:S(2)}) collective-permute-start(f32[3,1,3,1260]{3,0,2,1:T(4,128)S(1)} %get-tuple-element.141), channel_id=1, source_target_pairs={{32,0},{64,32},{96,64},{128,96},{160,128},{192,160},{224,192},{33,... | collective-permute-start | bytes 136088 | tf_op jit(solution)/shard_map/ppermute | solution.py:25
  163.9 2.9 %collective-permute-start.8 = (f32[3,1,3,1260]{3,0,2,1:T(4,128)S(1)}, f32[3,1,3,1260]{3,0,2,1:T(4,128)S(1)}, u32[]{:S(2)}, u32[]{:S(2)}) collective-permute-start(f32[3,1,3,1260]{3,0,2,1:T(4,128)S(1)} %get-tuple-element.140), channel_id=1, source_target_pairs={{0,32},{32,64},{64,96},{96,128},{128,160},{160,192},{192,224},{1,3... | collective-permute-start | bytes 136088 | tf_op jit(solution)/shard_map/ppermute | solution.py:23
  166.7 3.1 %slice_select_fusion = f32[3,3453]{0,1:T(8,128)S(1)} fusion(f32[3,13532]{0,1:T(8,128)} %scatter_custom_fusion.1, pred[3453]{0:T(1024)(128)(4,1)S(1)} %copy-done.52), kind=kLoop, calls=%fused_computation.25 | loop fusion | flops 10359 | bytes 86325 | tf_op jit(solution)/shard_map/concatenate | solution.py:205
  172.0 2.4 collective-permute-start.10
  174.4 3.8 %fusion.1 = f32[1,1,3452]{2,1,0:T(1,128)} fusion(f32[512,1]{0,1:T(1,128)S(1)} %bitcast.277, s32[512]{0:T(512)S(1)} %bitcast.230), kind=kOutput, calls=%fused_computation.11 | convolution fusion | flops 22976512 | bytes 17904 | tf_op jit(solution)/shard_map/jvp()/dot_general | solution.py:134
  178.2 3.4 %collective-permute-done.10 = f32[3,5,1,1260]{3,0,2,1:T(4,128)S(1)} collective-permute-done((f32[3,5,1,1260]{3,0,2,1:T(4,128)S(1)}, f32[3,5,1,1260]{3,0,2,1:T(4,128)S(1)}, u32[]{:S(2)}, u32[]{:S(2)}) %collective-permute-start.10) | collective-permute-done | bytes 75632 | tf_op jit(solution)/shard_map/ppermute | solution.py:23
  182.0 3.3 %copy.349 = f32[10080,3]{1,0:T(8,128)} copy(f32[10080,3]{0,1:T(4,128)S(1)} %bitcast.209) | data formatting | bytes 241920 | tf_op jit(solution)/shard_map/reshape | solution.py:147
  185.4 60.6 %scatter_fusion = f32[3,3453]{0,1:T(8,128)S(1)} fusion(f32[3,3453]{0,1:T(8,128)S(1)} %slice_select_fusion, s32[10080]{0:T(1024)S(1)} %copy-done.11, f32[10080,3]{1,0:T(8,128)} %copy.349), kind=kCustom, calls=%fused_computation.8 | custom fusion | flops 30240 | bytes 403200 | tf_op jit(solution)/shard_map/scatter-add | solution.py:206
  247.3 2.6 %copy.351 = f32[3,1,1,3452]{3,2,1,0:T(1,128)} copy(f32[3,1,1,3452]{0,3,2,1:T(8,128)} %fusion.13) | data formatting | bytes 82848
  (266 shorter events, 54.1 us)
Async XLA Ops:
  0.6 98.0 %copy-start = (bf16[256,256]{1,0:T(8,128)(2,1)S(1)}, bf16[256,256]{1,0:T(8,128)(2,1)}, u32[]{:S(2)}) copy-start(bf16[256,256]{1,0:T(8,128)(2,1)} %param.25) | copy-start | bytes 393220
  6.0 8.4 %copy-start.34 = (s32[1,1,8,1260]{3,2,1,0:T(8,128)S(1)}, s32[1,1,8,1260]{3,2,1,0:T(8,128)}, u32[]{:S(2)}) copy-start(s32[1,1,8,1260]{3,2,1,0:T(8,128)} %param.18) | copy-start | bytes 120964
  6.0 9.3 %copy-start.31 = (s32[1,1,512]{2,1,0:T(1,128)S(1)}, s32[1,1,512]{2,1,0:T(1,128)}, u32[]{:S(2)}) copy-start(s32[1,1,512]{2,1,0:T(1,128)} %param.19) | copy-start | bytes 6148
  6.0 9.3 %copy-start.53 = (s32[1,1,512]{2,1,0:T(1,128)S(1)}, s32[1,1,512]{2,1,0:T(1,128)}, u32[]{:S(2)}) copy-start(s32[1,1,512]{2,1,0:T(1,128)} %param.20) | copy-start | bytes 6148
  6.0 19.2 %copy-start.58 = (bf16[256]{0:T(256)(128)(2,1)S(1)}, bf16[256]{0:T(256)(128)(2,1)}, u32[]{:S(2)}) copy-start(bf16[256]{0:T(256)(128)(2,1)} %param.29) | copy-start | bytes 1540
  7.5 48.4 %copy-start.48 = (f32[9]{0:T(128)}, f32[9]{0:T(128)S(1)}, u32[]{:S(2)}) copy-start(f32[9]{0:T(128)S(1)} %pad.377.clone) | copy-start | bytes 112
  7.6 8.3 %collective-permute-start.1 = (f32[4,1,3,64]{3,0,2,1:T(4,128)S(1)}, f32[4,1,3,64]{3,0,2,1:T(4,128)S(1)}, u32[]{:S(2)}, u32[]{:S(2)}) collective-permute-start(f32[4,1,3,64]{3,0,2,1:T(4,128)S(1)} %get-tuple-element.157), channel_id=1, source_target_pairs={{32,0},{64,32},{96,64},{128,96},{160,128},{192,160},{224,192},{33,... | collective-permute-start | bytes 9224 | tf_op jit(solution)/shard_map/ppermute | solution.py:25
  10.2 5.7 %collective-permute-start = (f32[4,1,3,64]{3,0,2,1:T(4,128)S(1)}, f32[4,1,3,64]{3,0,2,1:T(4,128)S(1)}, u32[]{:S(2)}, u32[]{:S(2)}) collective-permute-start(f32[4,1,3,64]{3,0,2,1:T(4,128)S(1)} %get-tuple-element.156), channel_id=1, source_target_pairs={{0,32},{32,64},{64,96},{96,128},{128,160},{160,192},{192,224},{1,3... | collective-permute-start | bytes 9224 | tf_op jit(solution)/shard_map/ppermute | solution.py:23
  15.9 11.0 %collective-permute-start.3 = (f32[4,5,1,64]{3,0,2,1:T(4,128)S(1)}, f32[4,5,1,64]{3,0,2,1:T(4,128)S(1)}, u32[]{:S(2)}, u32[]{:S(2)}) collective-permute-start(f32[4,5,1,64]{3,0,2,1:T(4,128)S(1)} %get-tuple-element.153), channel_id=1, source_target_pairs={{1,0},{2,1},{3,2},{4,3},{5,4},{6,5},{7,6},{8,7},{9,8},{10,9},{11,1... | collective-permute-start | bytes 15368 | tf_op jit(solution)/shard_map/ppermute | solution.py:25
  23.2 8.6 %collective-permute-start.2 = (f32[4,5,1,64]{3,0,2,1:T(4,128)S(1)}, f32[4,5,1,64]{3,0,2,1:T(4,128)S(1)}, u32[]{:S(2)}, u32[]{:S(2)}) collective-permute-start(f32[4,5,1,64]{3,0,2,1:T(4,128)S(1)} %get-tuple-element.152), channel_id=1, source_target_pairs={{0,1},{1,2},{2,3},{3,4},{4,5},{5,6},{6,7},{7,8},{8,9},{9,10},{10,1... | collective-permute-start | bytes 15368 | tf_op jit(solution)/shard_map/ppermute | solution.py:23
  25.2 71.2 %copy-start.54 = (f32[8]{0:T(128)}, f32[8]{0:T(128)S(1)}, u32[]{:S(2)}) copy-start(f32[8]{0:T(128)S(1)} %iota_multiply_fusion) | copy-start | bytes 100
  56.2 7.0 %collective-permute-start.5 = (f32[4,1,3,1260]{3,0,2,1:T(4,128)S(1)}, f32[4,1,3,1260]{3,0,2,1:T(4,128)S(1)}, u32[]{:S(2)}, u32[]{:S(2)}) collective-permute-start(f32[4,1,3,1260]{3,0,2,1:T(4,128)S(1)} %get-tuple-element.145), channel_id=1, source_target_pairs={{32,0},{64,32},{96,64},{128,96},{160,128},{192,160},{224,192},{33,... | collective-permute-start | bytes 181448 | tf_op jit(solution)/shard_map/ppermute | solution.py:25
  58.6 6.2 %collective-permute-start.4 = (f32[4,1,3,1260]{3,0,2,1:T(4,128)S(1)}, f32[4,1,3,1260]{3,0,2,1:T(4,128)S(1)}, u32[]{:S(2)}, u32[]{:S(2)}) collective-permute-start(f32[4,1,3,1260]{3,0,2,1:T(4,128)S(1)} %get-tuple-element.144), channel_id=1, source_target_pairs={{0,32},{32,64},{64,96},{96,128},{128,160},{160,192},{192,224},{1,3... | collective-permute-start | bytes 181448 | tf_op jit(solution)/shard_map/ppermute | solution.py:23
  64.8 5.3 %collective-permute-start.7 = (f32[4,5,1,1260]{3,0,2,1:T(4,128)S(1)}, f32[4,5,1,1260]{3,0,2,1:T(4,128)S(1)}, u32[]{:S(2)}, u32[]{:S(2)}) collective-permute-start(f32[4,5,1,1260]{3,0,2,1:T(4,128)S(1)} %get-tuple-element.135), channel_id=1, source_target_pairs={{1,0},{2,1},{3,2},{4,3},{5,4},{6,5},{7,6},{8,7},{9,8},{10,9},{11,1... | collective-permute-start | bytes 302408 | tf_op jit(solution)/shard_map/ppermute | solution.py:25
  66.8 9.6 %collective-permute-start.6 = (f32[4,5,1,1260]{3,0,2,1:T(4,128)S(1)}, f32[4,5,1,1260]{3,0,2,1:T(4,128)S(1)}, u32[]{:S(2)}, u32[]{:S(2)}) collective-permute-start(f32[4,5,1,1260]{3,0,2,1:T(4,128)S(1)} %get-tuple-element.134), channel_id=1, source_target_pairs={{0,1},{1,2},{2,3},{3,4},{4,5},{5,6},{6,7},{7,8},{8,9},{9,10},{10,1... | collective-permute-start | bytes 302408 | tf_op jit(solution)/shard_map/ppermute | solution.py:23
  92.9 4.8 %copy-start.35 = (f32[512]{0:T(512)}, f32[512]{0:T(512)S(1)}, u32[]{:S(2)}) copy-start(f32[512]{0:T(512)S(1)} %gather_fusion.4) | copy-start | bytes 6148
  92.9 4.1 %copy-start.41 = (f32[8,256]{1,0:T(8,128)S(1)}, f32[8,256]{1,0:T(8,128)}, u32[]{:S(2)}) copy-start(f32[8,256]{1,0:T(8,128)} %param.22) | copy-start | bytes 24580
  92.9 4.8 %copy-start.50 = (f32[4,256]{1,0:T(4,128)S(1)}, f32[4,256]{1,0:T(4,128)}, u32[]{:S(2)}) copy-start(f32[4,256]{1,0:T(4,128)} %param.23) | copy-start | bytes 12292
  96.1 2.5 %copy-start.37 = (f32[512]{0:T(512)}, f32[512]{0:T(512)S(1)}, u32[]{:S(2)}) copy-start(f32[512]{0:T(512)S(1)} %gather_fusion.5) | copy-start | bytes 6148
  96.1 2.1 copy-start.51
  96.4 4.1 %copy-start.15 = (f32[1,512]{1,0:T(1,128)}, f32[1,512]{1,0:T(1,128)S(1)}, u32[]{:S(2)}) copy-start(f32[1,512]{1,0:T(1,128)S(1)} %get-tuple-element.161) | copy-start | bytes 6148
  96.4 2.2 copy-start.45
  102.6 2.9 %copy-start.13 = (f32[512]{0:T(512)S(1)}, f32[512]{0:T(512)}, u32[]{:S(2)}) copy-start(f32[512]{0:T(512)} %copy-done.12) | copy-start | bytes 6148
  114.8 2.9 %copy-start.14 = (f32[512]{0:T(512)S(1)}, f32[512]{0:T(512)}, u32[]{:S(2)}) copy-start(f32[512]{0:T(512)} %copy-done.12) | copy-start | bytes 6148
  155.7 3.7 %copy-start.49 = (f32[9]{0:T(128)S(1)}, f32[9]{0:T(128)}, u32[]{:S(2)}) copy-start(f32[9]{0:T(128)} %copy-done.48) | copy-start | bytes 112
  159.2 7.6 %copy-start.52 = (pred[3453]{0:T(1024)(128)(4,1)S(1)}, pred[3453]{0:T(1024)(128)(4,1)}, u32[]{:S(2)}) copy-start(pred[3453]{0:T(1024)(128)(4,1)} %constant.32.clone.1) | copy-start | bytes 10363
  159.6 10.2 %collective-permute-start.9 = (f32[3,1,3,1260]{3,0,2,1:T(4,128)S(1)}, f32[3,1,3,1260]{3,0,2,1:T(4,128)S(1)}, u32[]{:S(2)}, u32[]{:S(2)}) collective-permute-start(f32[3,1,3,1260]{3,0,2,1:T(4,128)S(1)} %get-tuple-element.141), channel_id=1, source_target_pairs={{32,0},{64,32},{96,64},{128,96},{160,128},{192,160},{224,192},{33,... | collective-permute-start | bytes 136088 | tf_op jit(solution)/shard_map/ppermute | solution.py:25
  163.9 10.5 %copy-start.33 = (s32[1,1,512]{2,1,0:T(1,128)S(1)}, s32[1,1,512]{2,1,0:T(1,128)}, u32[]{:S(2)}) copy-start(s32[1,1,512]{2,1,0:T(1,128)} %param.19) | copy-start | bytes 6148
  163.9 6.1 %collective-permute-start.8 = (f32[3,1,3,1260]{3,0,2,1:T(4,128)S(1)}, f32[3,1,3,1260]{3,0,2,1:T(4,128)S(1)}, u32[]{:S(2)}, u32[]{:S(2)}) collective-permute-start(f32[3,1,3,1260]{3,0,2,1:T(4,128)S(1)} %get-tuple-element.140), channel_id=1, source_target_pairs={{0,32},{32,64},{64,96},{96,128},{128,160},{160,192},{192,224},{1,3... | collective-permute-start | bytes 136088 | tf_op jit(solution)/shard_map/ppermute | solution.py:23
  170.0 8.1 %collective-permute-start.11 = (f32[3,5,1,1260]{3,0,2,1:T(4,128)S(1)}, f32[3,5,1,1260]{3,0,2,1:T(4,128)S(1)}, u32[]{:S(2)}, u32[]{:S(2)}) collective-permute-start(f32[3,5,1,1260]{3,0,2,1:T(4,128)S(1)} %get-tuple-element.133), channel_id=1, source_target_pairs={{1,0},{2,1},{3,2},{4,3},{5,4},{6,5},{7,6},{8,7},{9,8},{10,9},{11,1... | collective-permute-start | bytes 226808 | tf_op jit(solution)/shard_map/ppermute | solution.py:25
  172.0 9.6 %collective-permute-start.10 = (f32[3,5,1,1260]{3,0,2,1:T(4,128)S(1)}, f32[3,5,1,1260]{3,0,2,1:T(4,128)S(1)}, u32[]{:S(2)}, u32[]{:S(2)}) collective-permute-start(f32[3,5,1,1260]{3,0,2,1:T(4,128)S(1)} %get-tuple-element.132), channel_id=1, source_target_pairs={{0,1},{1,2},{2,3},{3,4},{4,5},{5,6},{6,7},{7,8},{8,9},{9,10},{10,1... | collective-permute-start | bytes 226808 | tf_op jit(solution)/shard_map/ppermute | solution.py:23
  182.0 3.4 %copy-start.11 = (s32[10080]{0:T(1024)S(1)}, s32[10080]{0:T(1024)}, u32[]{:S(2)}) copy-start(s32[10080]{0:T(1024)} %copy-done.10) | copy-start | bytes 120964
  (46 other events, 44.9 us)
where the time goes:
time: 255 us; the launch traced here: 250 us
  other arithmetic  93.2 us (37%)
  local copies, waits for them, and re-layouts  75.1 us (29%)
  starting transfers between devices  38.6 us (15%)
  matrix products  23.8 us (9%)
  waiting for transfers between devices  16.5 us (6%)
  between operations  2.95 us (1%)
    scatter-add x1, other arithmetic, per_device(): summed = summed.at[:, copies.reshape(-1)].add(from_cells(back_grown))  60.6 us
    gather x2, local copies, waits for them, and re-layouts, per_device(): owned_pad[:, copies.reshape(-1)].reshape(4, 8, copies.shape[1])  23 us
    ppermute x6, starting transfers between devices, extended_2(): lax.ppermute(head, axis, [((i + 1) % count, i) for i in range(ends)])  20.5 us
    ppermute x6, starting transfers between devices, extended_2(): lax.ppermute(tail, axis, [(i, (i + 1) % count) for i in range(ends)])  18.2 us
    ppermute x6, waiting for transfers between devices, extended_2(): lax.ppermute(tail, axis, [(i, (i + 1) % count) for i in range(ends)])  16.3 us
    unnamed x141, local copies, waits for them, and re-layouts  14.5 us
    dot_general x4, matrix products, local_energy(): env_at = jnp.dot(shared_center, terms, precision=high) * ENV_SCALE  10.3 us
    add_any x1, other arithmetic, local_energy(): delta = ext_pos[:, neighbor] - ext_pos[:, center]  9.36 us
  transfers between devices with their start and end apart: 12, of which 6 were waited for; matrix products, arithmetic and copies ran while one was open for 4% of the time, Pallas kernels for 0%

commit v1 on v0

v1 whole, which is shorter than its diff:
```python
import math

import jax
import jax.numpy as jnp
from jax import lax
from jax.experimental import pallas as pl
from jax.experimental.pallas import tpu as pltpu
from jax.sharding import PartitionSpec as P

CUTOFF = 6.0
SOFTENING = 0.01
BASIS_WIDTH = 0.8
ENV_SCALE = 0.3
ROOT3 = math.sqrt(3.0)
ROOT5 = math.sqrt(5.0)
ROOT15 = math.sqrt(15.0)
DIRS = ((-1, -1), (-1, 0), (-1, 1), (0, -1), (0, 1), (1, -1), (1, 0), (1, 1))
SLOTS = 2940
MOVES = 64
OWNED = 3452
GHOSTS = 1260
EDGES = 512
LANES = 128
KEPT_ROWS = 23
F32 = jnp.float32
BF16 = jnp.bfloat16
VMEM_LIMIT = 48 * 1024 * 1024

NN = (((1,), (0,)), ((), ()))
NT = (((1,), (1,)), ((), ()))
TN = (((0,), (0,)), ((), ()))


def mm(a, b, dims=NN):
    return lax.dot_general(a, b, dims, preferred_element_type=F32)


def mm_high(a, b, dims=NN):
    return lax.dot_general(
        a, b, dims, precision=lax.Precision.HIGHEST, preferred_element_type=F32
    )


def split(x):
    top = x.astype(BF16)
    return top, (x - top.astype(F32)).astype(BF16)


def lane_pick(row, low):
    table = jnp.broadcast_to(row, low.shape)
    return jnp.take_along_axis(table, low, axis=1, mode="promise_in_bounds")


def full_row(ref, lead, start, size):
    stop = min(start + LANES, size)
    piece = ref[lead + (slice(None), slice(start, stop))]
    if stop - start < LANES:
        pad = jnp.zeros((1, LANES - (stop - start)), piece.dtype)
        piece = jnp.concatenate([piece, pad], axis=1)
    return piece


def payload_row(pos_ref, kind_ref, chan, h):
    if chan < 3:
        return full_row(pos_ref, (chan,), h * LANES, SLOTS)
    return full_row(kind_ref, (), h * LANES, SLOTS).astype(F32)


def send_kernel(pos_ref, kind_ref, mig_ref, nbr_ref, msg_ref):
    rows = mig_ref[...]
    rows = jnp.concatenate([rows, jnp.full((8, LANES - MOVES), -1, jnp.int32)], axis=1)
    high, low = rows >> 7, rows & 127
    picked = [jnp.zeros((8, LANES), F32) for _ in range(4)]
    for h in range(KEPT_ROWS):
        here = high == h
        for c in range(4):
            got = lane_pick(payload_row(pos_ref, kind_ref, c, h), low)
            picked[c] = jnp.where(here, got, picked[c])
    for p in range(2):
        msg_ref[pl.ds(8 * p, 8), :] = picked[2 * p] + pltpu.roll(picked[2 * p + 1], MOVES, 1)
    for r in range(4):
        msg_ref[pl.ds(16 + r, 1), :] = nbr_ref[:, r * LANES : (r + 1) * LANES].astype(F32)
    msg_ref[pl.ds(20, 4), :] = jnp.zeros((4, LANES), F32)


def keep_kernel(pos_ref, kind_ref, mig_ref, kept_ref):
    rows = mig_ref[...]
    rows = jnp.concatenate([rows, jnp.full((8, LANES - MOVES), -1, jnp.int32)], axis=1)
    high, low = rows >> 7, rows & 127
    sub32 = lax.broadcasted_iota(jnp.int32, (32, LANES), 0)
    sub128 = lax.broadcasted_iota(jnp.int32, (LANES, LANES), 0)
    left = jnp.zeros((32, LANES), F32)
    for k in range(8):
        a = (sub32 == high[k : k + 1, :]).astype(F32).astype(BF16)
        b = (sub128 == low[k : k + 1, :]).astype(F32).astype(BF16)
        left = left + mm(a, b, NT)
    stay = left < 0.5
    for c in range(4):
        table = jnp.concatenate(
            [payload_row(pos_ref, kind_ref, c, h) for h in range(KEPT_ROWS)]
            + [jnp.zeros((1, LANES), F32)],
            axis=0,
        )
        kept_ref[c] = jnp.where(stay[:24, :], table, 0.0)


def answer_kernel(
    grid, where_ref, own_ref, below_ref, above_ref, ghost_ref, center_ref, kept_ref,
    left_ref, right_ref, same_ref, center_out, slot_ref, arrive_ref,
):
    nx, ny = grid
    ix, iy = where_ref[0], where_ref[1]
    by_dy = {-1: below_ref, 0: own_ref, 1: above_ref}
    inside = []
    for dx, dy in DIRS:
        ok = (ix + dx >= 0) & (ix + dx < nx) & (iy + dy >= 0) & (iy + dy < ny)
        inside.append(ok.astype(jnp.int32))
    for p in range(2):
        for k, (dx, dy) in enumerate(DIRS):
            row = by_dy[dy][dx + 1, pl.ds(8 * p + 7 - k, 1), :]
            arrive_ref[p, pl.ds(k, 1), :] = row * inside[k].astype(F32)
    groups = []
    for o in range(0, 8, 2):
        parts = []
        for d in (o, o + 1):
            dx, dy = DIRS[d]
            listed = by_dy[dy][dx + 1, pl.ds(16, 4), :].astype(jnp.int32)
            rank = listed - (OWNED + GHOSTS * (7 - d))
            ok = (rank >= 0) & (rank < GHOSTS) & (inside[d] > 0)
            parts.append(jnp.where(ok, rank, -1))
        rank = jnp.concatenate(parts, axis=0)
        high, low = rank >> 7, rank & 127
        slot = jnp.full((8, LANES), -1, jnp.int32)
        upper = lax.broadcasted_iota(jnp.int32, (8, LANES), 0) < 4
        for h in range(10):
            stop = min((h + 1) * LANES, GHOSTS)
            pair = []
            for d in (o, o + 1):
                row = ghost_ref[pl.ds(d, 1), h * LANES : stop]
                if stop - h * LANES < LANES:
                    pad = jnp.full((1, LANES - (stop - h * LANES)), -1, jnp.int32)
                    row = jnp.concatenate([row, pad], axis=1)
                pair.append(jnp.broadcast_to(row, (8, LANES)))
            table = jnp.where(upper, pair[0], pair[1])
            got = jnp.take_along_axis(table, low, axis=1, mode="promise_in_bounds")
            slot = jnp.where(high == h, got, slot)
        groups.append(jnp.where(slot >= OWNED, -1, slot))
    near = own_ref[1, pl.ds(16, 4), :].astype(jnp.int32)
    near = jnp.where(near < OWNED, near, -1)
    core = jnp.concatenate(
        [center_ref[:, r * LANES : (r + 1) * LANES] for r in range(4)], axis=0
    )
    groups.append(jnp.concatenate([near, core], axis=0))
    for q in range(5):
        slot = groups[q]
        slot_ref[pl.ds(8 * q, 8), :] = slot
        late = slot - SLOTS
        is_late = late >= 0
        high = jnp.where(is_late, KEPT_ROWS + (late >> 6), slot >> 7)
        low_a = jnp.where(is_late, late & 63, slot & 127)
        low_b = jnp.where(is_late, (late & 63) + MOVES, slot & 127)
        found = [jnp.zeros((8, LANES), F32) for _ in range(4)]
        for h in range(KEPT_ROWS + 8):
            here = high == h
            for c in range(4):
                if h < KEPT_ROWS:
                    row = kept_ref[c, pl.ds(h, 1), :]
                else:
                    row = arrive_ref[c // 2, pl.ds(h - KEPT_ROWS, 1), :]
                got = lane_pick(row, low_b if c % 2 else low_a)
                found[c] = jnp.where(here, got, found[c])
        for half in range(2):
            item = 2 * q + half
            for c in range(4):
                rows = found[c][4 * half : 4 * half + 4, :]
                if item < 8:
                    dx, dy = DIRS[item]
                    ref = {-1: left_ref, 0: same_ref, 1: right_ref}[dx]
                    ref[dy + 1, pl.ds(4 * c, 4), :] = rows
                elif item == 8:
                    same_ref[1, pl.ds(4 * c, 4), :] = rows
                else:
                    center_out[pl.ds(4 * c, 4), :] = rows


def edge_kernel(
    layers,
    blocks_ref, same_ref, below_ref, above_ref, center_ref, core_row_ref, core_col_ref,
    w_in_t_ref, w_rad_ref, w_two_t_ref, w_two_ref, w_mix_t_ref, w_mix_ref, w_up_t_ref,
    w_up_ref, w_out_ref,
    msg_ref,
    lhs_ref, rhs_ref, back_ref, joined_ref, latent_ref, d_latent_ref, edge_mix_ref, env_mix_ref,
    pooled_ref, act_ref, slope_ref,
):
    near = same_ref[1] + below_ref[...] + above_ref[...]
    mid = center_ref[...]

    def flat(rows, c):
        return jnp.concatenate([rows[4 * c + r : 4 * c + r + 1, :] for r in range(4)], axis=1)

    delta = [flat(near, c) - flat(mid, c) for c in range(3)]
    kind_n, kind_c = flat(near, 3), flat(mid, 3)
    radius = jnp.sqrt(delta[0] * delta[0] + delta[1] * delta[1] + delta[2] * delta[2] + SOFTENING)
    inv_radius = 1.0 / radius
    block = lax.broadcasted_iota(jnp.int32, (1, EDGES), 1) >> 7
    live = (block < blocks_ref[0]) & (kind_c > 0.5) & (kind_n > 0.5)
    live = jnp.where(live, 1.0, 0.0)
    ramp = jnp.maximum(0.0, 1.0 - radius * radius / (CUTOFF * CUTOFF))
    envelope = live * ramp * ramp
    ux, uy, uz = (d * (1.0 / CUTOFF) for d in delta)
    sph = [
        ROOT3 * ux,
        ROOT3 * uy,
        ROOT3 * uz,
        ROOT15 * ux * uy,
        ROOT15 * uy * uz,
        ROOT15 * ux * uz,
        (0.5 * ROOT5) * (2.0 * uz * uz - ux * ux - uy * uy),
        (0.5 * ROOT15) * (ux * ux - uy * uy),
    ]
    q8 = lax.broadcasted_iota(jnp.int32, (8, EDGES), 0)
    shift = radius - q8.astype(F32) * (CUTOFF / 7.0)
    radial = jnp.exp(-(shift * shift) * (1.0 / (BASIS_WIDTH * BASIS_WIDTH)))
    ids = (q8 & 3) + 1
    kinds = jnp.where(q8 < 4, kind_c, kind_n)
    onehot = jnp.where(kinds == ids.astype(F32), 1.0, 0.0)
    same_center = core_col_ref[...] == core_row_ref[...]
    zero_row = jnp.zeros((1, EDGES), F32)

    def gram(rows):
        top, rest = [], []
        for row in rows:
            a, b = split(row)
            top.append(a.astype(F32))
            rest.append(b.astype(F32))
        fill = [jnp.zeros((LANES - 3 * len(rows), EDGES), F32)]
        a = jnp.concatenate(top + top + rest + fill, axis=0).astype(BF16)
        b = jnp.concatenate(top + rest + top + fill, axis=0).astype(BF16)
        return jnp.where(same_center, mm(a, b, TN), 0.0).astype(BF16)

    grams = [jnp.where(same_center, 1.0, 0.0).astype(BF16), gram(sph[:3]), gram(sph[3:])]

    feats = jnp.concatenate([radial, onehot, jnp.zeros((LANES - 16, EDGES), F32)], axis=0)
    pre = mm_high(w_in_t_ref[...], feats)

    def sigmoid(x):
        return 0.5 * jnp.tanh(0.5 * x) + 0.5

    gate0 = sigmoid(pre)
    hidden = (pre * gate0).astype(BF16)
    slope0 = gate0 * (1.0 + pre * (1.0 - gate0))
    two = mm(w_two_t_ref[...], hidden)
    gate1 = sigmoid(two)
    act1 = two * gate1
    slope1 = gate1 * (1.0 + two * (1.0 - gate1))
    latent_ref[...] = act1 * envelope
    spare = jnp.zeros((64, EDGES), BF16)

    def forward(t, carry):
        latent = latent_ref[...]
        latent_b = latent.astype(BF16)
        mixed = mm(w_mix_t_ref[t], latent_b)
        edge_mix, env_mix = mixed[:192, :], mixed[192:, :].astype(BF16)
        pooled = jnp.concatenate(
            [mm(env_mix[64 * l : 64 * l + 64, :], grams[l]) for l in range(3)], axis=0
        ) * ENV_SCALE
        invariants = (edge_mix * pooled).astype(BF16)
        update = mm(w_up_t_ref[t], jnp.concatenate([latent_b, invariants, spare], axis=0))
        gate = sigmoid(update)
        act = update * gate
        edge_mix_ref[t] = edge_mix
        env_mix_ref[t] = env_mix
        pooled_ref[t] = pooled
        act_ref[t] = act
        slope_ref[t] = gate * (1.0 + update * (1.0 - gate))
        latent_ref[...] = latent + act * envelope
        return carry

    lax.fori_loop(0, layers, forward, 0)
    w_out = w_out_ref[...]
    read = jnp.sum(latent_ref[...].astype(BF16).astype(F32) * w_out, axis=0, keepdims=True)
    energy = envelope * read
    d_latent_ref[...] = (w_out * envelope).astype(BF16).astype(F32)

    def backward(s, d_env):
        t = layers - 1 - s
        d_latent = d_latent_ref[...]
        d_env = d_env + jnp.sum(d_latent * act_ref[t], axis=0, keepdims=True)
        d_update = (d_latent * envelope * slope_ref[t]).astype(BF16)
        joined_ref[...] = mm(w_up_ref[t], d_update)
        d_inv = joined_ref[pl.ds(256, 192), :]
        d_edge_mix = (d_inv * pooled_ref[t]).astype(BF16)
        d_pooled = (d_inv * edge_mix_ref[t] * ENV_SCALE).astype(BF16)
        d_env_mix = jnp.concatenate(
            [mm(d_pooled[64 * l : 64 * l + 64, :], grams[l]) for l in range(3)], axis=0
        ).astype(BF16)
        for l in range(1, 3):
            mix_l = env_mix_ref[t, pl.ds(64 * l, 64), :]
            pool_l = d_pooled[64 * l : 64 * l + 64, :]
            lhs_ref[l - 1, t] = jnp.concatenate([pool_l, mix_l], axis=0)
            rhs_ref[l - 1, t] = jnp.concatenate([mix_l, pool_l], axis=0)
        back_ref[...] = mm(
            w_mix_ref[t], jnp.concatenate([d_edge_mix, d_env_mix, spare, spare], axis=0)
        )
        d_latent_ref[...] = d_latent + joined_ref[pl.ds(0, 256), :] + back_ref[...]
        return d_env

    d_env = lax.fori_loop(0, layers, backward, read)
    d_latent = d_latent_ref[...]
    d_env = d_env + jnp.sum(d_latent * act1, axis=0, keepdims=True)
    d_two = (d_latent * envelope * slope1).astype(BF16)
    d_pre = mm(w_two_ref[...], d_two) * slope0
    d_radial = mm_high(w_rad_ref[...], d_pre)
    d_radius = jnp.sum(
        d_radial * radial * shift, axis=0, keepdims=True
    ) * (-2.0 / (BASIS_WIDTH * BASIS_WIDTH))
    d_radius = d_radius - d_env * live * ramp * radius * (4.0 / (CUTOFF * CUTOFF))

    def both(ref, l):
        return jnp.concatenate([ref[l - 1, t] for t in range(layers)], axis=0)

    d_sph = []
    for l, rows in ((1, sph[:3]), (2, sph[3:])):
        pairs = jnp.where(same_center, mm(both(lhs_ref, l), both(rhs_ref, l), TN), 0.0)
        top, rest = split(pairs)
        fill = [zero_row] * (8 - len(rows))
        ya, yb = split(jnp.concatenate(list(rows) + fill, axis=0))
        got = mm(ya, top) + mm(yb, top) + mm(ya, rest)
        d_sph += [got[i : i + 1, :] for i in range(len(rows))]
    d1, d2, d3, d4, d5, d6, d7, d8 = d_sph
    du = [
        ROOT3 * d1 + ROOT15 * (uy * d4 + uz * d6 + ux * d8) - ROOT5 * ux * d7,
        ROOT3 * d2 + ROOT15 * (ux * d4 + uz * d5 - uy * d8) - ROOT5 * uy * d7,
        ROOT3 * d3 + ROOT15 * (uy * d5 + ux * d6) + (2.0 * ROOT5) * uz * d7,
    ]
    scale = d_radius * inv_radius
    for c in range(3):
        grad = scale * delta[c] + du[c] * (1.0 / CUTOFF)
        for r in range(4):
            msg_ref[pl.ds(4 * c + r, 1), :] = grad[:, r * LANES : (r + 1) * LANES]
    for r in range(4):
        msg_ref[pl.ds(12 + r, 1), :] = energy[:, r * LANES : (r + 1) * LANES]


def spread(slot_rows, value_rows):
    chans = len(value_rows[0])
    sub32 = lax.broadcasted_iota(jnp.int32, (32, LANES), 0)
    sub128 = lax.broadcasted_iota(jnp.int32, (LANES, LANES), 0)
    total = jnp.zeros((2 * chans * 32, LANES), F32)
    for first in range(0, len(slot_rows), 2):
        a_parts, b_parts = [], []
        for slot, values in zip(slot_rows[first : first + 2], value_rows[first : first + 2]):
            here = sub32 == (slot >> 7)
            pieces = []
            for value in values:
                top, rest = split(value)
                pieces.append(jnp.where(here, top.astype(F32), 0.0))
                pieces.append(jnp.where(here, rest.astype(F32), 0.0))
            a_parts.append(jnp.concatenate(pieces, axis=0))
            b_parts.append(jnp.where(sub128 == (slot & 127), 1.0, 0.0))
        a = jnp.concatenate(a_parts, axis=1).astype(BF16)
        b = jnp.concatenate(b_parts, axis=1).astype(BF16)
        total = total + mm(a, b, NT)
    return [total[64 * c : 64 * c + 32, :] + total[64 * c + 32 : 64 * c + 64, :] for c in range(chans)]


def store_flat(ref, lead, table):
    for h in range(27):
        stop = min((h + 1) * LANES, OWNED)
        ref[lead + (slice(None), slice(h * LANES, stop))] = table[h : h + 1, : stop - h * LANES]


def home_kernel(msg_ref, slot_ref, force_ref, atom_ref):
    slot_rows, value_rows, energies = [], [], []
    for r in range(4):
        grads = [msg_ref[pl.ds(4 * c + r, 1), :] for c in range(3)]
        slot_rows.append(slot_ref[pl.ds(32 + r, 1), :])
        value_rows.append([-g for g in grads])
    for r in range(4):
        grads = [msg_ref[pl.ds(4 * c + r, 1), :] for c in range(3)]
        slot_rows.append(slot_ref[pl.ds(36 + r, 1), :])
        value_rows.append(grads)
    for c, table in enumerate(spread(slot_rows, value_rows)):
        force_ref[c] = table
    energies = [[msg_ref[pl.ds(12 + r, 1), :]] for r in range(4)]
    store_flat(atom_ref, (0,), spread(slot_rows[4:], energies)[0])


def return_kernel(own_ref, below_ref, above_ref, slot_ref, force_in_ref, force_ref):
    by_dy = {-1: below_ref, 0: own_ref, 1: above_ref}
    slot_rows, value_rows = [], []
    for o, (dx, dy) in enumerate(DIRS):
        for r in range(4):
            slot_rows.append(slot_ref[pl.ds(4 * o + r, 1), :])
            value_rows.append(
                [by_dy[dy][dx + 1, pl.ds(4 * c + r, 1), :] for c in range(3)]
            )
    for c, table in enumerate(spread(slot_rows, value_rows)):
        store_flat(force_ref, (c,), force_in_ref[c] - table)


def whole(count, smem=()):
    return [
        pl.BlockSpec(memory_space=pltpu.SMEM if i in smem else pltpu.VMEM) for i in range(count)
    ]


def call(kernel, outs, args, smem=(), scratch=(), cost=None):
    many = isinstance(outs, (list, tuple))
    return pl.pallas_call(
        kernel,
        out_shape=outs,
        in_specs=whole(len(args), smem),
        out_specs=whole(len(outs)) if many else whole(1)[0],
        scratch_shapes=list(scratch),
        compiler_params=pltpu.CompilerParams(vmem_limit_bytes=VMEM_LIMIT),
    )(*args)


def shift(x, axis, step):
    count = lax.axis_size(axis)
    return lax.ppermute(x, axis, [(i, (i + step) % count) for i in range(count)])


def around(x, axis):
    return shift(x, axis, 1), shift(x, axis, -1)


def shaped(*dims, dtype=F32):
    return jax.ShapeDtypeStruct(dims, dtype)


def per_device(
    positions,
    species,
    mig_rows,
    ghost_rows,
    edge_center,
    edge_neighbor,
    edge_blocks,
    w_radial,
    w_kind_center,
    w_kind_neigh,
    w_two,
    w_edge,
    w_env,
    w_update,
    w_out,
):
    layers = w_edge.shape[0]
    pos = positions.reshape(3, 1, SLOTS)
    kind = species.reshape(1, SLOTS)
    mig = mig_rows.reshape(8, MOVES)
    ghosts = ghost_rows.reshape(8, GHOSTS)
    centers = edge_center.reshape(1, EDGES)
    nbrs = edge_neighbor.reshape(1, EDGES)
    blocks = edge_blocks.reshape(1)
    grid = (lax.axis_size("gx"), lax.axis_size("gy"))
    place = jnp.stack([lax.axis_index("gx"), lax.axis_index("gy")]).astype(jnp.int32)

    msg = call(send_kernel, shaped(24, LANES), (pos, kind, mig, nbrs))
    left, right = around(msg, "gx")
    column = jnp.stack([left, msg, right])
    kept = call(keep_kernel, shaped(4, 24, LANES), (pos, kind, mig))
    below, above = around(column, "gy")

    to_left, to_right, same, mids, slots, arrived = call(
        lambda *refs: answer_kernel(grid, *refs),
        (
            shaped(3, 16, LANES),
            shaped(3, 16, LANES),
            shaped(3, 16, LANES),
            shaped(16, LANES),
            shaped(40, LANES, dtype=jnp.int32),
            shaped(2, 8, LANES),
        ),
        (place, column, below, above, ghosts, centers, kept),
        smem=(0,),
    )
    from_left = shift(to_right, "gx", 1)
    from_right = shift(to_left, "gx", -1)
    same = same + from_left + from_right
    from_below = shift(same[2], "gy", 1)
    from_above = shift(same[0], "gy", -1)

    stay = kept[:3].reshape(3, 24 * LANES)[:, :SLOTS]
    late = arrived.reshape(2, 8, 2, MOVES).transpose(0, 2, 1, 3).reshape(4, 8 * MOVES)[:3]
    owned_positions = jnp.concatenate([stay, late], 1).reshape(3, 1, 1, OWNED)

    w_in = jnp.concatenate([w_radial, w_kind_center, w_kind_neigh], 0)
    w_in_t = jnp.pad(w_in, ((0, LANES - 16), (0, 0))).T
    w_mix = jnp.concatenate([w_edge, w_env], 2)
    w_mix_wide = jnp.pad(w_mix, ((0, 0), (0, 0), (0, LANES)))
    w_up_t = jnp.pad(w_update, ((0, 0), (0, 64), (0, 0))).transpose(0, 2, 1)
    grad = call(
        lambda *refs: edge_kernel(layers, *refs),
        shaped(16, LANES),
        (
            blocks, same, from_below, from_above, mids, centers, edge_center.reshape(EDGES, 1),
            w_in_t, w_radial, w_two.T, w_two, w_mix.transpose(0, 2, 1), w_mix_wide, w_up_t, w_update,
            w_out.astype(F32).reshape(-1, 1),
        ),
        smem=(0,),
        scratch=(
            pltpu.VMEM((2, layers, 128, EDGES), BF16),
            pltpu.VMEM((2, layers, 128, EDGES), BF16),
            pltpu.VMEM((256, EDGES), F32),
            pltpu.VMEM((448, EDGES), F32),
            pltpu.VMEM((256, EDGES), F32),
            pltpu.VMEM((256, EDGES), F32),
            pltpu.VMEM((layers, 192, EDGES), F32),
            pltpu.VMEM((layers, 192, EDGES), BF16),
            pltpu.VMEM((layers, 192, EDGES), F32),
            pltpu.VMEM((layers, 256, EDGES), F32),
            pltpu.VMEM((layers, 256, EDGES), F32),
        ),
    )
    left, right = around(grad, "gx")
    column = jnp.stack([left, grad, right])
    force_home, atoms = call(
        home_kernel, (shaped(3, 32, LANES), shaped(1, 1, OWNED)), (grad, slots)
    )
    below, above = around(column, "gy")
    forces = call(
        return_kernel, shaped(3, 1, OWNED), (column, below, above, slots, force_home)
    )
    return (owned_positions, forces.reshape(3, 1, 1, OWNED), atoms)


def solution(mesh):
    placed = (
        P(None, "gx", "gy", None),
        P("gx", "gy", None),
        P("gx", "gy", None, None),
        P("gx", "gy", None, None),
        P("gx", "gy", None),
        P("gx", "gy", None),
        P("gx", "gy"),
        P(),
        P(),
        P(),
        P(),
        P(),
        P(),
        P(),
        P(),
    )
    return jax.shard_map(
        per_device,
        mesh=mesh,
        in_specs=placed,
        out_specs=(P(None, "gx", "gy", None), P(None, "gx", "gy", None), P("gx", "gy", None)),
        check_vma=False,
    )
```

time: 255 us -> 56 us (0.22)
  the two profiles are of different devices: /device:TPU:26 before, /device:TPU:14 now
where the time goes in v1:
time: 56 us; the launch traced here: 55.7 us
  starting transfers between devices  22.6 us (40%)
  waiting for transfers between devices  13.2 us (24%)
  Pallas kernels  11.4 us (20%)
  local copies, waits for them, and re-layouts  6.45 us (12%)
  between operations  1.54 us (3%)
    ppermute x12, starting transfers between devices, shift(): lax.ppermute(x, axis, [(i, (i + step) % count) for i in range(count)])  22.6 us
    ppermute x12, waiting for transfers between devices, shift(): lax.ppermute(x, axis, [(i, (i + step) % count) for i in range(count)])  13.2 us
    pallas_call x6, Pallas kernels, call(): pl.pallas_call(kernel, out_shape=outs, in_specs=whole(len(args), smem), o...  11.4 us
    unnamed x36, local copies, waits for them, and re-layouts  4.96 us
  transfers between devices with their start and end apart: 12, of which 6 were waited for; matrix products, arithmetic and copies ran while one was open for 6% of the time, Pallas kernels for 2%

profile of v1, /device:TPU:14, one launch (start us, length us, event | category | flops | bytes accessed | tf_op | source)
XLA Modules:
  0.0 55.7 jit_solution(10860457967182390374)
XLA Ops:
  0.7 0.7 %copy-done.9 = s32[1,1,8,64]{3,2,1,0:T(8,128)S(1)} copy-done((s32[1,1,8,64]{3,2,1,0:T(8,128)S(1)}, s32[1,1,8,64]{3,2,1,0:T(8,128)}, u32[]{:S(2)}) %copy-start.9) | copy-done | bytes 2072
  1.3 0.8 %copy-done.2 = f32[3,1,1,2940]{3,2,1,0:T(1,128)S(1)} copy-done((f32[3,1,1,2940]{3,2,1,0:T(1,128)S(1)}, f32[3,1,1,2940]{3,2,1,0:T(1,128)}, u32[]{:S(2)}) %copy-start.2) | copy-done | bytes 35304
  2.1 0.7 %copy-done.4 = s32[1,1,2940]{2,1,0:T(1,128)S(1)} copy-done((s32[1,1,2940]{2,1,0:T(1,128)S(1)}, s32[1,1,2940]{2,1,0:T(1,128)}, u32[]{:S(2)}) %copy-start.4) | copy-done | bytes 11784
  2.8 0.2 shard_map.167
  3.0 2.1 %collective-permute-start = (f32[24,128]{1,0:T(8,128)S(1)}, f32[24,128]{1,0:T(8,128)S(1)}, u32[]{:S(2)}, u32[]{:S(2)}) collective-permute-start(f32[24,128]{1,0:T(8,128)S(1)} %shard_map.167), channel_id=1, source_target_pairs={{0,32},{32,64},{64,96},{96,128},{128,160},{160,192},{192,224},{224... | collective-permute-start | bytes 36872 | tf_op jit(solution)/shard_map/ppermute | solution.py:422
  5.2 1.1 %copy.43 = bf16[2,256,192]{2,1,0:T(8,128)(2,1)S(1)} copy(bf16[2,256,192]{1,2,0:T(8,128)(2,1)} %param.26) | data formatting | bytes 393216 | tf_op args[11]
  6.4 0.2 copy.45
  6.7 0.2 pad_maximum_fusion
  6.8 0.2 fusion
  7.0 4.0 %collective-permute-done.1 = f32[24,128]{1,0:T(8,128)S(1)} collective-permute-done((f32[24,128]{1,0:T(8,128)S(1)}, f32[24,128]{1,0:T(8,128)S(1)}, u32[]{:S(2)}, u32[]{:S(2)}) %collective-permute-start.1) | collective-permute-done | bytes 12320 | tf_op jit(solution)/shard_map/ppermute | solution.py:422
  11.1 5.3 %collective-permute-start.3 = (f32[3,24,128]{2,1,0:T(8,128)S(1)}, f32[3,24,128]{2,1,0:T(8,128)S(1)}, u32[]{:S(2)}, u32[]{:S(2)}) collective-permute-start(f32[3,24,128]{2,1,0:T(8,128)S(1)} %pad_maximum_fusion.2.refs_1_), channel_id=1, source_target_pairs={{0,31},{1,0},{2,1},{3,2},{4,3},{5,4},{6,5},{7,6},{8,7},{9,8},{10,9... | collective-permute-start | bytes 110600 | tf_op jit(solution)/shard_map/ppermute | solution.py:422
  16.5 0.3 shard_map.166.refs_6_
  16.8 1.3 %collective-permute-done.2.refs_2_ = f32[3,24,128]{2,1,0:T(8,128)S(1)} collective-permute-done((f32[3,24,128]{2,1,0:T(8,128)S(1)}, f32[3,24,128]{2,1,0:T(8,128)S(1)}, u32[]{:S(2)}, u32[]{:S(2)}) %collective-permute-start.2) | collective-permute-done | bytes 36896 | tf_op jit(solution)/shard_map/ppermute | solution.py:422
  18.1 2.0 %shard_map.168 = (f32[3,16,128]{2,1,0:T(8,128)S(1)}, f32[3,16,128]{2,1,0:T(8,128)S(1)}, f32[3,16,128]{2,1,0:T(8,128)S(1)}, f32[16,128]{1,0:T(8,128)S(1)}, s32[40...) custom-call(s32[2]{0:T(128)S(1)} %pad_add_fusion.refs_0_, f32[3,24,128]{2,1,0:T(8,128)S(1)} %pad_maximum_fusion.2.refs_1_, ...), custom_call_target="tpu_custom_call" | custom-call | tf_op jit(solution)/shard_map/pallas_call | solution.py:410
  20.1 0.6 %collective-permute-start.4 = (f32[3,16,128]{2,1,0:T(8,128)S(1)}, f32[3,16,128]{2,1,0:T(8,128)S(1)}, u32[]{:S(2)}, u32[]{:S(2)}) collective-permute-start(f32[3,16,128]{2,1,0:T(8,128)S(1)} %get-tuple-element.13), channel_id=1, source_target_pairs={{0,32},{32,64},{64,96},{96,128},{128,160},{160,192},{192,224},{224... | collective-permute-start | bytes 73736 | tf_op jit(solution)/shard_map/ppermute | solution.py:422
  20.7 1.5 %collective-permute-start.5 = (f32[3,16,128]{2,1,0:T(8,128)S(1)}, f32[3,16,128]{2,1,0:T(8,128)S(1)}, u32[]{:S(2)}, u32[]{:S(2)}) collective-permute-start(f32[3,16,128]{2,1,0:T(8,128)S(1)} %get-tuple-element.14), channel_id=1, source_target_pairs={{0,224},{32,0},{64,32},{96,64},{128,96},{160,128},{192,160},{224,1... | collective-permute-start | bytes 73736 | tf_op jit(solution)/shard_map/ppermute | solution.py:422
  22.3 1.7 %collective-permute-done.4 = f32[3,16,128]{2,1,0:T(8,128)S(1)} collective-permute-done((f32[3,16,128]{2,1,0:T(8,128)S(1)}, f32[3,16,128]{2,1,0:T(8,128)S(1)}, u32[]{:S(2)}, u32[]{:S(2)}) %collective-permute-start.4) | collective-permute-done | bytes 24608 | tf_op jit(solution)/shard_map/ppermute | solution.py:422
  24.0 2.6 %collective-permute-done.5 = f32[3,16,128]{2,1,0:T(8,128)S(1)} collective-permute-done((f32[3,16,128]{2,1,0:T(8,128)S(1)}, f32[3,16,128]{2,1,0:T(8,128)S(1)}, u32[]{:S(2)}, u32[]{:S(2)}) %collective-permute-start.5) | collective-permute-done | bytes 24608 | tf_op jit(solution)/shard_map/ppermute | solution.py:422
  26.8 5.3 %collective-permute-start.7 = (f32[16,128]{1,0:T(8,128)S(1)}, f32[16,128]{1,0:T(8,128)S(1)}, u32[]{:S(2)}, u32[]{:S(2)}) collective-permute-start(f32[16,128]{1,0:T(8,128)S(1)} %get-tuple-element.28), channel_id=1, source_target_pairs={{0,31},{1,0},{2,1},{3,2},{4,3},{5,4},{6,5},{7,6},{8,7},{9,8},{10,9... | collective-permute-start | bytes 24584 | tf_op jit(solution)/shard_map/ppermute | solution.py:422
  32.1 0.2 copy.47.refs_11_
  32.3 0.1 copy.46.refs_6_
  32.5 0.5 copy-done.14
  33.0 0.1 copy.48.refs_15_
  33.1 0.8 %copy-done.1 = bf16[256,256]{1,0:T(8,128)(2,1)S(1)} copy-done((bf16[256,256]{1,0:T(8,128)(2,1)S(1)}, bf16[256,256]{1,0:T(8,128)(2,1)}, u32[]{:S(2)}) %copy-start.1) | copy-done | bytes 131096
  34.7 6.8 %shard_map.169.msg_ref = f32[16,128]{1,0:T(8,128)S(1)} custom-call(s32[1]{0:T(128)} %bitcast.40.refs_0_, f32[3,16,128]{2,1,0:T(8,128)S(1)} %add_add_fusion.refs_1_, f32[16,128]{1,0:T(8,128)S(1)} %collective-permute-done.6.refs_2_, f32[16,128]{1,0:T(8,128)S(1)} %collective-permute-done.7.refs_3_, f32[16,128]{1,0:T(8,128)S(1)} %get-tuple-element.15.refs_4_, ...), custom_call_target="tpu_custom_call" | custom-call | tf_op jit(solution)/shard_map/pallas_call | solution.py:410
  41.6 2.0 %collective-permute-start.9 = (f32[16,128]{1,0:T(8,128)S(1)}, f32[16,128]{1,0:T(8,128)S(1)}, u32[]{:S(2)}, u32[]{:S(2)}) collective-permute-start(f32[16,128]{1,0:T(8,128)S(1)} %shard_map.169.msg_ref), channel_id=1, source_target_pairs={{0,224},{32,0},{64,32},{96,64},{128,96},{160,128},{192,160},{224,1... | collective-permute-start | bytes 24584 | tf_op jit(solution)/shard_map/ppermute | solution.py:422
  43.8 1.4 %collective-permute-done.8 = f32[16,128]{1,0:T(8,128)S(1)} collective-permute-done((f32[16,128]{1,0:T(8,128)S(1)}, f32[16,128]{1,0:T(8,128)S(1)}, u32[]{:S(2)}, u32[]{:S(2)}) %collective-permute-start.8) | collective-permute-done | bytes 8224 | tf_op jit(solution)/shard_map/ppermute | solution.py:422
  45.3 2.2 %collective-permute-done.9 = f32[16,128]{1,0:T(8,128)S(1)} collective-permute-done((f32[16,128]{1,0:T(8,128)S(1)}, f32[16,128]{1,0:T(8,128)S(1)}, u32[]{:S(2)}, u32[]{:S(2)}) %collective-permute-start.9) | collective-permute-done | bytes 8224 | tf_op jit(solution)/shard_map/ppermute | solution.py:422
  47.5 5.4 %collective-permute-start.11 = (f32[3,16,128]{2,1,0:T(8,128)S(1)}, f32[3,16,128]{2,1,0:T(8,128)S(1)}, u32[]{:S(2)}, u32[]{:S(2)}) collective-permute-start(f32[3,16,128]{2,1,0:T(8,128)S(1)} %pad_maximum_fusion.3.own_ref), channel_id=1, source_target_pairs={{0,31},{1,0},{2,1},{3,2},{4,3},{5,4},{6,5},{7,6},{8,7},{9,8},{10,9... | collective-permute-start | bytes 73736 | tf_op jit(solution)/shard_map/ppermute | solution.py:422
  52.9 0.6 %reshape.59 = f32[3,1,1,3452]{3,2,1,0:T(1,128)} reshape(f32[3,3452]{1,0:T(4,128)S(1)} %pad_maximum_fusion.1) | data formatting | bytes 82848 | tf_op jit(solution)/shard_map/reshape | solution.py:488
  53.5 0.9 %shard_map.170 = (f32[3,32,128]{2,1,0:T(8,128)S(1)}, f32[1,1,3452]{2,1,0:T(1,128)}) custom-call(f32[16,128]{1,0:T(8,128)S(1)} %shard_map.169.msg_ref, s32[40,128]{1,0:T(8,128)S(1)} %get-tuple-element.16.slot_ref), custom_call_target="tpu_custom_call" | custom-call | tf_op jit(solution)/shard_map/pallas_call | solution.py:410
  54.5 1.2 %shard_map.171 = f32[3,1,3452]{2,1,0:T(1,128)} custom-call(f32[3,16,128]{2,1,0:T(8,128)S(1)} %pad_maximum_fusion.3.own_ref, f32[3,16,128]{2,1,0:T(8,128)S(1)} %collective-permute-done.10.below_ref, f32[3,16,128]{2,1,0:T(8,128)S(1)} %collective-permute-done.11.above_ref, s32[40,128]{1,0:T(8,128)S(1)} %get-tuple-element.16.slot_ref, ...), custom_call_target="tpu_custom_call" | custom-call | tf_op jit(solution)/shard_map/pallas_call | solution.py:410
  (56 shorter events, 1.1 us)
Async XLA Ops:
  0.6 0.7 %copy-start.9 = (s32[1,1,8,64]{3,2,1,0:T(8,128)S(1)}, s32[1,1,8,64]{3,2,1,0:T(8,128)}, u32[]{:S(2)}) copy-start(s32[1,1,8,64]{3,2,1,0:T(8,128)} %param.17) | copy-start | bytes 6148
  0.6 0.7 %copy-start.10 = (s32[1,1,512]{2,1,0:T(1,128)S(1)}, s32[1,1,512]{2,1,0:T(1,128)}, u32[]{:S(2)}) copy-start(s32[1,1,512]{2,1,0:T(1,128)} %param.20) | copy-start | bytes 6148
  1.3 0.8 %copy-start.2 = (f32[3,1,1,2940]{3,2,1,0:T(1,128)S(1)}, f32[3,1,1,2940]{3,2,1,0:T(1,128)}, u32[]{:S(2)}) copy-start(f32[3,1,1,2940]{3,2,1,0:T(1,128)} %param.15) | copy-start | bytes 105844
  2.1 0.7 %copy-start.4 = (s32[1,1,2940]{2,1,0:T(1,128)S(1)}, s32[1,1,2940]{2,1,0:T(1,128)}, u32[]{:S(2)}) copy-start(s32[1,1,2940]{2,1,0:T(1,128)} %param.16) | copy-start | bytes 35284
  2.8 3.4 %copy-start.11 = (bf16[2,256,192]{1,2,0:T(8,128)(2,1)S(1)}, bf16[2,256,192]{1,2,0:T(8,128)(2,1)}, u32[]{:S(2)}) copy-start(bf16[2,256,192]{1,2,0:T(8,128)(2,1)} %param.27) | copy-start | bytes 589828
  3.0 3.4 %copy-start = (bf16[2,448,256]{2,1,0:T(8,128)(2,1)S(1)}, bf16[2,448,256]{2,1,0:T(8,128)(2,1)}, u32[]{:S(2)}) copy-start(bf16[2,448,256]{2,1,0:T(8,128)(2,1)} %refs_14_.1) | copy-start | bytes 1376260
  3.0 4.0 %collective-permute-start = (f32[24,128]{1,0:T(8,128)S(1)}, f32[24,128]{1,0:T(8,128)S(1)}, u32[]{:S(2)}, u32[]{:S(2)}) collective-permute-start(f32[24,128]{1,0:T(8,128)S(1)} %shard_map.167), channel_id=1, source_target_pairs={{0,32},{32,64},{64,96},{96,128},{128,160},{160,192},{192,224},{224... | collective-permute-start | bytes 36872 | tf_op jit(solution)/shard_map/ppermute | solution.py:422
  5.2 5.8 %collective-permute-start.1 = (f32[24,128]{1,0:T(8,128)S(1)}, f32[24,128]{1,0:T(8,128)S(1)}, u32[]{:S(2)}, u32[]{:S(2)}) collective-permute-start(f32[24,128]{1,0:T(8,128)S(1)} %shard_map.167), channel_id=1, source_target_pairs={{0,224},{32,0},{64,32},{96,64},{128,96},{160,128},{192,160},{224,1... | collective-permute-start | bytes 36872 | tf_op jit(solution)/shard_map/ppermute | solution.py:422
  11.0 5.5 %copy-start.3 = (f32[3,1,1,2940]{3,2,1,0:T(1,128)S(1)}, f32[3,1,1,2940]{3,2,1,0:T(1,128)}, u32[]{:S(2)}) copy-start(f32[3,1,1,2940]{3,2,1,0:T(1,128)} %param.15) | copy-start | bytes 105844
  11.0 5.5 %copy-start.5 = (s32[1,1,2940]{2,1,0:T(1,128)S(1)}, s32[1,1,2940]{2,1,0:T(1,128)}, u32[]{:S(2)}) copy-start(s32[1,1,2940]{2,1,0:T(1,128)} %param.16) | copy-start | bytes 35284
  11.0 7.1 %collective-permute-start.2 = (f32[3,24,128]{2,1,0:T(8,128)S(1)}, f32[3,24,128]{2,1,0:T(8,128)S(1)}, u32[]{:S(2)}, u32[]{:S(2)}) collective-permute-start(f32[3,24,128]{2,1,0:T(8,128)S(1)} %pad_maximum_fusion.2.refs_1_), channel_id=1, source_target_pairs={{0,1},{1,2},{2,3},{3,4},{4,5},{5,6},{6,7},{7,8},{8,9},{9,10},{10,1... | collective-permute-start | bytes 110600 | tf_op jit(solution)/shard_map/ppermute | solution.py:422
  11.1 7.0 %collective-permute-start.3 = (f32[3,24,128]{2,1,0:T(8,128)S(1)}, f32[3,24,128]{2,1,0:T(8,128)S(1)}, u32[]{:S(2)}, u32[]{:S(2)}) collective-permute-start(f32[3,24,128]{2,1,0:T(8,128)S(1)} %pad_maximum_fusion.2.refs_1_), channel_id=1, source_target_pairs={{0,31},{1,0},{2,1},{3,2},{4,3},{5,4},{6,5},{7,6},{8,7},{9,8},{10,9... | collective-permute-start | bytes 110600 | tf_op jit(solution)/shard_map/ppermute | solution.py:422
  16.5 1.6 %copy-start.6 = (s32[1,1,8,1260]{3,2,1,0:T(8,128)S(1)}, s32[1,1,8,1260]{3,2,1,0:T(8,128)}, u32[]{:S(2)}) copy-start(s32[1,1,8,1260]{3,2,1,0:T(8,128)} %param.18) | copy-start | bytes 120964
  16.8 1.3 %copy-start.8 = (s32[1,1,512]{2,1,0:T(1,128)S(1)}, s32[1,1,512]{2,1,0:T(1,128)}, u32[]{:S(2)}) copy-start(s32[1,1,512]{2,1,0:T(1,128)} %param.19) | copy-start | bytes 6148
  18.1 4.2 %copy-start.7 = (f32[8,256]{1,0:T(8,128)S(1)}, f32[8,256]{1,0:T(8,128)}, u32[]{:S(2)}) copy-start(f32[8,256]{1,0:T(8,128)} %refs_8_.1) | copy-start | bytes 24580
  18.1 4.1 %copy-start.12 = (f32[4,256]{1,0:T(4,128)S(1)}, f32[4,256]{1,0:T(4,128)}, u32[]{:S(2)}) copy-start(f32[4,256]{1,0:T(4,128)} %param.24) | copy-start | bytes 12292
  18.1 4.1 %copy-start.13 = (f32[4,256]{1,0:T(4,128)S(1)}, f32[4,256]{1,0:T(4,128)}, u32[]{:S(2)}) copy-start(f32[4,256]{1,0:T(4,128)} %param.23) | copy-start | bytes 12292
  20.1 3.9 %collective-permute-start.4 = (f32[3,16,128]{2,1,0:T(8,128)S(1)}, f32[3,16,128]{2,1,0:T(8,128)S(1)}, u32[]{:S(2)}, u32[]{:S(2)}) collective-permute-start(f32[3,16,128]{2,1,0:T(8,128)S(1)} %get-tuple-element.13), channel_id=1, source_target_pairs={{0,32},{32,64},{64,96},{96,128},{128,160},{160,192},{192,224},{224... | collective-permute-start | bytes 73736 | tf_op jit(solution)/shard_map/ppermute | solution.py:422
  20.7 5.9 %collective-permute-start.5 = (f32[3,16,128]{2,1,0:T(8,128)S(1)}, f32[3,16,128]{2,1,0:T(8,128)S(1)}, u32[]{:S(2)}, u32[]{:S(2)}) collective-permute-start(f32[3,16,128]{2,1,0:T(8,128)S(1)} %get-tuple-element.14), channel_id=1, source_target_pairs={{0,224},{32,0},{64,32},{96,64},{128,96},{160,128},{192,160},{224,1... | collective-permute-start | bytes 73736 | tf_op jit(solution)/shard_map/ppermute | solution.py:422
  26.7 8.0 %collective-permute-start.6 = (f32[16,128]{1,0:T(8,128)S(1)}, f32[16,128]{1,0:T(8,128)S(1)}, u32[]{:S(2)}, u32[]{:S(2)}) collective-permute-start(f32[16,128]{1,0:T(8,128)S(1)} %get-tuple-element.29), channel_id=1, source_target_pairs={{0,1},{1,2},{2,3},{3,4},{4,5},{5,6},{6,7},{7,8},{8,9},{9,10},{10,1... | collective-permute-start | bytes 24584 | tf_op jit(solution)/shard_map/ppermute | solution.py:422
  26.8 7.9 %collective-permute-start.7 = (f32[16,128]{1,0:T(8,128)S(1)}, f32[16,128]{1,0:T(8,128)S(1)}, u32[]{:S(2)}, u32[]{:S(2)}) collective-permute-start(f32[16,128]{1,0:T(8,128)S(1)} %get-tuple-element.28), channel_id=1, source_target_pairs={{0,31},{1,0},{2,1},{3,2},{4,3},{5,4},{6,5},{7,6},{8,7},{9,8},{10,9... | collective-permute-start | bytes 24584 | tf_op jit(solution)/shard_map/ppermute | solution.py:422
  32.3 0.7 %copy-start.14 = (bf16[256]{0:T(256)(128)(2,1)S(1)}, bf16[256]{0:T(256)(128)(2,1)}, u32[]{:S(2)}) copy-start(bf16[256]{0:T(256)(128)(2,1)} %param.29) | copy-start | bytes 1540
  33.0 0.9 %copy-start.1 = (bf16[256,256]{1,0:T(8,128)(2,1)S(1)}, bf16[256,256]{1,0:T(8,128)(2,1)}, u32[]{:S(2)}) copy-start(bf16[256,256]{1,0:T(8,128)(2,1)} %refs_10_.1) | copy-start | bytes 393220
  41.5 3.7 %collective-permute-start.8 = (f32[16,128]{1,0:T(8,128)S(1)}, f32[16,128]{1,0:T(8,128)S(1)}, u32[]{:S(2)}, u32[]{:S(2)}) collective-permute-start(f32[16,128]{1,0:T(8,128)S(1)} %shard_map.169.msg_ref), channel_id=1, source_target_pairs={{0,32},{32,64},{64,96},{96,128},{128,160},{160,192},{192,224},{224... | collective-permute-start | bytes 24584 | tf_op jit(solution)/shard_map/ppermute | solution.py:422
  41.6 5.8 %collective-permute-start.9 = (f32[16,128]{1,0:T(8,128)S(1)}, f32[16,128]{1,0:T(8,128)S(1)}, u32[]{:S(2)}, u32[]{:S(2)}) collective-permute-start(f32[16,128]{1,0:T(8,128)S(1)} %shard_map.169.msg_ref), channel_id=1, source_target_pairs={{0,224},{32,0},{64,32},{96,64},{128,96},{160,128},{192,160},{224,1... | collective-permute-start | bytes 24584 | tf_op jit(solution)/shard_map/ppermute | solution.py:422
  47.5 7.0 %collective-permute-start.10 = (f32[3,16,128]{2,1,0:T(8,128)S(1)}, f32[3,16,128]{2,1,0:T(8,128)S(1)}, u32[]{:S(2)}, u32[]{:S(2)}) collective-permute-start(f32[3,16,128]{2,1,0:T(8,128)S(1)} %pad_maximum_fusion.3.own_ref), channel_id=1, source_target_pairs={{0,1},{1,2},{2,3},{3,4},{4,5},{5,6},{6,7},{7,8},{8,9},{9,10},{10,1... | collective-permute-start | bytes 73736 | tf_op jit(solution)/shard_map/ppermute | solution.py:422
  47.5 7.0 %collective-permute-start.11 = (f32[3,16,128]{2,1,0:T(8,128)S(1)}, f32[3,16,128]{2,1,0:T(8,128)S(1)}, u32[]{:S(2)}, u32[]{:S(2)}) collective-permute-start(f32[3,16,128]{2,1,0:T(8,128)S(1)} %pad_maximum_fusion.3.own_ref), channel_id=1, source_target_pairs={{0,31},{1,0},{2,1},{3,2},{4,3},{5,4},{6,5},{7,6},{8,7},{9,8},{10,9... | collective-permute-start | bytes 73736 | tf_op jit(solution)/shard_map/ppermute | solution.py:422

commit v2 on v1

--- a/solution.py
+++ b/solution.py
@@ -25,6 +25,7 @@
 F32 = jnp.float32
 BF16 = jnp.bfloat16
 VMEM_LIMIT = 48 * 1024 * 1024
+WHOLE_VMEM = 64 * 1024 * 1024
 
 NN = (((1,), (0,)), ((), ()))
 NT = (((1,), (1,)), ((), ()))
@@ -35,15 +36,14 @@
     return lax.dot_general(a, b, dims, preferred_element_type=F32)
 
 
-def mm_high(a, b, dims=NN):
-    return lax.dot_general(
-        a, b, dims, precision=lax.Precision.HIGHEST, preferred_element_type=F32
-    )
-
-
 def split(x):
     top = x.astype(BF16)
     return top, (x - top.astype(F32)).astype(BF16)
+
+
+def halves(x):
+    top = x.astype(BF16).astype(F32)
+    return top, x - top
 
 
 def lane_pick(row, low):
@@ -66,10 +66,25 @@
     return full_row(kind_ref, (), h * LANES, SLOTS).astype(F32)
 
 
-def send_kernel(pos_ref, kind_ref, mig_ref, nbr_ref, msg_ref):
+def send_kernel(pos_hbm, kind_hbm, mig_hbm, nbr_hbm, msg_ref, pos_ref, kind_ref, mig_ref, nbr_ref, sems):
+    copies = [
+        pltpu.make_async_copy(a, b, sems.at[i])
+        for i, (a, b) in enumerate(
+            ((mig_hbm, mig_ref), (nbr_hbm, nbr_ref), (kind_hbm, kind_ref), (pos_hbm, pos_ref))
+        )
+    ]
+    for copy in copies:
+        copy.start()
+    copies[0].wait()
     rows = mig_ref[...]
     rows = jnp.concatenate([rows, jnp.full((8, LANES - MOVES), -1, jnp.int32)], axis=1)
     high, low = rows >> 7, rows & 127
+    copies[1].wait()
+    for r in range(4):
+        msg_ref[pl.ds(16 + r, 1), :] = nbr_ref[:, r * LANES : (r + 1) * LANES].astype(F32)
+    msg_ref[pl.ds(20, 4), :] = jnp.zeros((4, LANES), F32)
+    copies[2].wait()
+    copies[3].wait()
     picked = [jnp.zeros((8, LANES), F32) for _ in range(4)]
     for h in range(KEPT_ROWS):
         here = high == h
@@ -78,9 +93,6 @@
             picked[c] = jnp.where(here, got, picked[c])
     for p in range(2):
         msg_ref[pl.ds(8 * p, 8), :] = picked[2 * p] + pltpu.roll(picked[2 * p + 1], MOVES, 1)
-    for r in range(4):
-        msg_ref[pl.ds(16 + r, 1), :] = nbr_ref[:, r * LANES : (r + 1) * LANES].astype(F32)
-    msg_ref[pl.ds(20, 4), :] = jnp.zeros((4, LANES), F32)
 
 
 def keep_kernel(pos_ref, kind_ref, mig_ref, kept_ref):
@@ -104,27 +116,37 @@
         kept_ref[c] = jnp.where(stay[:24, :], table, 0.0)
 
 
+def arrange(ix, iy, own_ref, even_ref, odd_ref, grid_ref):
+    odd_x, odd_y = ix & 1, iy & 1
+    for dx in (-1, 0, 1):
+        block = {-1: 2 - 2 * odd_x, 0: 1, 1: 2 * odd_x}[dx]
+        even, odd = even_ref[block], odd_ref[block]
+        grid_ref[0, dx + 1] = jnp.where(odd_y > 0, even, odd)
+        grid_ref[1, dx + 1] = own_ref[block]
+        grid_ref[2, dx + 1] = jnp.where(odd_y > 0, odd, even)
+
+
 def answer_kernel(
-    grid, where_ref, own_ref, below_ref, above_ref, ghost_ref, center_ref, kept_ref,
-    left_ref, right_ref, same_ref, center_out, slot_ref, arrive_ref,
+    grid, where_ref, own_ref, even_ref, odd_ref, ghost_ref, center_ref, kept_ref,
+    to_even_ref, to_odd_ref, same_ref, center_out, slot_ref, arrive_ref, grid_ref,
 ):
     nx, ny = grid
     ix, iy = where_ref[0], where_ref[1]
-    by_dy = {-1: below_ref, 0: own_ref, 1: above_ref}
+    arrange(ix, iy, own_ref, even_ref, odd_ref, grid_ref)
     inside = []
     for dx, dy in DIRS:
         ok = (ix + dx >= 0) & (ix + dx < nx) & (iy + dy >= 0) & (iy + dy < ny)
         inside.append(ok.astype(jnp.int32))
     for p in range(2):
         for k, (dx, dy) in enumerate(DIRS):
-            row = by_dy[dy][dx + 1, pl.ds(8 * p + 7 - k, 1), :]
+            row = grid_ref[dy + 1, dx + 1, pl.ds(8 * p + 7 - k, 1), :]
             arrive_ref[p, pl.ds(k, 1), :] = row * inside[k].astype(F32)
     groups = []
     for o in range(0, 8, 2):
         parts = []
         for d in (o, o + 1):
             dx, dy = DIRS[d]
-            listed = by_dy[dy][dx + 1, pl.ds(16, 4), :].astype(jnp.int32)
+            listed = grid_ref[dy + 1, dx + 1, pl.ds(16, 4), :].astype(jnp.int32)
             rank = listed - (OWNED + GHOSTS * (7 - d))
             ok = (rank >= 0) & (rank < GHOSTS) & (inside[d] > 0)
             parts.append(jnp.where(ok, rank, -1))
@@ -151,6 +173,7 @@
         [center_ref[:, r * LANES : (r + 1) * LANES] for r in range(4)], axis=0
     )
     groups.append(jnp.concatenate([near, core], axis=0))
+    sides = {-1: [], 0: [], 1: []}
     for q in range(5):
         slot = groups[q]
         slot_ref[pl.ds(8 * q, 8), :] = slot
@@ -175,19 +198,23 @@
                 rows = found[c][4 * half : 4 * half + 4, :]
                 if item < 8:
                     dx, dy = DIRS[item]
-                    ref = {-1: left_ref, 0: same_ref, 1: right_ref}[dx]
-                    ref[dy + 1, pl.ds(4 * c, 4), :] = rows
+                    if dx == 0:
+                        same_ref[dy + 1, pl.ds(4 * c, 4), :] = rows
+                    sides[dx].append((dy + 1, 4 * c, rows))
                 elif item == 8:
                     same_ref[1, pl.ds(4 * c, 4), :] = rows
                 else:
                     center_out[pl.ds(4 * c, 4), :] = rows
+    flip = (ix & 1) > 0
+    for (d, start, left), (_, _, right) in zip(sides[-1], sides[1]):
+        to_even_ref[d, pl.ds(start, 4), :] = jnp.where(flip, left, right)
+        to_odd_ref[d, pl.ds(start, 4), :] = jnp.where(flip, right, left)
 
 
 def edge_kernel(
     layers,
     blocks_ref, same_ref, below_ref, above_ref, center_ref, core_row_ref, core_col_ref,
-    w_in_t_ref, w_rad_ref, w_two_t_ref, w_two_ref, w_mix_t_ref, w_mix_ref, w_up_t_ref,
-    w_up_ref, w_out_ref,
+    w_rad_ref, w_kc_ref, w_kn_ref, w_two_ref, w_edge_t_ref, w_env_t_ref, w_up_ref, w_out_ref,
     msg_ref,
     lhs_ref, rhs_ref, back_ref, joined_ref, latent_ref, d_latent_ref, edge_mix_ref, env_mix_ref,
     pooled_ref, act_ref, slope_ref,
@@ -240,8 +267,13 @@
 
     grams = [jnp.where(same_center, 1.0, 0.0).astype(BF16), gram(sph[:3]), gram(sph[3:])]
 
-    feats = jnp.concatenate([radial, onehot, jnp.zeros((LANES - 16, EDGES), F32)], axis=0)
-    pre = mm_high(w_in_t_ref[...], feats)
+    w_top, w_rest = halves(
+        jnp.concatenate([w_rad_ref[...], w_kc_ref[...], w_kn_ref[...]], axis=0)
+    )
+    f_top, f_rest = halves(jnp.concatenate([radial, onehot], axis=0))
+    w_in = jnp.concatenate([w_top, w_rest, w_top, jnp.zeros((LANES - 48, 256), F32)], axis=0)
+    feats = jnp.concatenate([f_top, f_top, f_rest, jnp.zeros((LANES - 48, EDGES), F32)], axis=0)
+    pre = mm(w_in.astype(BF16), feats.astype(BF16), TN)
 
     def sigmoid(x):
         return 0.5 * jnp.tanh(0.5 * x) + 0.5
@@ -249,23 +281,22 @@
     gate0 = sigmoid(pre)
     hidden = (pre * gate0).astype(BF16)
     slope0 = gate0 * (1.0 + pre * (1.0 - gate0))
-    two = mm(w_two_t_ref[...], hidden)
+    two = mm(w_two_ref[...], hidden, TN)
     gate1 = sigmoid(two)
     act1 = two * gate1
     slope1 = gate1 * (1.0 + two * (1.0 - gate1))
     latent_ref[...] = act1 * envelope
-    spare = jnp.zeros((64, EDGES), BF16)
 
     def forward(t, carry):
         latent = latent_ref[...]
         latent_b = latent.astype(BF16)
-        mixed = mm(w_mix_t_ref[t], latent_b)
-        edge_mix, env_mix = mixed[:192, :], mixed[192:, :].astype(BF16)
+        edge_mix = mm(w_edge_t_ref[t], latent_b)
+        env_mix = mm(w_env_t_ref[t], latent_b).astype(BF16)
         pooled = jnp.concatenate(
             [mm(env_mix[64 * l : 64 * l + 64, :], grams[l]) for l in range(3)], axis=0
         ) * ENV_SCALE
         invariants = (edge_mix * pooled).astype(BF16)
-        update = mm(w_up_t_ref[t], jnp.concatenate([latent_b, invariants, spare], axis=0))
+        update = mm(w_up_ref[t], jnp.concatenate([latent_b, invariants], axis=0), TN)
         gate = sigmoid(update)
         act = update * gate
         edge_mix_ref[t] = edge_mix
@@ -300,7 +331,9 @@
             lhs_ref[l - 1, t] = jnp.concatenate([pool_l, mix_l], axis=0)
             rhs_ref[l - 1, t] = jnp.concatenate([mix_l, pool_l], axis=0)
         back_ref[...] = mm(
-            w_mix_ref[t], jnp.concatenate([d_edge_mix, d_env_mix, spare, spare], axis=0)
+            jnp.concatenate([w_edge_t_ref[t], w_env_t_ref[t]], axis=0),
+            jnp.concatenate([d_edge_mix, d_env_mix], axis=0),
+            TN,
         )
         d_latent_ref[...] = d_latent + joined_ref[pl.ds(0, 256), :] + back_ref[...]
         return d_env
@@ -310,7 +343,9 @@
     d_env = d_env + jnp.sum(d_latent * act1, axis=0, keepdims=True)
     d_two = (d_latent * envelope * slope1).astype(BF16)
     d_pre = mm(w_two_ref[...], d_two) * slope0
-    d_radial = mm_high(w_rad_ref[...], d_pre)
+    w_back = jnp.concatenate([w_top[:8, :], w_rest[:8, :]], axis=0).astype(BF16)
+    d_radial = mm(w_back, d_pre.astype(BF16))
+    d_radial = d_radial[:8, :] + d_radial[8:, :]
     d_radius = jnp.sum(
         d_radial * radial * shift, axis=0, keepdims=True
     ) * (-2.0 / (BASIS_WIDTH * BASIS_WIDTH))
@@ -322,10 +357,10 @@
     d_sph = []
     for l, rows in ((1, sph[:3]), (2, sph[3:])):
         pairs = jnp.where(same_center, mm(both(lhs_ref, l), both(rhs_ref, l), TN), 0.0)
-        top, rest = split(pairs)
         fill = [zero_row] * (8 - len(rows))
-        ya, yb = split(jnp.concatenate(list(rows) + fill, axis=0))
-        got = mm(ya, top) + mm(yb, top) + mm(ya, rest)
+        y_top, y_rest = halves(jnp.concatenate(list(rows) + fill, axis=0))
+        got = mm(jnp.concatenate([y_top, y_rest], axis=0).astype(BF16), pairs.astype(BF16))
+        got = got[:8, :] + got[8:, :]
         d_sph += [got[i : i + 1, :] for i in range(len(rows))]
     d1, d2, d3, d4, d5, d6, d7, d8 = d_sph
     du = [
@@ -342,26 +377,22 @@
         msg_ref[pl.ds(12 + r, 1), :] = energy[:, r * LANES : (r + 1) * LANES]
 
 
-def spread(slot_rows, value_rows):
-    chans = len(value_rows[0])
+def spread(entries, chans):
     sub32 = lax.broadcasted_iota(jnp.int32, (32, LANES), 0)
     sub128 = lax.broadcasted_iota(jnp.int32, (LANES, LANES), 0)
-    total = jnp.zeros((2 * chans * 32, LANES), F32)
-    for first in range(0, len(slot_rows), 2):
+    pieces = len(entries[0][2]) // chans
+    total = jnp.zeros((pieces * chans * 32, LANES), F32)
+    for first in range(0, len(entries), 2):
         a_parts, b_parts = [], []
-        for slot, values in zip(slot_rows[first : first + 2], value_rows[first : first + 2]):
-            here = sub32 == (slot >> 7)
-            pieces = []
-            for value in values:
-                top, rest = split(value)
-                pieces.append(jnp.where(here, top.astype(F32), 0.0))
-                pieces.append(jnp.where(here, rest.astype(F32), 0.0))
-            a_parts.append(jnp.concatenate(pieces, axis=0))
-            b_parts.append(jnp.where(sub128 == (slot & 127), 1.0, 0.0))
+        for high, low, values in entries[first : first + 2]:
+            here = sub32 == high
+            a_parts.append(jnp.concatenate([jnp.where(here, v, 0.0) for v in values], axis=0))
+            b_parts.append(jnp.where(sub128 == low, 1.0, 0.0))
         a = jnp.concatenate(a_parts, axis=1).astype(BF16)
         b = jnp.concatenate(b_parts, axis=1).astype(BF16)
         total = total + mm(a, b, NT)
-    return [total[64 * c : 64 * c + 32, :] + total[64 * c + 32 : 64 * c + 64, :] for c in range(chans)]
+    tables = [total[32 * i : 32 * i + 32, :] for i in range(pieces * chans)]
+    return [sum(tables[c * pieces + 1 : (c + 1) * pieces], tables[c * pieces]) for c in range(chans)]
 
 
 def store_flat(ref, lead, table):
@@ -371,63 +402,102 @@
 
 
 def home_kernel(msg_ref, slot_ref, force_ref, atom_ref):
-    slot_rows, value_rows, energies = [], [], []
-    for r in range(4):
-        grads = [msg_ref[pl.ds(4 * c + r, 1), :] for c in range(3)]
-        slot_rows.append(slot_ref[pl.ds(32 + r, 1), :])
-        value_rows.append([-g for g in grads])
-    for r in range(4):
-        grads = [msg_ref[pl.ds(4 * c + r, 1), :] for c in range(3)]
-        slot_rows.append(slot_ref[pl.ds(36 + r, 1), :])
-        value_rows.append(grads)
-    for c, table in enumerate(spread(slot_rows, value_rows)):
+    top, rest = halves(msg_ref[...])
+    slots = slot_ref[pl.ds(32, 8), :]
+    high, low = slots >> 7, slots & 127
+
+    def entry(row, values):
+        return (high[row : row + 1, :], low[row : row + 1, :], values)
+
+    def parts(c, r):
+        return [top[4 * c + r : 4 * c + r + 1, :], rest[4 * c + r : 4 * c + r + 1, :]]
+
+    grads = [sum((parts(c, r) for c in range(3)), []) for r in range(4)]
+    entries = [entry(r, [-g for g in grads[r]]) for r in range(4)]
+    entries += [entry(4 + r, grads[r]) for r in range(4)]
+    for c, table in enumerate(spread(entries, 3)):
         force_ref[c] = table
-    energies = [[msg_ref[pl.ds(12 + r, 1), :]] for r in range(4)]
-    store_flat(atom_ref, (0,), spread(slot_rows[4:], energies)[0])
-
-
-def return_kernel(own_ref, below_ref, above_ref, slot_ref, force_in_ref, force_ref):
-    by_dy = {-1: below_ref, 0: own_ref, 1: above_ref}
-    slot_rows, value_rows = [], []
+    store_flat(atom_ref, (0,), spread([entry(4 + r, parts(3, r)) for r in range(4)], 1)[0])
+
+
+def return_kernel(where_ref, own_ref, even_ref, odd_ref, slot_ref, force_in_ref, force_ref, grid_ref):
+    arrange(where_ref[0], where_ref[1], own_ref, even_ref, odd_ref, grid_ref)
+    slots = slot_ref[pl.ds(0, 32), :]
+    high, low = slots >> 7, slots & 127
+    entries = []
     for o, (dx, dy) in enumerate(DIRS):
+        top, rest = halves(grid_ref[dy + 1, dx + 1])
         for r in range(4):
-            slot_rows.append(slot_ref[pl.ds(4 * o + r, 1), :])
-            value_rows.append(
-                [by_dy[dy][dx + 1, pl.ds(4 * c + r, 1), :] for c in range(3)]
-            )
-    for c, table in enumerate(spread(slot_rows, value_rows)):
+            values = []
+            for c in range(3):
+                row = slice(4 * c + r, 4 * c + r + 1)
+                values += [top[row, :], rest[row, :]]
+            row = slice(4 * o + r, 4 * o + r + 1)
+            entries.append((high[row, :], low[row, :], values))
+    for c, table in enumerate(spread(entries, 3)):
         store_flat(force_ref, (c,), force_in_ref[c] - table)
 
 
-def whole(count, smem=()):
-    return [
-        pl.BlockSpec(memory_space=pltpu.SMEM if i in smem else pltpu.VMEM) for i in range(count)
-    ]
-
-
-def call(kernel, outs, args, smem=(), scratch=(), cost=None):
+def call(kernel, outs, args, smem=(), scratch=(), hbm=False):
     many = isinstance(outs, (list, tuple))
+    inside = pl.BlockSpec(memory_space=pltpu.VMEM)
+    scalar = pl.BlockSpec(memory_space=pltpu.SMEM)
+    outside = pl.BlockSpec(memory_space=pltpu.HBM)
     return pl.pallas_call(
         kernel,
         out_shape=outs,
-        in_specs=whole(len(args), smem),
-        out_specs=whole(len(outs)) if many else whole(1)[0],
+        in_specs=[outside if hbm else scalar if i in smem else inside for i in range(len(args))],
+        out_specs=[inside] * len(outs) if many else inside,
         scratch_shapes=list(scratch),
-        compiler_params=pltpu.CompilerParams(vmem_limit_bytes=VMEM_LIMIT),
+        compiler_params=pltpu.CompilerParams(vmem_limit_bytes=WHOLE_VMEM if hbm else VMEM_LIMIT),
     )(*args)
 
 
-def shift(x, axis, step):
-    count = lax.axis_size(axis)
-    return lax.ppermute(x, axis, [(i, (i + step) % count) for i in range(count)])
-
-
-def around(x, axis):
-    return shift(x, axis, 1), shift(x, axis, -1)
+def exchange(to_even, to_odd, axis):
+    nx, ny = lax.axis_size("gx"), lax.axis_size("gy")
+    even, odd = [], []
+    for i in range(nx):
+        for j in range(ny):
+            k, count = (i, nx) if axis == "gx" else (j, ny)
+            pair = k ^ 1
+            other = ((k + 1) ^ 1) - 1
+            ends = other < 0 or other >= count
+            if axis == "gx":
+                to = (pair, j)
+                far = (i, j ^ 1) if ends else (other, j)
+            else:
+                to = (i, pair)
+                far = (i ^ 1, j) if ends else (i, other)
+            even.append((i * ny + j, to[0] * ny + to[1]))
+            odd.append((i * ny + j, far[0] * ny + far[1]))
+    axes = ("gx", "gy")
+    return lax.ppermute(to_even, axes, even), lax.ppermute(to_odd, axes, odd)
 
 
 def shaped(*dims, dtype=F32):
     return jax.ShapeDtypeStruct(dims, dtype)
+
+
+def edge_call(layers, args):
+    return call(
+        lambda *refs: edge_kernel(layers, *refs),
+        shaped(16, LANES),
+        args,
+        smem=(0,),
+        scratch=(
+            pltpu.VMEM((2, layers, 128, EDGES), BF16),
+            pltpu.VMEM((2, layers, 128, EDGES), BF16),
+            pltpu.VMEM((256, EDGES), F32),
+            pltpu.VMEM((448, EDGES), F32),
+            pltpu.VMEM((256, EDGES), F32),
+            pltpu.VMEM((256, EDGES), F32),
+            pltpu.VMEM((layers, 192, EDGES), F32),
+            pltpu.VMEM((layers, 192, EDGES), BF16),
+            pltpu.VMEM((layers, 192, EDGES), F32),
+            pltpu.VMEM((layers, 256, EDGES), F32),
+            pltpu.VMEM((layers, 256, EDGES), F32),
+        ),
+    )
 
 
 def per_device(
@@ -458,13 +528,27 @@
     grid = (lax.axis_size("gx"), lax.axis_size("gy"))
     place = jnp.stack([lax.axis_index("gx"), lax.axis_index("gy")]).astype(jnp.int32)
 
-    msg = call(send_kernel, shaped(24, LANES), (pos, kind, mig, nbrs))
-    left, right = around(msg, "gx")
-    column = jnp.stack([left, msg, right])
+    odd_y = (place[1] & 1) > 0
+
+    msg = call(
+        send_kernel,
+        shaped(24, LANES),
+        (pos, kind, mig, nbrs),
+        hbm=True,
+        scratch=(
+            pltpu.VMEM((3, 1, SLOTS), F32),
+            pltpu.VMEM((1, SLOTS), jnp.int32),
+            pltpu.VMEM((8, MOVES), jnp.int32),
+            pltpu.VMEM((1, EDGES), jnp.int32),
+            pltpu.SemaphoreType.DMA((4,)),
+        ),
+    )
+    even, odd = exchange(msg, msg, "gx")
+    column = jnp.stack([even, msg, odd])
     kept = call(keep_kernel, shaped(4, 24, LANES), (pos, kind, mig))
-    below, above = around(column, "gy")
-
-    to_left, to_right, same, mids, slots, arrived = call(
+    even, odd = exchange(column, column, "gy")
+
+    to_even, to_odd, same, mids, slots, arrived = call(
         lambda *refs: answer_kernel(grid, *refs),
         (
             shaped(3, 16, LANES),
@@ -474,55 +558,43 @@
             shaped(40, LANES, dtype=jnp.int32),
             shaped(2, 8, LANES),
         ),
-        (place, column, below, above, ghosts, centers, kept),
+        (place, column, even, odd, ghosts, centers, kept),
         smem=(0,),
-    )
-    from_left = shift(to_right, "gx", 1)
-    from_right = shift(to_left, "gx", -1)
-    same = same + from_left + from_right
-    from_below = shift(same[2], "gy", 1)
-    from_above = shift(same[0], "gy", -1)
+        scratch=(pltpu.VMEM((3, 3, 24, LANES), F32),),
+    )
+    even, odd = exchange(to_even, to_odd, "gx")
 
     stay = kept[:3].reshape(3, 24 * LANES)[:, :SLOTS]
     late = arrived.reshape(2, 8, 2, MOVES).transpose(0, 2, 1, 3).reshape(4, 8 * MOVES)[:3]
     owned_positions = jnp.concatenate([stay, late], 1).reshape(3, 1, 1, OWNED)
 
-    w_in = jnp.concatenate([w_radial, w_kind_center, w_kind_neigh], 0)
-    w_in_t = jnp.pad(w_in, ((0, LANES - 16), (0, 0))).T
-    w_mix = jnp.concatenate([w_edge, w_env], 2)
-    w_mix_wide = jnp.pad(w_mix, ((0, 0), (0, 0), (0, LANES)))
-    w_up_t = jnp.pad(w_update, ((0, 0), (0, 64), (0, 0))).transpose(0, 2, 1)
-    grad = call(
-        lambda *refs: edge_kernel(layers, *refs),
-        shaped(16, LANES),
+    same, owned_positions = lax.optimization_barrier((same, owned_positions))
+    same = same + even + odd
+    down, up = same[0], same[2]
+    even, odd = exchange(jnp.where(odd_y, down, up), jnp.where(odd_y, up, down), "gy")
+
+    grad = edge_call(
+        layers,
         (
-            blocks, same, from_below, from_above, mids, centers, edge_center.reshape(EDGES, 1),
-            w_in_t, w_radial, w_two.T, w_two, w_mix.transpose(0, 2, 1), w_mix_wide, w_up_t, w_update,
+            blocks, same, even, odd, mids, centers, edge_center.reshape(EDGES, 1),
+            w_radial, w_kind_center, w_kind_neigh, w_two,
+            w_edge.transpose(0, 2, 1), w_env.transpose(0, 2, 1), w_update,
             w_out.astype(F32).reshape(-1, 1),
         ),
-        smem=(0,),
-        scratch=(
-            pltpu.VMEM((2, layers, 128, EDGES), BF16),
-            pltpu.VMEM((2, layers, 128, EDGES), BF16),
-            pltpu.VMEM((256, EDGES), F32),
-            pltpu.VMEM((448, EDGES), F32),
-            pltpu.VMEM((256, EDGES), F32),
-            pltpu.VMEM((256, EDGES), F32),
-            pltpu.VMEM((layers, 192, EDGES), F32),
-            pltpu.VMEM((layers, 192, EDGES), BF16),
-            pltpu.VMEM((layers, 192, EDGES), F32),
-            pltpu.VMEM((layers, 256, EDGES), F32),
-            pltpu.VMEM((layers, 256, EDGES), F32),
-        ),
-    )
-    left, right = around(grad, "gx")
-    column = jnp.stack([left, grad, right])
+    )
+    even, odd = exchange(grad, grad, "gx")
     force_home, atoms = call(
         home_kernel, (shaped(3, 32, LANES), shaped(1, 1, OWNED)), (grad, slots)
     )
-    below, above = around(column, "gy")
+    column = jnp.stack([even, grad, odd])
+    column, force_home, atoms = lax.optimization_barrier((column, force_home, atoms))
+    even, odd = exchange(column, column, "gy")
     forces = call(
-        return_kernel, shaped(3, 1, OWNED), (column, below, above, slots, force_home)
+        return_kernel,
+        shaped(3, 1, OWNED),
+        (place, column, even, odd, slots, force_home),
+        smem=(0,),
+        scratch=(pltpu.VMEM((3, 3, 16, LANES), F32),),
     )
     return (owned_positions, forces.reshape(3, 1, 1, OWNED), atoms)
 

time: 56 us -> 50.5 us (0.902)
  the two profiles are of different devices: /device:TPU:14 before, /device:TPU:26 now
where the time goes in v2:
time: 50.5 us; the launch traced here: 49.8 us
  starting transfers between devices  18 us (36%)
  waiting for transfers between devices  14.2 us (28%)
  Pallas kernels  12.5 us (25%)
  local copies, waits for them, and re-layouts  3.34 us (7%)
  between operations  1.52 us (3%)
    ppermute x12, starting transfers between devices, exchange(): return (lax.ppermute(to_even, axes, even), lax.ppermute(to_odd, axes, odd))  18 us
    ppermute x12, waiting for transfers between devices, exchange(): return (lax.ppermute(to_even, axes, even), lax.ppermute(to_odd, axes, odd))  14.2 us
    pallas_call x6, Pallas kernels, call(): pl.pallas_call(kernel, out_shape=outs, in_specs=[outside if hbm else scal...  12.5 us
    unnamed x30, local copies, waits for them, and re-layouts  2.24 us
  transfers between devices with their start and end apart: 12, of which 9 were waited for; matrix products, arithmetic and copies ran while one was open for 2% of the time, Pallas kernels for 2%

profile of v2, /device:TPU:26, one launch (start us, length us, event | category | flops | bytes accessed | tf_op | source)
XLA Modules:
  0.0 49.8 jit_solution(10936429363384887672)
XLA Ops:
  0.6 1.7 %shard_map.166 = f32[24,128]{1,0:T(8,128)} custom-call(f32[3,1,2940]{2,1,0:T(1,128)} %bitcast.38, s32[1,2940]{1,0:T(1,128)} %bitcast.41, s32[8,64]{1,0:T(8,128)} %bitcast.47, s32[1,512]{1,0:T(1,128)} %bitcast.58), custom_call_target="tpu_custom_call" | custom-call | tf_op jit(solution)/shard_map/pallas_call | solution.py:446
  2.3 1.8 %collective-permute-start.1 = (f32[24,128]{1,0:T(8,128)}, f32[24,128]{1,0:T(8,128)S(1)}, u32[]{:S(2)}, u32[]{:S(2)}) collective-permute-start(f32[24,128]{1,0:T(8,128)} %shard_map.166), channel_id=1, source_target_pairs={{0,1},{1,0},{2,3},{3,2},{4,5},{5,4},{6,7},{7,6},{8,9},{9,8},{10,11... | collective-permute-start | bytes 36872 | tf_op jit(solution)/shard_map/ppermute | solution.py:474
  4.1 0.3 collective-permute-start
  4.4 0.8 %copy-done.3 = f32[3,1,1,2940]{3,2,1,0:T(1,128)S(1)} copy-done((f32[3,1,1,2940]{3,2,1,0:T(1,128)S(1)}, f32[3,1,1,2940]{3,2,1,0:T(1,128)}, u32[]{:S(2)}) %copy-start.3) | copy-done | bytes 35304
  5.2 0.7 %copy-done.5 = s32[1,1,2940]{2,1,0:T(1,128)S(1)} copy-done((s32[1,1,2940]{2,1,0:T(1,128)S(1)}, s32[1,1,2940]{2,1,0:T(1,128)}, u32[]{:S(2)}) %copy-start.5) | copy-done | bytes 11784
  5.9 0.7 %copy-done.8 = s32[1,1,8,64]{3,2,1,0:T(8,128)S(1)} copy-done((s32[1,1,8,64]{3,2,1,0:T(8,128)S(1)}, s32[1,1,8,64]{3,2,1,0:T(8,128)}, u32[]{:S(2)}) %copy-start.8) | copy-done | bytes 2072
  6.5 0.3 shard_map.167.refs_6_
  6.8 0.4 collective-permute-done.1
  7.2 0.8 %collective-permute-done = f32[24,128]{1,0:T(8,128)S(1)} collective-permute-done((f32[24,128]{1,0:T(8,128)}, f32[24,128]{1,0:T(8,128)S(1)}, u32[]{:S(2)}, u32[]{:S(2)}) %collective-permute-start) | collective-permute-done | bytes 12320 | tf_op jit(solution)/shard_map/ppermute | solution.py:474
  8.0 5.0 %collective-permute-start.3 = (f32[3,24,128]{2,1,0:T(8,128)S(1)}, f32[3,24,128]{2,1,0:T(8,128)S(1)}, u32[]{:S(2)}, u32[]{:S(2)}) collective-permute-start(f32[3,24,128]{2,1,0:T(8,128)S(1)} %pad_maximum_fusion.1.refs_1_), channel_id=1, source_target_pairs={{0,32},{1,2},{2,1},{3,4},{4,3},{5,6},{6,5},{7,8},{8,7},{9,10},{10,... | collective-permute-start | bytes 110600 | tf_op jit(solution)/shard_map/ppermute | solution.py:474
  13.1 1.9 %collective-permute-done.3.refs_3_ = f32[3,24,128]{2,1,0:T(8,128)S(1)} collective-permute-done((f32[3,24,128]{2,1,0:T(8,128)S(1)}, f32[3,24,128]{2,1,0:T(8,128)S(1)}, u32[]{:S(2)}, u32[]{:S(2)}) %collective-permute-start.3) | collective-permute-done | bytes 36896 | tf_op jit(solution)/shard_map/ppermute | solution.py:474
  15.0 2.0 %shard_map.168 = (f32[3,16,128]{2,1,0:T(8,128)S(1)}, f32[3,16,128]{2,1,0:T(8,128)S(1)}, f32[3,16,128]{2,1,0:T(8,128)S(1)}, f32[16,128]{1,0:T(8,128)S(1)}, s32[40...) custom-call(s32[2]{0:T(128)S(1)} %pad_add_fusion.refs_0_.where_ref, f32[3,24,128]{2,1,0:T(8,128)S(1)} %pad_maximum_fusion.1.refs_1_, ...), custom_call_target="tpu_custom_call" | custom-call | tf_op jit(solution)/shard_map/pallas_call | solution.py:446
  17.0 0.1 reshape.61
  17.1 0.1 reshape.62
  17.2 1.3 %collective-permute-start.4 = (f32[3,16,128]{2,1,0:T(8,128)S(1)}, f32[3,16,128]{2,1,0:T(8,128)S(1)}, u32[]{:S(2)}, u32[]{:S(2)}) collective-permute-start(f32[3,16,128]{2,1,0:T(8,128)S(1)} %get-tuple-element.20), channel_id=1, source_target_pairs={{0,32},{1,33},{2,34},{3,35},{4,36},{5,37},{6,38},{7,39},{8,40},{9,... | collective-permute-start | bytes 73736 | tf_op jit(solution)/shard_map/ppermute | solution.py:474
  18.5 1.4 %collective-permute-start.5 = (f32[3,16,128]{2,1,0:T(8,128)S(1)}, f32[3,16,128]{2,1,0:T(8,128)S(1)}, u32[]{:S(2)}, u32[]{:S(2)}) collective-permute-start(f32[3,16,128]{2,1,0:T(8,128)S(1)} %get-tuple-element.21), channel_id=1, source_target_pairs={{0,1},{1,0},{2,3},{3,2},{4,5},{5,4},{6,7},{7,6},{8,9},{9,8},{10,11... | collective-permute-start | bytes 73736 | tf_op jit(solution)/shard_map/ppermute | solution.py:474
  20.0 0.6 %reshape.63 = f32[3,1,1,3452]{3,2,1,0:T(1,128)} reshape(f32[3,3452]{1,0:T(4,128)S(1)} %pad_maximum_fusion) | data formatting | bytes 82848 | tf_op jit(solution)/shard_map/reshape | solution.py:569
  20.6 0.5 collective-permute-done.4
  21.1 2.1 %collective-permute-done.5 = f32[3,16,128]{2,1,0:T(8,128)S(1)} collective-permute-done((f32[3,16,128]{2,1,0:T(8,128)S(1)}, f32[3,16,128]{2,1,0:T(8,128)S(1)}, u32[]{:S(2)}, u32[]{:S(2)}) %collective-permute-start.5) | collective-permute-done | bytes 24608 | tf_op jit(solution)/shard_map/ppermute | solution.py:474
  23.2 3.8 %collective-permute-start.7 = (f32[16,128]{1,0:T(8,128)S(1)}, f32[16,128]{1,0:T(8,128)S(1)}, u32[]{:S(2)}, u32[]{:S(2)}) collective-permute-start(f32[16,128]{1,0:T(8,128)S(1)} %get-tuple-element.35), channel_id=1, source_target_pairs={{0,32},{1,2},{2,1},{3,4},{4,3},{5,6},{6,5},{7,8},{8,7},{9,10},{10,... | collective-permute-start | bytes 24584 | tf_op jit(solution)/shard_map/ppermute | solution.py:474
  27.7 0.1 copy.22.refs_14_
  27.9 0.1 copy.21.refs_6_
  28.0 2.0 %collective-permute-done.7.refs_3_ = f32[16,128]{1,0:T(8,128)S(1)} collective-permute-done((f32[16,128]{1,0:T(8,128)S(1)}, f32[16,128]{1,0:T(8,128)S(1)}, u32[]{:S(2)}, u32[]{:S(2)}) %collective-permute-start.7) | collective-permute-done | bytes 8224 | tf_op jit(solution)/shard_map/ppermute | solution.py:474
  30.1 5.9 %shard_map.169.msg_ref = f32[16,128]{1,0:T(8,128)S(1)} custom-call(s32[1]{0:T(128)} %bitcast.35.refs_0_, f32[3,16,128]{2,1,0:T(8,128)S(1)} %add_add_fusion.refs_1_, f32[16,128]{1,0:T(8,128)S(1)} %collective-permute-done.6.refs_2_, f32[16,128]{1,0:T(8,128)S(1)} %collective-permute-done.7.refs_3_, f32[16,128]{1,0:T(8,128)S(1)} %get-tuple-element.22.refs_4_, ...), custom_call_target="tpu_custom_call" | custom-call | tf_op jit(solution)/shard_map/pallas_call | solution.py:446
  36.0 1.5 %collective-permute-start.9 = (f32[16,128]{1,0:T(8,128)S(1)}, f32[16,128]{1,0:T(8,128)S(1)}, u32[]{:S(2)}, u32[]{:S(2)}) collective-permute-start(f32[16,128]{1,0:T(8,128)S(1)} %shard_map.169.msg_ref), channel_id=1, source_target_pairs={{0,1},{1,0},{2,3},{3,2},{4,5},{5,4},{6,7},{7,6},{8,9},{9,8},{10,11... | collective-permute-start | bytes 24584 | tf_op jit(solution)/shard_map/ppermute | solution.py:474
  37.5 0.6 %collective-permute-start.8 = (f32[16,128]{1,0:T(8,128)S(1)}, f32[16,128]{1,0:T(8,128)S(1)}, u32[]{:S(2)}, u32[]{:S(2)}) collective-permute-start(f32[16,128]{1,0:T(8,128)S(1)} %shard_map.169.msg_ref), channel_id=1, source_target_pairs={{0,32},{1,33},{2,34},{3,35},{4,36},{5,37},{6,38},{7,39},{8,40},{9,... | collective-permute-start | bytes 24584 | tf_op jit(solution)/shard_map/ppermute | solution.py:474
  38.1 0.9 %shard_map.170 = (f32[3,32,128]{2,1,0:T(8,128)S(1)}, f32[1,1,3452]{2,1,0:T(1,128)}) custom-call(f32[16,128]{1,0:T(8,128)S(1)} %shard_map.169.msg_ref, s32[40,128]{1,0:T(8,128)S(1)} %get-tuple-element.23.slot_ref), custom_call_target="tpu_custom_call" | custom-call | tf_op jit(solution)/shard_map/pallas_call | solution.py:446
  39.0 1.6 %collective-permute-done.9 = f32[16,128]{1,0:T(8,128)S(1)} collective-permute-done((f32[16,128]{1,0:T(8,128)S(1)}, f32[16,128]{1,0:T(8,128)S(1)}, u32[]{:S(2)}, u32[]{:S(2)}) %collective-permute-start.9) | collective-permute-done | bytes 8224 | tf_op jit(solution)/shard_map/ppermute | solution.py:474
  40.6 0.5 %collective-permute-done.8 = f32[16,128]{1,0:T(8,128)S(1)} collective-permute-done((f32[16,128]{1,0:T(8,128)S(1)}, f32[16,128]{1,0:T(8,128)S(1)}, u32[]{:S(2)}, u32[]{:S(2)}) %collective-permute-start.8) | collective-permute-done | bytes 8224 | tf_op jit(solution)/shard_map/ppermute | solution.py:474
  41.1 2.4 %collective-permute-start.11 = (f32[3,16,128]{2,1,0:T(8,128)S(1)}, f32[3,16,128]{2,1,0:T(8,128)S(1)}, u32[]{:S(2)}, u32[]{:S(2)}) collective-permute-start(f32[3,16,128]{2,1,0:T(8,128)S(1)} %pad_maximum_fusion.2.own_ref), channel_id=1, source_target_pairs={{0,32},{1,2},{2,1},{3,4},{4,3},{5,6},{6,5},{7,8},{8,7},{9,10},{10,... | collective-permute-start | bytes 73736 | tf_op jit(solution)/shard_map/ppermute | solution.py:474
  43.5 4.5 %collective-permute-done.11.odd_ref = f32[3,16,128]{2,1,0:T(8,128)S(1)} collective-permute-done((f32[3,16,128]{2,1,0:T(8,128)S(1)}, f32[3,16,128]{2,1,0:T(8,128)S(1)}, u32[]{:S(2)}, u32[]{:S(2)}) %collective-permute-start.11) | collective-permute-done | bytes 24608 | tf_op jit(solution)/shard_map/ppermute | solution.py:474
  48.0 1.8 %shard_map.171 = f32[3,1,3452]{2,1,0:T(1,128)} custom-call(s32[2]{0:T(128)S(1)} %pad_add_fusion.refs_0_.where_ref, f32[3,16,128]{2,1,0:T(8,128)S(1)} %pad_maximum_fusion.2.own_ref, f32[3,16,128]{2,1,0:T(8,128)S(1)} %collective-permute-done.10.even_ref, f32[3,16,128]{2,1,0:T(8,128)S(1)} %collective-permute-done.11.odd_ref, ...), custom_call_target="tpu_custom_call" | custom-call | tf_op jit(solution)/shard_map/pallas_call | solution.py:446
  (42 shorter events, 0.3 us)
Async XLA Ops:
  2.3 4.9 %collective-permute-start.1 = (f32[24,128]{1,0:T(8,128)}, f32[24,128]{1,0:T(8,128)S(1)}, u32[]{:S(2)}, u32[]{:S(2)}) collective-permute-start(f32[24,128]{1,0:T(8,128)} %shard_map.166), channel_id=1, source_target_pairs={{0,1},{1,0},{2,3},{3,2},{4,5},{5,4},{6,7},{7,6},{8,9},{9,8},{10,11... | collective-permute-start | bytes 36872 | tf_op jit(solution)/shard_map/ppermute | solution.py:474
  4.1 3.9 %collective-permute-start = (f32[24,128]{1,0:T(8,128)}, f32[24,128]{1,0:T(8,128)S(1)}, u32[]{:S(2)}, u32[]{:S(2)}) collective-permute-start(f32[24,128]{1,0:T(8,128)} %shard_map.166), channel_id=1, source_target_pairs={{0,32},{1,33},{2,34},{3,35},{4,36},{5,37},{6,38},{7,39},{8,40},{9,... | collective-permute-start | bytes 36872 | tf_op jit(solution)/shard_map/ppermute | solution.py:474
  4.4 0.8 %copy-start.3 = (f32[3,1,1,2940]{3,2,1,0:T(1,128)S(1)}, f32[3,1,1,2940]{3,2,1,0:T(1,128)}, u32[]{:S(2)}) copy-start(f32[3,1,1,2940]{3,2,1,0:T(1,128)} %param.15) | copy-start | bytes 105844
  5.2 0.7 %copy-start.5 = (s32[1,1,2940]{2,1,0:T(1,128)S(1)}, s32[1,1,2940]{2,1,0:T(1,128)}, u32[]{:S(2)}) copy-start(s32[1,1,2940]{2,1,0:T(1,128)} %param.16) | copy-start | bytes 35284
  5.9 0.7 %copy-start.8 = (s32[1,1,8,64]{3,2,1,0:T(8,128)S(1)}, s32[1,1,8,64]{3,2,1,0:T(8,128)}, u32[]{:S(2)}) copy-start(s32[1,1,8,64]{3,2,1,0:T(8,128)} %param.17) | copy-start | bytes 6148
  6.8 1.2 %copy-start.12 = (f32[24,128]{1,0:T(8,128)S(1)}, f32[24,128]{1,0:T(8,128)}, u32[]{:S(2)}) copy-start(f32[24,128]{1,0:T(8,128)} %shard_map.166) | copy-start | bytes 36868
  8.0 7.0 %collective-permute-start.3 = (f32[3,24,128]{2,1,0:T(8,128)S(1)}, f32[3,24,128]{2,1,0:T(8,128)S(1)}, u32[]{:S(2)}, u32[]{:S(2)}) collective-permute-start(f32[3,24,128]{2,1,0:T(8,128)S(1)} %pad_maximum_fusion.1.refs_1_), channel_id=1, source_target_pairs={{0,32},{1,2},{2,1},{3,4},{4,3},{5,6},{6,5},{7,8},{8,7},{9,10},{10,... | collective-permute-start | bytes 110600 | tf_op jit(solution)/shard_map/ppermute | solution.py:474
  12.9 2.0 %collective-permute-start.2 = (f32[3,24,128]{2,1,0:T(8,128)S(1)}, f32[3,24,128]{2,1,0:T(8,128)S(1)}, u32[]{:S(2)}, u32[]{:S(2)}) collective-permute-start(f32[3,24,128]{2,1,0:T(8,128)S(1)} %pad_maximum_fusion.1.refs_1_), channel_id=1, source_target_pairs={{0,1},{1,0},{2,3},{3,2},{4,5},{5,4},{6,7},{7,6},{8,9},{9,8},{10,11... | collective-permute-start | bytes 110600 | tf_op jit(solution)/shard_map/ppermute | solution.py:474
  13.0 1.9 %copy-start.6 = (s32[1,1,8,1260]{3,2,1,0:T(8,128)S(1)}, s32[1,1,8,1260]{3,2,1,0:T(8,128)}, u32[]{:S(2)}) copy-start(s32[1,1,8,1260]{3,2,1,0:T(8,128)} %param.18) | copy-start | bytes 120964
  13.1 1.9 %copy-start.7 = (s32[1,1,512]{2,1,0:T(1,128)S(1)}, s32[1,1,512]{2,1,0:T(1,128)}, u32[]{:S(2)}) copy-start(s32[1,1,512]{2,1,0:T(1,128)} %param.19) | copy-start | bytes 6148
  15.0 12.7 %copy-start.13 = (bf16[256]{0:T(256)(128)(2,1)S(1)}, bf16[256]{0:T(256)(128)(2,1)}, u32[]{:S(2)}) copy-start(bf16[256]{0:T(256)(128)(2,1)} %param.29) | copy-start | bytes 1540
  15.0 15.0 %copy-start.2 = (bf16[2,256,192]{1,2,0:T(8,128)(2,1)S(1)}, bf16[2,256,192]{1,2,0:T(8,128)(2,1)}, u32[]{:S(2)}) copy-start(bf16[2,256,192]{1,2,0:T(8,128)(2,1)} %param.27) | copy-start | bytes 589828
  17.0 13.0 %copy-start = (bf16[2,448,256]{2,1,0:T(8,128)(2,1)S(1)}, bf16[2,448,256]{2,1,0:T(8,128)(2,1)}, u32[]{:S(2)}) copy-start(bf16[2,448,256]{2,1,0:T(8,128)(2,1)} %refs_13_.1) | copy-start | bytes 1376260
  17.2 3.9 %collective-permute-start.4 = (f32[3,16,128]{2,1,0:T(8,128)S(1)}, f32[3,16,128]{2,1,0:T(8,128)S(1)}, u32[]{:S(2)}, u32[]{:S(2)}) collective-permute-start(f32[3,16,128]{2,1,0:T(8,128)S(1)} %get-tuple-element.20), channel_id=1, source_target_pairs={{0,32},{1,33},{2,34},{3,35},{4,36},{5,37},{6,38},{7,39},{8,40},{9,... | collective-permute-start | bytes 73736 | tf_op jit(solution)/shard_map/ppermute | solution.py:474
  18.5 4.7 %collective-permute-start.5 = (f32[3,16,128]{2,1,0:T(8,128)S(1)}, f32[3,16,128]{2,1,0:T(8,128)S(1)}, u32[]{:S(2)}, u32[]{:S(2)}) collective-permute-start(f32[3,16,128]{2,1,0:T(8,128)S(1)} %get-tuple-element.21), channel_id=1, source_target_pairs={{0,1},{1,0},{2,3},{3,2},{4,5},{5,4},{6,7},{7,6},{8,9},{9,8},{10,11... | collective-permute-start | bytes 73736 | tf_op jit(solution)/shard_map/ppermute | solution.py:474
  23.2 6.8 %collective-permute-start.7 = (f32[16,128]{1,0:T(8,128)S(1)}, f32[16,128]{1,0:T(8,128)S(1)}, u32[]{:S(2)}, u32[]{:S(2)}) collective-permute-start(f32[16,128]{1,0:T(8,128)S(1)} %get-tuple-element.35), channel_id=1, source_target_pairs={{0,32},{1,2},{2,1},{3,4},{4,3},{5,6},{6,5},{7,8},{8,7},{9,10},{10,... | collective-permute-start | bytes 24584 | tf_op jit(solution)/shard_map/ppermute | solution.py:474
  27.0 3.0 %collective-permute-start.6 = (f32[16,128]{1,0:T(8,128)S(1)}, f32[16,128]{1,0:T(8,128)S(1)}, u32[]{:S(2)}, u32[]{:S(2)}) collective-permute-start(f32[16,128]{1,0:T(8,128)S(1)} %get-tuple-element.36), channel_id=1, source_target_pairs={{0,1},{1,0},{2,3},{3,2},{4,5},{5,4},{6,7},{7,6},{8,9},{9,8},{10,11... | collective-permute-start | bytes 24584 | tf_op jit(solution)/shard_map/ppermute | solution.py:474
  27.7 2.3 %copy-start.1 = (bf16[2,256,192]{1,2,0:T(8,128)(2,1)S(1)}, bf16[2,256,192]{1,2,0:T(8,128)(2,1)}, u32[]{:S(2)}) copy-start(bf16[2,256,192]{1,2,0:T(8,128)(2,1)} %param.26) | copy-start | bytes 589828
  27.8 2.2 %copy-start.4 = (bf16[256,256]{1,0:T(8,128)(2,1)S(1)}, bf16[256,256]{1,0:T(8,128)(2,1)}, u32[]{:S(2)}) copy-start(bf16[256,256]{1,0:T(8,128)(2,1)} %refs_10_.1) | copy-start | bytes 393220
  27.8 2.2 %copy-start.9 = (f32[8,256]{1,0:T(8,128)S(1)}, f32[8,256]{1,0:T(8,128)}, u32[]{:S(2)}) copy-start(f32[8,256]{1,0:T(8,128)} %refs_7_.1) | copy-start | bytes 24580
  27.8 2.2 %copy-start.11 = (f32[4,256]{1,0:T(4,128)S(1)}, f32[4,256]{1,0:T(4,128)}, u32[]{:S(2)}) copy-start(f32[4,256]{1,0:T(4,128)} %refs_9_.1) | copy-start | bytes 12292
  28.0 2.0 %copy-start.10 = (f32[4,256]{1,0:T(4,128)S(1)}, f32[4,256]{1,0:T(4,128)}, u32[]{:S(2)}) copy-start(f32[4,256]{1,0:T(4,128)} %refs_8_.1) | copy-start | bytes 12292
  36.0 4.6 %collective-permute-start.9 = (f32[16,128]{1,0:T(8,128)S(1)}, f32[16,128]{1,0:T(8,128)S(1)}, u32[]{:S(2)}, u32[]{:S(2)}) collective-permute-start(f32[16,128]{1,0:T(8,128)S(1)} %shard_map.169.msg_ref), channel_id=1, source_target_pairs={{0,1},{1,0},{2,3},{3,2},{4,5},{5,4},{6,7},{7,6},{8,9},{9,8},{10,11... | collective-permute-start | bytes 24584 | tf_op jit(solution)/shard_map/ppermute | solution.py:474
  37.5 3.7 %collective-permute-start.8 = (f32[16,128]{1,0:T(8,128)S(1)}, f32[16,128]{1,0:T(8,128)S(1)}, u32[]{:S(2)}, u32[]{:S(2)}) collective-permute-start(f32[16,128]{1,0:T(8,128)S(1)} %shard_map.169.msg_ref), channel_id=1, source_target_pairs={{0,32},{1,33},{2,34},{3,35},{4,36},{5,37},{6,38},{7,39},{8,40},{9,... | collective-permute-start | bytes 24584 | tf_op jit(solution)/shard_map/ppermute | solution.py:474
  41.1 6.9 %collective-permute-start.11 = (f32[3,16,128]{2,1,0:T(8,128)S(1)}, f32[3,16,128]{2,1,0:T(8,128)S(1)}, u32[]{:S(2)}, u32[]{:S(2)}) collective-permute-start(f32[3,16,128]{2,1,0:T(8,128)S(1)} %pad_maximum_fusion.2.own_ref), channel_id=1, source_target_pairs={{0,32},{1,2},{2,1},{3,4},{4,3},{5,6},{6,5},{7,8},{8,7},{9,10},{10,... | collective-permute-start | bytes 73736 | tf_op jit(solution)/shard_map/ppermute | solution.py:474
  43.5 4.5 %collective-permute-start.10 = (f32[3,16,128]{2,1,0:T(8,128)S(1)}, f32[3,16,128]{2,1,0:T(8,128)S(1)}, u32[]{:S(2)}, u32[]{:S(2)}) collective-permute-start(f32[3,16,128]{2,1,0:T(8,128)S(1)} %pad_maximum_fusion.2.own_ref), channel_id=1, source_target_pairs={{0,1},{1,0},{2,3},{3,2},{4,5},{5,4},{6,7},{7,6},{8,9},{9,8},{10,11... | collective-permute-start | bytes 73736 | tf_op jit(solution)/shard_map/ppermute | solution.py:474

commit v3 on v2

--- a/solution.py
+++ b/solution.py
@@ -44,6 +44,10 @@
 def halves(x):
     top = x.astype(BF16).astype(F32)
     return top, x - top
+
+
+def column_of(row):
+    return jnp.broadcast_to(row, (8, row.shape[1])).T[:, :1]
 
 
 def lane_pick(row, low):
@@ -95,7 +99,70 @@
         msg_ref[pl.ds(8 * p, 8), :] = picked[2 * p] + pltpu.roll(picked[2 * p + 1], MOVES, 1)
 
 
-def keep_kernel(pos_ref, kind_ref, mig_ref, kept_ref):
+def ghost_slots(pair, listed, inside, ghost_ref):
+    parts = []
+    for d in pair:
+        rank = listed[d].astype(jnp.int32) - (OWNED + GHOSTS * (7 - d))
+        ok = (rank >= 0) & (rank < GHOSTS) & (inside[d] > 0)
+        parts.append(jnp.where(ok, rank, -1))
+    rank = jnp.concatenate(parts, axis=0)
+    high, low = rank >> 7, rank & 127
+    slot = jnp.full((8, LANES), -1, jnp.int32)
+    upper = lax.broadcasted_iota(jnp.int32, (8, LANES), 0) < 4
+    for h in range(10):
+        stop = min((h + 1) * LANES, GHOSTS)
+        rows = []
+        for d in pair:
+            row = ghost_ref[pl.ds(d, 1), h * LANES : stop]
+            if stop - h * LANES < LANES:
+                pad = jnp.full((1, LANES - (stop - h * LANES)), -1, jnp.int32)
+                row = jnp.concatenate([row, pad], axis=1)
+            rows.append(jnp.broadcast_to(row, (8, LANES)))
+        table = jnp.where(upper, rows[0], rows[1])
+        got = jnp.take_along_axis(table, low, axis=1, mode="promise_in_bounds")
+        slot = jnp.where(high == h, got, slot)
+    return jnp.where(slot >= OWNED, -1, slot)
+
+
+def kept_values(slot, kept_ref):
+    high = jnp.where(slot < SLOTS, slot >> 7, -1)
+    low = slot & 127
+    found = [jnp.zeros((8, LANES), F32) for _ in range(4)]
+    for h in range(KEPT_ROWS):
+        here = high == h
+        for c in range(4):
+            got = lane_pick(kept_ref[c, pl.ds(h, 1), :], low)
+            found[c] = jnp.where(here, got, found[c])
+    return found
+
+
+def late_values(slot, arrive_ref, found):
+    late = slot - SLOTS
+    high = jnp.where(late >= 0, late >> 6, -1)
+    low = late & 63
+    found = list(found)
+    for h in range(8):
+        here = high == h
+        for c in range(4):
+            got = lane_pick(arrive_ref[c // 2, pl.ds(h, 1), :], low + MOVES if c % 2 else low)
+            found[c] = jnp.where(here, got, found[c])
+    return found
+
+
+def on_grid(grid, where_ref):
+    nx, ny = grid
+    ix, iy = where_ref[0], where_ref[1]
+    inside = []
+    for dx, dy in DIRS:
+        ok = (ix + dx >= 0) & (ix + dx < nx) & (iy + dy >= 0) & (iy + dy < ny)
+        inside.append(ok.astype(jnp.int32))
+    return inside
+
+
+def keep_kernel(
+    grid, where_ref, pos_ref, kind_ref, mig_ref, column_ref, ghost_ref, center_ref,
+    kept_ref, early_ref, early_slot_ref,
+):
     rows = mig_ref[...]
     rows = jnp.concatenate([rows, jnp.full((8, LANES - MOVES), -1, jnp.int32)], axis=1)
     high, low = rows >> 7, rows & 127
@@ -114,6 +181,21 @@
             axis=0,
         )
         kept_ref[c] = jnp.where(stay[:24, :], table, 0.0)
+    odd_x = where_ref[0] & 1
+    listed = {
+        1: column_ref[2 - 2 * odd_x, pl.ds(16, 4), :],
+        6: column_ref[2 * odd_x, pl.ds(16, 4), :],
+    }
+    near = column_ref[1, pl.ds(16, 4), :].astype(jnp.int32)
+    core = [center_ref[:, r * LANES : (r + 1) * LANES] for r in range(4)]
+    asked = (
+        ghost_slots((1, 6), listed, on_grid(grid, where_ref), ghost_ref),
+        jnp.concatenate([jnp.where(near < OWNED, near, -1)] + core, axis=0),
+    )
+    for g, slot in enumerate(asked):
+        early_slot_ref[pl.ds(8 * g, 8), :] = slot
+        for c, found in enumerate(kept_values(slot, kept_ref)):
+            early_ref[g, c] = found
 
 
 def arrange(ix, iy, own_ref, even_ref, odd_ref, grid_ref):
@@ -127,93 +209,45 @@
 
 
 def answer_kernel(
-    grid, where_ref, own_ref, even_ref, odd_ref, ghost_ref, center_ref, kept_ref,
+    grid, where_ref, own_ref, even_ref, odd_ref, ghost_ref, kept_ref, early_ref, early_slot_ref,
     to_even_ref, to_odd_ref, same_ref, center_out, slot_ref, arrive_ref, grid_ref,
 ):
-    nx, ny = grid
     ix, iy = where_ref[0], where_ref[1]
     arrange(ix, iy, own_ref, even_ref, odd_ref, grid_ref)
-    inside = []
-    for dx, dy in DIRS:
-        ok = (ix + dx >= 0) & (ix + dx < nx) & (iy + dy >= 0) & (iy + dy < ny)
-        inside.append(ok.astype(jnp.int32))
-    for p in range(2):
-        for k, (dx, dy) in enumerate(DIRS):
+    inside = on_grid(grid, where_ref)
+    listed = []
+    for k, (dx, dy) in enumerate(DIRS):
+        listed.append(grid_ref[dy + 1, dx + 1, pl.ds(16, 4), :])
+        for p in range(2):
             row = grid_ref[dy + 1, dx + 1, pl.ds(8 * p + 7 - k, 1), :]
             arrive_ref[p, pl.ds(k, 1), :] = row * inside[k].astype(F32)
-    groups = []
-    for o in range(0, 8, 2):
-        parts = []
-        for d in (o, o + 1):
-            dx, dy = DIRS[d]
-            listed = grid_ref[dy + 1, dx + 1, pl.ds(16, 4), :].astype(jnp.int32)
-            rank = listed - (OWNED + GHOSTS * (7 - d))
-            ok = (rank >= 0) & (rank < GHOSTS) & (inside[d] > 0)
-            parts.append(jnp.where(ok, rank, -1))
-        rank = jnp.concatenate(parts, axis=0)
-        high, low = rank >> 7, rank & 127
-        slot = jnp.full((8, LANES), -1, jnp.int32)
-        upper = lax.broadcasted_iota(jnp.int32, (8, LANES), 0) < 4
-        for h in range(10):
-            stop = min((h + 1) * LANES, GHOSTS)
-            pair = []
-            for d in (o, o + 1):
-                row = ghost_ref[pl.ds(d, 1), h * LANES : stop]
-                if stop - h * LANES < LANES:
-                    pad = jnp.full((1, LANES - (stop - h * LANES)), -1, jnp.int32)
-                    row = jnp.concatenate([row, pad], axis=1)
-                pair.append(jnp.broadcast_to(row, (8, LANES)))
-            table = jnp.where(upper, pair[0], pair[1])
-            got = jnp.take_along_axis(table, low, axis=1, mode="promise_in_bounds")
-            slot = jnp.where(high == h, got, slot)
-        groups.append(jnp.where(slot >= OWNED, -1, slot))
-    near = own_ref[1, pl.ds(16, 4), :].astype(jnp.int32)
-    near = jnp.where(near < OWNED, near, -1)
-    core = jnp.concatenate(
-        [center_ref[:, r * LANES : (r + 1) * LANES] for r in range(4)], axis=0
-    )
-    groups.append(jnp.concatenate([near, core], axis=0))
-    sides = {-1: [], 0: [], 1: []}
-    for q in range(5):
-        slot = groups[q]
-        slot_ref[pl.ds(8 * q, 8), :] = slot
-        late = slot - SLOTS
-        is_late = late >= 0
-        high = jnp.where(is_late, KEPT_ROWS + (late >> 6), slot >> 7)
-        low_a = jnp.where(is_late, late & 63, slot & 127)
-        low_b = jnp.where(is_late, (late & 63) + MOVES, slot & 127)
-        found = [jnp.zeros((8, LANES), F32) for _ in range(4)]
-        for h in range(KEPT_ROWS + 8):
-            here = high == h
-            for c in range(4):
-                if h < KEPT_ROWS:
-                    row = kept_ref[c, pl.ds(h, 1), :]
-                else:
-                    row = arrive_ref[c // 2, pl.ds(h - KEPT_ROWS, 1), :]
-                got = lane_pick(row, low_b if c % 2 else low_a)
-                found[c] = jnp.where(here, got, found[c])
-        for half in range(2):
-            item = 2 * q + half
-            for c in range(4):
-                rows = found[c][4 * half : 4 * half + 4, :]
-                if item < 8:
-                    dx, dy = DIRS[item]
-                    if dx == 0:
-                        same_ref[dy + 1, pl.ds(4 * c, 4), :] = rows
-                    sides[dx].append((dy + 1, 4 * c, rows))
-                elif item == 8:
-                    same_ref[1, pl.ds(4 * c, 4), :] = rows
-                else:
-                    center_out[pl.ds(4 * c, 4), :] = rows
+    values = {}
+    for pair in ((1, 6), (8, 9), (0, 2), (5, 7), (3, 4)):
+        if pair in ((1, 6), (8, 9)):
+            g = 0 if pair == (1, 6) else 1
+            slot = early_slot_ref[pl.ds(8 * g, 8), :]
+            found = [early_ref[g, c] for c in range(4)]
+        else:
+            slot = ghost_slots(pair, listed, inside, ghost_ref)
+            found = kept_values(slot, kept_ref)
+        found = late_values(slot, arrive_ref, found)
+        for half, d in enumerate(pair):
+            rows = slice(4 * half, 4 * half + 4)
+            slot_ref[pl.ds(4 * d, 4), :] = slot[rows, :]
+            values[d] = [found[c][rows, :] for c in range(4)]
     flip = (ix & 1) > 0
-    for (d, start, left), (_, _, right) in zip(sides[-1], sides[1]):
-        to_even_ref[d, pl.ds(start, 4), :] = jnp.where(flip, left, right)
-        to_odd_ref[d, pl.ds(start, 4), :] = jnp.where(flip, right, left)
+    for c in range(4):
+        rows = pl.ds(4 * c, 4)
+        center_out[rows, :] = values[9][c]
+        for y, (lower, mid, upper) in enumerate(((0, 3, 5), (1, 8, 6), (2, 4, 7))):
+            same_ref[y, rows, :] = values[mid][c]
+            to_even_ref[y, rows, :] = jnp.where(flip, values[lower][c], values[upper][c])
+            to_odd_ref[y, rows, :] = jnp.where(flip, values[upper][c], values[lower][c])
 
 
 def edge_kernel(
     layers,
-    blocks_ref, same_ref, below_ref, above_ref, center_ref, core_row_ref, core_col_ref,
+    blocks_ref, same_ref, below_ref, above_ref, center_ref, core_row_ref,
     w_rad_ref, w_kc_ref, w_kn_ref, w_two_ref, w_edge_t_ref, w_env_t_ref, w_up_ref, w_out_ref,
     msg_ref,
     lhs_ref, rhs_ref, back_ref, joined_ref, latent_ref, d_latent_ref, edge_mix_ref, env_mix_ref,
@@ -251,7 +285,8 @@
     ids = (q8 & 3) + 1
     kinds = jnp.where(q8 < 4, kind_c, kind_n)
     onehot = jnp.where(kinds == ids.astype(F32), 1.0, 0.0)
-    same_center = core_col_ref[...] == core_row_ref[...]
+    core_row = core_row_ref[...].astype(F32)
+    same_center = column_of(core_row) == core_row
     zero_row = jnp.zeros((1, EDGES), F32)
 
     def gram(rows):
@@ -308,7 +343,7 @@
         return carry
 
     lax.fori_loop(0, layers, forward, 0)
-    w_out = w_out_ref[...]
+    w_out = column_of(w_out_ref[...].astype(F32))
     read = jnp.sum(latent_ref[...].astype(BF16).astype(F32) * w_out, axis=0, keepdims=True)
     energy = envelope * read
     d_latent_ref[...] = (w_out * envelope).astype(BF16).astype(F32)
@@ -401,32 +436,14 @@
         ref[lead + (slice(None), slice(h * LANES, stop))] = table[h : h + 1, : stop - h * LANES]
 
 
-def home_kernel(msg_ref, slot_ref, force_ref, atom_ref):
-    top, rest = halves(msg_ref[...])
-    slots = slot_ref[pl.ds(32, 8), :]
-    high, low = slots >> 7, slots & 127
-
-    def entry(row, values):
-        return (high[row : row + 1, :], low[row : row + 1, :], values)
-
-    def parts(c, r):
-        return [top[4 * c + r : 4 * c + r + 1, :], rest[4 * c + r : 4 * c + r + 1, :]]
-
-    grads = [sum((parts(c, r) for c in range(3)), []) for r in range(4)]
-    entries = [entry(r, [-g for g in grads[r]]) for r in range(4)]
-    entries += [entry(4 + r, grads[r]) for r in range(4)]
-    for c, table in enumerate(spread(entries, 3)):
-        force_ref[c] = table
-    store_flat(atom_ref, (0,), spread([entry(4 + r, parts(3, r)) for r in range(4)], 1)[0])
-
-
-def return_kernel(where_ref, own_ref, even_ref, odd_ref, slot_ref, force_in_ref, force_ref, grid_ref):
-    arrange(where_ref[0], where_ref[1], own_ref, even_ref, odd_ref, grid_ref)
+def ghost_entries(slot_ref, block_of, wanted):
     slots = slot_ref[pl.ds(0, 32), :]
     high, low = slots >> 7, slots & 127
     entries = []
     for o, (dx, dy) in enumerate(DIRS):
-        top, rest = halves(grid_ref[dy + 1, dx + 1])
+        if (dy == 0) != wanted:
+            continue
+        top, rest = halves(block_of(dx, dy))
         for r in range(4):
             values = []
             for c in range(3):
@@ -434,7 +451,42 @@
                 values += [top[row, :], rest[row, :]]
             row = slice(4 * o + r, 4 * o + r + 1)
             entries.append((high[row, :], low[row, :], values))
-    for c, table in enumerate(spread(entries, 3)):
+    return entries
+
+
+def home_kernel(where_ref, column_ref, slot_ref, force_ref, atom_ref):
+    top, rest = halves(column_ref[1])
+    slots = slot_ref[pl.ds(32, 8), :]
+    high, low = slots >> 7, slots & 127
+    odd_x = where_ref[0] & 1
+
+    def entry(row, values):
+        return (high[row : row + 1, :], low[row : row + 1, :], values)
+
+    def parts(c, r):
+        return [top[4 * c + r : 4 * c + r + 1, :], rest[4 * c + r : 4 * c + r + 1, :]]
+
+    def block_of(dx, dy):
+        return column_ref[2 - 2 * odd_x if dx < 0 else 2 * odd_x]
+
+    grads = [sum((parts(c, r) for c in range(3)), []) for r in range(4)]
+    entries = [entry(r, [-g for g in grads[r]]) for r in range(4)]
+    entries += [entry(4 + r, grads[r]) for r in range(4)]
+    ghosts = [(h, l, [-v for v in values]) for h, l, values in ghost_entries(slot_ref, block_of, True)]
+    for c, table in enumerate(spread(entries + ghosts, 3)):
+        force_ref[c] = table
+    store_flat(atom_ref, (0,), spread([entry(4 + r, parts(3, r)) for r in range(4)], 1)[0])
+
+
+def return_kernel(where_ref, even_ref, odd_ref, slot_ref, force_in_ref, force_ref):
+    odd_x, odd_y = where_ref[0] & 1, where_ref[1] & 1
+
+    def block_of(dx, dy):
+        block = {-1: 2 - 2 * odd_x, 0: 1, 1: 2 * odd_x}[dx]
+        use_even = (odd_y > 0) if dy < 0 else (odd_y == 0)
+        return jnp.where(use_even, even_ref[block], odd_ref[block])
+
+    for c, table in enumerate(spread(ghost_entries(slot_ref, block_of, False), 3)):
         store_flat(force_ref, (c,), force_in_ref[c] - table)
 
 
@@ -471,7 +523,8 @@
             even.append((i * ny + j, to[0] * ny + to[1]))
             odd.append((i * ny + j, far[0] * ny + far[1]))
     axes = ("gx", "gy")
-    return lax.ppermute(to_even, axes, even), lax.ppermute(to_odd, axes, odd)
+    b = lax.optimization_barrier((lax.ppermute(to_odd, axes, odd), lax.ppermute(to_even, axes, even)))
+    return b[1], b[0]
 
 
 def shaped(*dims, dtype=F32):
@@ -545,7 +598,16 @@
     )
     even, odd = exchange(msg, msg, "gx")
     column = jnp.stack([even, msg, odd])
-    kept = call(keep_kernel, shaped(4, 24, LANES), (pos, kind, mig))
+    kept, early, early_slots = call(
+        lambda *refs: keep_kernel(grid, *refs),
+        (
+            shaped(4, 24, LANES),
+            shaped(2, 4, 8, LANES),
+            shaped(16, LANES, dtype=jnp.int32),
+        ),
+        (place, pos, kind, mig, column, ghosts, centers),
+        smem=(0,),
+    )
     even, odd = exchange(column, column, "gy")
 
     to_even, to_odd, same, mids, slots, arrived = call(
@@ -558,7 +620,7 @@
             shaped(40, LANES, dtype=jnp.int32),
             shaped(2, 8, LANES),
         ),
-        (place, column, even, odd, ghosts, centers, kept),
+        (place, column, even, odd, ghosts, kept, early, early_slots),
         smem=(0,),
         scratch=(pltpu.VMEM((3, 3, 24, LANES), F32),),
     )
@@ -568,33 +630,28 @@
     late = arrived.reshape(2, 8, 2, MOVES).transpose(0, 2, 1, 3).reshape(4, 8 * MOVES)[:3]
     owned_positions = jnp.concatenate([stay, late], 1).reshape(3, 1, 1, OWNED)
 
-    same, owned_positions = lax.optimization_barrier((same, owned_positions))
     same = same + even + odd
     down, up = same[0], same[2]
     even, odd = exchange(jnp.where(odd_y, down, up), jnp.where(odd_y, up, down), "gy")
 
+    mids, owned_positions = lax.optimization_barrier((mids, owned_positions))
     grad = edge_call(
         layers,
         (
-            blocks, same, even, odd, mids, centers, edge_center.reshape(EDGES, 1),
+            blocks, same, even, odd, mids, centers,
             w_radial, w_kind_center, w_kind_neigh, w_two,
             w_edge.transpose(0, 2, 1), w_env.transpose(0, 2, 1), w_update,
-            w_out.astype(F32).reshape(-1, 1),
+            w_out.reshape(1, -1),
         ),
     )
     even, odd = exchange(grad, grad, "gx")
+    column = jnp.stack([even, grad, odd])
     force_home, atoms = call(
-        home_kernel, (shaped(3, 32, LANES), shaped(1, 1, OWNED)), (grad, slots)
-    )
-    column = jnp.stack([even, grad, odd])
-    column, force_home, atoms = lax.optimization_barrier((column, force_home, atoms))
+        home_kernel, (shaped(3, 32, LANES), shaped(1, 1, OWNED)), (place, column, slots), smem=(0,)
+    )
     even, odd = exchange(column, column, "gy")
     forces = call(
-        return_kernel,
-        shaped(3, 1, OWNED),
-        (place, column, even, odd, slots, force_home),
-        smem=(0,),
-        scratch=(pltpu.VMEM((3, 3, 16, LANES), F32),),
+        return_kernel, shaped(3, 1, OWNED), (place, even, odd, slots, force_home), smem=(0,)
     )
     return (owned_positions, forces.reshape(3, 1, 1, OWNED), atoms)
 

time: 50.5 us -> 48.8 us (0.966)
  waiting for transfers between devices: 14.2 us -> 17.3 us
  starting transfers between devices: 18 us -> 15.2 us
  local copies, waits for them, and re-layouts: 3.34 us -> 0.91 us
  Pallas kernels: 12.5 us -> 13.4 us
    ppermute x12, waiting for transfers between devices: 14.2 us -> 17.3 us  [the longest x6 15.4 us: exchange(): lax.ppermute(to_odd, axes, odd)]
    ppermute x12, starting transfers between devices: 18 us -> 15.2 us  [the longest x6 13.8 us: exchange(): lax.ppermute(to_odd, axes, odd)]
    unnamed x30, local copies, waits for them, and re-layouts: 2.24 us -> 0.09 us
    pallas_call x6, Pallas kernels: 12.5 us -> 13.4 us  [call(): pl.pallas_call(kernel, out_shape=outs, in_specs=[outside if hbm else scal...]
  transfers between devices with their start and end apart: 12 -> 12, of which waited for: 9 -> 9; matrix products, arithmetic and copies ran while one was open for 2% -> 2% of each run, Pallas kernels for 2% -> 5%
where the time goes in v3:
time: 48.8 us; the launch traced here: 48.6 us
  waiting for transfers between devices  17.3 us (35%)
  starting transfers between devices  15.2 us (31%)
  Pallas kernels  13.4 us (27%)
  between operations  1.51 us (3%)
  local copies, waits for them, and re-layouts  0.91 us (2%)
    ppermute x6, waiting for transfers between devices, exchange(): lax.ppermute(to_odd, axes, odd)  15.4 us
    ppermute x6, starting transfers between devices, exchange(): lax.ppermute(to_odd, axes, odd)  13.8 us
    pallas_call x6, Pallas kernels, call(): pl.pallas_call(kernel, out_shape=outs, in_specs=[outside if hbm else scal...  13.4 us
    ppermute x6, waiting for transfers between devices, exchange(): lax.ppermute(to_even, axes, even)  1.91 us
    ppermute x6, starting transfers between devices, exchange(): lax.ppermute(to_even, axes, even)  1.4 us
  transfers between devices with their start and end apart: 12, of which 9 were waited for; matrix products, arithmetic and copies ran while one was open for 2% of the time, Pallas kernels for 5%

profile of v3, /device:TPU:26, one launch (start us, length us, event | category | flops | bytes accessed | tf_op | source)
XLA Modules:
  0.0 48.6 jit_solution(11923482485264785928)
XLA Ops:
  0.6 1.7 %shard_map.166 = f32[24,128]{1,0:T(8,128)} custom-call(f32[3,1,2940]{2,1,0:T(1,128)} %bitcast.38, s32[1,2940]{1,0:T(1,128)} %bitcast.40, s32[8,64]{1,0:T(8,128)} %bitcast.43, s32[1,512]{1,0:T(1,128)} %bitcast.56), custom_call_target="tpu_custom_call" | custom-call | tf_op jit(solution)/shard_map/pallas_call | solution.py:498
  2.3 0.0 copy-start.12
  2.3 1.8 %collective-permute-start = (f32[24,128]{1,0:T(8,128)}, f32[24,128]{1,0:T(8,128)S(1)}, u32[]{:S(2)}, u32[]{:S(2)}) collective-permute-start(f32[24,128]{1,0:T(8,128)} %shard_map.166), channel_id=1, source_target_pairs={{0,1},{1,0},{2,3},{3,2},{4,5},{5,4},{6,7},{7,6},{8,9},{9,8},{10,11... | collective-permute-start | bytes 36872 | tf_op jit(solution)/shard_map/ppermute | solution.py:526
  4.1 0.3 collective-permute-start.1
  4.4 2.8 %collective-permute-done = f32[24,128]{1,0:T(8,128)S(1)} collective-permute-done((f32[24,128]{1,0:T(8,128)}, f32[24,128]{1,0:T(8,128)S(1)}, u32[]{:S(2)}, u32[]{:S(2)}) %collective-permute-start) | collective-permute-done | bytes 12320 | tf_op jit(solution)/shard_map/ppermute | solution.py:526
  7.2 0.8 %collective-permute-done.1 = f32[24,128]{1,0:T(8,128)S(1)} collective-permute-done((f32[24,128]{1,0:T(8,128)}, f32[24,128]{1,0:T(8,128)S(1)}, u32[]{:S(2)}, u32[]{:S(2)}) %collective-permute-start.1) | collective-permute-done | bytes 12320 | tf_op jit(solution)/shard_map/ppermute | solution.py:526
  8.0 0.0 copy-start.3
  8.0 0.0 copy-start.4
  8.0 4.3 %collective-permute-start.2 = (f32[3,24,128]{2,1,0:T(8,128)S(1)}, f32[3,24,128]{2,1,0:T(8,128)S(1)}, u32[]{:S(2)}, u32[]{:S(2)}) collective-permute-start(f32[3,24,128]{2,1,0:T(8,128)S(1)} %pad_maximum_fusion.1.refs_4_.refs_1_), channel_id=1, source_target_pairs={{0,32},{1,2},{2,1},{3,4},{4,3},{5,6},{6,5},{7,8},{8,7},{9,10},{10,... | collective-permute-start | bytes 110600 | tf_op jit(solution)/shard_map/ppermute | solution.py:526
  12.4 0.1 pad_add_fusion.refs_0_.where_ref
  13.2 1.1 %shard_map.167 = (f32[4,24,128]{2,1,0:T(8,128)S(1)}, f32[2,4,8,128]{3,2,1,0:T(8,128)S(1)}, s32[16,128]{1,0:T(8,128)S(1)}) custom-call(s32[2]{0:T(128)S(1)} %pad_add_fusion.refs_0_.where_ref, f32[3,1,2940]{2,1,0:T(1,128)S(1)} %bitcast.39, s32[1,2940]{1,0:T(1,128)S(1)} %bitcast.41, s32[8,64]{1,0:T(8,128)S(1)} %bitcast.44, ...), custom_call_target="tpu_custom_call" | custom-call | tf_op jit(solution)/shard_map/pallas_call | solution.py:498
  14.3 0.9 %collective-permute-done.2.refs_3_ = f32[3,24,128]{2,1,0:T(8,128)S(1)} collective-permute-done((f32[3,24,128]{2,1,0:T(8,128)S(1)}, f32[3,24,128]{2,1,0:T(8,128)S(1)}, u32[]{:S(2)}, u32[]{:S(2)}) %collective-permute-start.2) | collective-permute-done | bytes 36896 | tf_op jit(solution)/shard_map/ppermute | solution.py:526
  15.1 1.5 %shard_map.168 = (f32[3,16,128]{2,1,0:T(8,128)S(1)}, f32[3,16,128]{2,1,0:T(8,128)S(1)}, f32[3,16,128]{2,1,0:T(8,128)S(1)}, f32[16,128]{1,0:T(8,128)S(1)}, s32[40...) custom-call(s32[2]{0:T(128)S(1)} %pad_add_fusion.refs_0_.where_ref, f32[3,24,128]{2,1,0:T(8,128)S(1)} %pad_maximum_fusion.1.refs_4_.refs_1_, ...), custom_call_target="tpu_custom_call" | custom-call | tf_op jit(solution)/shard_map/pallas_call | solution.py:498
  16.6 1.3 %collective-permute-start.4 = (f32[3,16,128]{2,1,0:T(8,128)S(1)}, f32[3,16,128]{2,1,0:T(8,128)S(1)}, u32[]{:S(2)}, u32[]{:S(2)}) collective-permute-start(f32[3,16,128]{2,1,0:T(8,128)S(1)} %get-tuple-element.39), channel_id=1, source_target_pairs={{0,1},{1,0},{2,3},{3,2},{4,5},{5,4},{6,7},{7,6},{8,9},{9,8},{10,11... | collective-permute-start | bytes 73736 | tf_op jit(solution)/shard_map/ppermute | solution.py:526
  18.0 0.7 %collective-permute-start.5 = (f32[3,16,128]{2,1,0:T(8,128)S(1)}, f32[3,16,128]{2,1,0:T(8,128)S(1)}, u32[]{:S(2)}, u32[]{:S(2)}) collective-permute-start(f32[3,16,128]{2,1,0:T(8,128)S(1)} %get-tuple-element.40), channel_id=1, source_target_pairs={{0,32},{1,33},{2,34},{3,35},{4,36},{5,37},{6,38},{7,39},{8,40},{9,... | collective-permute-start | bytes 73736 | tf_op jit(solution)/shard_map/ppermute | solution.py:526
  18.8 0.1 reshape.56
  18.9 0.1 reshape.57
  18.9 2.5 %collective-permute-done.4 = f32[3,16,128]{2,1,0:T(8,128)S(1)} collective-permute-done((f32[3,16,128]{2,1,0:T(8,128)S(1)}, f32[3,16,128]{2,1,0:T(8,128)S(1)}, u32[]{:S(2)}, u32[]{:S(2)}) %collective-permute-start.4) | collective-permute-done | bytes 24608 | tf_op jit(solution)/shard_map/ppermute | solution.py:526
  21.4 0.4 collective-permute-done.5
  21.8 3.2 %collective-permute-start.6 = (f32[16,128]{1,0:T(8,128)S(1)}, f32[16,128]{1,0:T(8,128)S(1)}, u32[]{:S(2)}, u32[]{:S(2)}) collective-permute-start(f32[16,128]{1,0:T(8,128)S(1)} %get-tuple-element.57), channel_id=1, source_target_pairs={{0,32},{1,2},{2,1},{3,4},{4,3},{5,6},{6,5},{7,8},{8,7},{9,10},{10,... | collective-permute-start | bytes 24584 | tf_op jit(solution)/shard_map/ppermute | solution.py:526
  25.0 0.1 pad_maximum_fusion
  25.1 0.6 %reshape.58 = f32[3,1,1,3452]{3,2,1,0:T(1,128)} reshape(f32[3,3452]{1,0:T(4,128)S(1)} %pad_maximum_fusion) | data formatting | bytes 82848 | tf_op jit(solution)/shard_map/reshape | solution.py:631
  25.7 2.9 %collective-permute-done.6.refs_3_ = f32[16,128]{1,0:T(8,128)S(1)} collective-permute-done((f32[16,128]{1,0:T(8,128)S(1)}, f32[16,128]{1,0:T(8,128)S(1)}, u32[]{:S(2)}, u32[]{:S(2)}) %collective-permute-start.6) | collective-permute-done | bytes 8224 | tf_op jit(solution)/shard_map/ppermute | solution.py:526
  28.7 6.0 %shard_map.169 = f32[16,128]{1,0:T(8,128)S(1)} custom-call(s32[1]{0:T(128)} %bitcast.33.refs_0_, f32[3,16,128]{2,1,0:T(8,128)S(1)} %add_add_fusion.refs_1_, f32[16,128]{1,0:T(8,128)S(1)} %collective-permute-done.7.refs_2_, f32[16,128]{1,0:T(8,128)S(1)} %collective-permute-done.6.refs_3_, f32[16,128]{1,0:T(8,128)S(1)} %get-tuple-element.45.refs_4_, ...), custom_call_target="tpu_custom_call" | custom-call | tf_op jit(solution)/shard_map/pallas_call | solution.py:498
  34.6 1.8 %collective-permute-start.8 = (f32[16,128]{1,0:T(8,128)S(1)}, f32[16,128]{1,0:T(8,128)S(1)}, u32[]{:S(2)}, u32[]{:S(2)}) collective-permute-start(f32[16,128]{1,0:T(8,128)S(1)} %shard_map.169), channel_id=1, source_target_pairs={{0,1},{1,0},{2,3},{3,2},{4,5},{5,4},{6,7},{7,6},{8,9},{9,8},{10,11... | collective-permute-start | bytes 24584 | tf_op jit(solution)/shard_map/ppermute | solution.py:526
  36.4 0.3 collective-permute-start.9
  36.7 2.5 %collective-permute-done.8 = f32[16,128]{1,0:T(8,128)S(1)} collective-permute-done((f32[16,128]{1,0:T(8,128)S(1)}, f32[16,128]{1,0:T(8,128)S(1)}, u32[]{:S(2)}, u32[]{:S(2)}) %collective-permute-start.8) | collective-permute-done | bytes 8224 | tf_op jit(solution)/shard_map/ppermute | solution.py:526
  39.3 0.8 %collective-permute-done.9 = f32[16,128]{1,0:T(8,128)S(1)} collective-permute-done((f32[16,128]{1,0:T(8,128)S(1)}, f32[16,128]{1,0:T(8,128)S(1)}, u32[]{:S(2)}, u32[]{:S(2)}) %collective-permute-start.9) | collective-permute-done | bytes 8224 | tf_op jit(solution)/shard_map/ppermute | solution.py:526
  40.0 1.4 %collective-permute-start.10 = (f32[3,16,128]{2,1,0:T(8,128)S(1)}, f32[3,16,128]{2,1,0:T(8,128)S(1)}, u32[]{:S(2)}, u32[]{:S(2)}) collective-permute-start(f32[3,16,128]{2,1,0:T(8,128)S(1)} %pad_maximum_fusion.2.column_ref), channel_id=1, source_target_pairs={{0,32},{1,2},{2,1},{3,4},{4,3},{5,6},{6,5},{7,8},{8,7},{9,10},{10,... | collective-permute-start | bytes 73736 | tf_op jit(solution)/shard_map/ppermute | solution.py:526
  41.5 1.6 %shard_map.170 = (f32[3,32,128]{2,1,0:T(8,128)S(1)}, f32[1,1,3452]{2,1,0:T(1,128)}) custom-call(s32[2]{0:T(128)S(1)} %pad_add_fusion.refs_0_.where_ref, f32[3,16,128]{2,1,0:T(8,128)S(1)} %pad_maximum_fusion.2.column_ref, s32[40,128]{1,0:T(8,128)S(1)} %get-tuple-element.50.slot_ref), custom_call_target="tpu_custom_call" | custom-call | tf_op jit(solution)/shard_map/pallas_call | solution.py:498
  43.1 3.9 %collective-permute-done.10.odd_ref = f32[3,16,128]{2,1,0:T(8,128)S(1)} collective-permute-done((f32[3,16,128]{2,1,0:T(8,128)S(1)}, f32[3,16,128]{2,1,0:T(8,128)S(1)}, u32[]{:S(2)}, u32[]{:S(2)}) %collective-permute-start.10) | collective-permute-done | bytes 24608 | tf_op jit(solution)/shard_map/ppermute | solution.py:526
  46.9 1.7 %shard_map.171 = f32[3,1,3452]{2,1,0:T(1,128)} custom-call(s32[2]{0:T(128)S(1)} %pad_add_fusion.refs_0_.where_ref, f32[3,16,128]{2,1,0:T(8,128)S(1)} %collective-permute-done.11.even_ref, f32[3,16,128]{2,1,0:T(8,128)S(1)} %collective-permute-done.10.odd_ref, s32[40,128]{1,0:T(8,128)S(1)} %get-tuple-element.50.slot_ref, ...), custom_call_target="tpu_custom_call" | custom-call | tf_op jit(solution)/shard_map/pallas_call | solution.py:498
  (40 shorter events, 0.1 us)
Async XLA Ops:
  2.3 5.7 %copy-start.12 = (f32[24,128]{1,0:T(8,128)S(1)}, f32[24,128]{1,0:T(8,128)}, u32[]{:S(2)}) copy-start(f32[24,128]{1,0:T(8,128)} %shard_map.166) | copy-start | bytes 36868
  2.3 4.9 %collective-permute-start = (f32[24,128]{1,0:T(8,128)}, f32[24,128]{1,0:T(8,128)S(1)}, u32[]{:S(2)}, u32[]{:S(2)}) collective-permute-start(f32[24,128]{1,0:T(8,128)} %shard_map.166), channel_id=1, source_target_pairs={{0,1},{1,0},{2,3},{3,2},{4,5},{5,4},{6,7},{7,6},{8,9},{9,8},{10,11... | collective-permute-start | bytes 36872 | tf_op jit(solution)/shard_map/ppermute | solution.py:526
  4.1 3.9 %collective-permute-start.1 = (f32[24,128]{1,0:T(8,128)}, f32[24,128]{1,0:T(8,128)S(1)}, u32[]{:S(2)}, u32[]{:S(2)}) collective-permute-start(f32[24,128]{1,0:T(8,128)} %shard_map.166), channel_id=1, source_target_pairs={{0,32},{1,33},{2,34},{3,35},{4,36},{5,37},{6,38},{7,39},{8,40},{9,... | collective-permute-start | bytes 36872 | tf_op jit(solution)/shard_map/ppermute | solution.py:526
  8.0 5.1 %copy-start.9 = (s32[1,1,512]{2,1,0:T(1,128)S(1)}, s32[1,1,512]{2,1,0:T(1,128)}, u32[]{:S(2)}) copy-start(s32[1,1,512]{2,1,0:T(1,128)} %param.19) | copy-start | bytes 6148
  8.0 5.1 %copy-start.7 = (s32[1,1,8,64]{3,2,1,0:T(8,128)S(1)}, s32[1,1,8,64]{3,2,1,0:T(8,128)}, u32[]{:S(2)}) copy-start(s32[1,1,8,64]{3,2,1,0:T(8,128)} %param.17) | copy-start | bytes 6148
  8.0 4.5 %copy-start.13 = (bf16[256]{0:T(256)(128)(2,1)S(1)}, bf16[256]{0:T(256)(128)(2,1)}, u32[]{:S(2)}) copy-start(bf16[256]{0:T(256)(128)(2,1)} %param.29) | copy-start | bytes 1540
  8.0 5.1 %copy-start.3 = (s32[1,1,8,1260]{3,2,1,0:T(8,128)S(1)}, s32[1,1,8,1260]{3,2,1,0:T(8,128)}, u32[]{:S(2)}) copy-start(s32[1,1,8,1260]{3,2,1,0:T(8,128)} %param.18) | copy-start | bytes 120964
  8.0 5.1 %copy-start.4 = (f32[3,1,1,2940]{3,2,1,0:T(1,128)S(1)}, f32[3,1,1,2940]{3,2,1,0:T(1,128)}, u32[]{:S(2)}) copy-start(f32[3,1,1,2940]{3,2,1,0:T(1,128)} %param.15) | copy-start | bytes 105844
  8.0 5.1 %copy-start.6 = (s32[1,1,2940]{2,1,0:T(1,128)S(1)}, s32[1,1,2940]{2,1,0:T(1,128)}, u32[]{:S(2)}) copy-start(s32[1,1,2940]{2,1,0:T(1,128)} %param.16) | copy-start | bytes 35284
  8.0 7.1 %collective-permute-start.2 = (f32[3,24,128]{2,1,0:T(8,128)S(1)}, f32[3,24,128]{2,1,0:T(8,128)S(1)}, u32[]{:S(2)}, u32[]{:S(2)}) collective-permute-start(f32[3,24,128]{2,1,0:T(8,128)S(1)} %pad_maximum_fusion.1.refs_4_.refs_1_), channel_id=1, source_target_pairs={{0,32},{1,2},{2,1},{3,4},{4,3},{5,6},{6,5},{7,8},{8,7},{9,10},{10,... | collective-permute-start | bytes 110600 | tf_op jit(solution)/shard_map/ppermute | solution.py:526
  12.4 2.8 %collective-permute-start.3 = (f32[3,24,128]{2,1,0:T(8,128)S(1)}, f32[3,24,128]{2,1,0:T(8,128)S(1)}, u32[]{:S(2)}, u32[]{:S(2)}) collective-permute-start(f32[3,24,128]{2,1,0:T(8,128)S(1)} %pad_maximum_fusion.1.refs_4_.refs_1_), channel_id=1, source_target_pairs={{0,1},{1,0},{2,3},{3,2},{4,5},{5,4},{6,7},{7,6},{8,9},{9,8},{10,11... | collective-permute-start | bytes 110600 | tf_op jit(solution)/shard_map/ppermute | solution.py:526
  13.2 15.4 %copy-start.5 = (bf16[256,256]{1,0:T(8,128)(2,1)S(1)}, bf16[256,256]{1,0:T(8,128)(2,1)}, u32[]{:S(2)}) copy-start(bf16[256,256]{1,0:T(8,128)(2,1)} %refs_9_.1) | copy-start | bytes 393220
  15.1 13.5 %copy-start = (bf16[2,448,256]{2,1,0:T(8,128)(2,1)S(1)}, bf16[2,448,256]{2,1,0:T(8,128)(2,1)}, u32[]{:S(2)}) copy-start(bf16[2,448,256]{2,1,0:T(8,128)(2,1)} %refs_12_.1) | copy-start | bytes 1376260
  16.6 4.8 %collective-permute-start.4 = (f32[3,16,128]{2,1,0:T(8,128)S(1)}, f32[3,16,128]{2,1,0:T(8,128)S(1)}, u32[]{:S(2)}, u32[]{:S(2)}) collective-permute-start(f32[3,16,128]{2,1,0:T(8,128)S(1)} %get-tuple-element.39), channel_id=1, source_target_pairs={{0,1},{1,0},{2,3},{3,2},{4,5},{5,4},{6,7},{7,6},{8,9},{9,8},{10,11... | collective-permute-start | bytes 73736 | tf_op jit(solution)/shard_map/ppermute | solution.py:526
  18.0 3.8 %collective-permute-start.5 = (f32[3,16,128]{2,1,0:T(8,128)S(1)}, f32[3,16,128]{2,1,0:T(8,128)S(1)}, u32[]{:S(2)}, u32[]{:S(2)}) collective-permute-start(f32[3,16,128]{2,1,0:T(8,128)S(1)} %get-tuple-element.40), channel_id=1, source_target_pairs={{0,32},{1,33},{2,34},{3,35},{4,36},{5,37},{6,38},{7,39},{8,40},{9,... | collective-permute-start | bytes 73736 | tf_op jit(solution)/shard_map/ppermute | solution.py:526
  18.8 9.8 %copy-start.2 = (bf16[2,256,192]{1,2,0:T(8,128)(2,1)S(1)}, bf16[2,256,192]{1,2,0:T(8,128)(2,1)}, u32[]{:S(2)}) copy-start(bf16[2,256,192]{1,2,0:T(8,128)(2,1)} %param.27) | copy-start | bytes 589828
  18.9 9.8 %copy-start.1 = (bf16[2,256,192]{1,2,0:T(8,128)(2,1)S(1)}, bf16[2,256,192]{1,2,0:T(8,128)(2,1)}, u32[]{:S(2)}) copy-start(bf16[2,256,192]{1,2,0:T(8,128)(2,1)} %param.26) | copy-start | bytes 589828
  21.8 6.8 %collective-permute-start.6 = (f32[16,128]{1,0:T(8,128)S(1)}, f32[16,128]{1,0:T(8,128)S(1)}, u32[]{:S(2)}, u32[]{:S(2)}) collective-permute-start(f32[16,128]{1,0:T(8,128)S(1)} %get-tuple-element.57), channel_id=1, source_target_pairs={{0,32},{1,2},{2,1},{3,4},{4,3},{5,6},{6,5},{7,8},{8,7},{9,10},{10,... | collective-permute-start | bytes 24584 | tf_op jit(solution)/shard_map/ppermute | solution.py:526
  25.0 3.6 %collective-permute-start.7 = (f32[16,128]{1,0:T(8,128)S(1)}, f32[16,128]{1,0:T(8,128)S(1)}, u32[]{:S(2)}, u32[]{:S(2)}) collective-permute-start(f32[16,128]{1,0:T(8,128)S(1)} %get-tuple-element.56), channel_id=1, source_target_pairs={{0,1},{1,0},{2,3},{3,2},{4,5},{5,4},{6,7},{7,6},{8,9},{9,8},{10,11... | collective-permute-start | bytes 24584 | tf_op jit(solution)/shard_map/ppermute | solution.py:526
  25.1 3.5 %copy-start.8 = (f32[8,256]{1,0:T(8,128)S(1)}, f32[8,256]{1,0:T(8,128)}, u32[]{:S(2)}) copy-start(f32[8,256]{1,0:T(8,128)} %refs_6_.1) | copy-start | bytes 24580
  25.1 3.5 %copy-start.11 = (f32[4,256]{1,0:T(4,128)S(1)}, f32[4,256]{1,0:T(4,128)}, u32[]{:S(2)}) copy-start(f32[4,256]{1,0:T(4,128)} %refs_8_.1) | copy-start | bytes 12292
  25.7 2.9 %copy-start.10 = (f32[4,256]{1,0:T(4,128)S(1)}, f32[4,256]{1,0:T(4,128)}, u32[]{:S(2)}) copy-start(f32[4,256]{1,0:T(4,128)} %refs_7_.1) | copy-start | bytes 12292
  34.6 4.6 %collective-permute-start.8 = (f32[16,128]{1,0:T(8,128)S(1)}, f32[16,128]{1,0:T(8,128)S(1)}, u32[]{:S(2)}, u32[]{:S(2)}) collective-permute-start(f32[16,128]{1,0:T(8,128)S(1)} %shard_map.169), channel_id=1, source_target_pairs={{0,1},{1,0},{2,3},{3,2},{4,5},{5,4},{6,7},{7,6},{8,9},{9,8},{10,11... | collective-permute-start | bytes 24584 | tf_op jit(solution)/shard_map/ppermute | solution.py:526
  36.4 3.7 %collective-permute-start.9 = (f32[16,128]{1,0:T(8,128)S(1)}, f32[16,128]{1,0:T(8,128)S(1)}, u32[]{:S(2)}, u32[]{:S(2)}) collective-permute-start(f32[16,128]{1,0:T(8,128)S(1)} %shard_map.169), channel_id=1, source_target_pairs={{0,32},{1,33},{2,34},{3,35},{4,36},{5,37},{6,38},{7,39},{8,40},{9,... | collective-permute-start | bytes 24584 | tf_op jit(solution)/shard_map/ppermute | solution.py:526
  40.0 6.9 %collective-permute-start.10 = (f32[3,16,128]{2,1,0:T(8,128)S(1)}, f32[3,16,128]{2,1,0:T(8,128)S(1)}, u32[]{:S(2)}, u32[]{:S(2)}) collective-permute-start(f32[3,16,128]{2,1,0:T(8,128)S(1)} %pad_maximum_fusion.2.column_ref), channel_id=1, source_target_pairs={{0,32},{1,2},{2,1},{3,4},{4,3},{5,6},{6,5},{7,8},{8,7},{9,10},{10,... | collective-permute-start | bytes 73736 | tf_op jit(solution)/shard_map/ppermute | solution.py:526
  41.5 5.4 %collective-permute-start.11 = (f32[3,16,128]{2,1,0:T(8,128)S(1)}, f32[3,16,128]{2,1,0:T(8,128)S(1)}, u32[]{:S(2)}, u32[]{:S(2)}) collective-permute-start(f32[3,16,128]{2,1,0:T(8,128)S(1)} %pad_maximum_fusion.2.column_ref), channel_id=1, source_target_pairs={{0,1},{1,0},{2,3},{3,2},{4,5},{5,4},{6,7},{7,6},{8,9},{9,8},{10,11... | collective-permute-start | bytes 73736 | tf_op jit(solution)/shard_map/ppermute | solution.py:526

commit v4 on v3

--- a/solution.py
+++ b/solution.py
@@ -289,6 +289,8 @@
     same_center = column_of(core_row) == core_row
     zero_row = jnp.zeros((1, EDGES), F32)
 
+    together = jnp.where(same_center, 1.0, 0.0).astype(BF16)
+
     def gram(rows):
         top, rest = [], []
         for row in rows:
@@ -298,9 +300,9 @@
         fill = [jnp.zeros((LANES - 3 * len(rows), EDGES), F32)]
         a = jnp.concatenate(top + top + rest + fill, axis=0).astype(BF16)
         b = jnp.concatenate(top + rest + top + fill, axis=0).astype(BF16)
-        return jnp.where(same_center, mm(a, b, TN), 0.0).astype(BF16)
-
-    grams = [jnp.where(same_center, 1.0, 0.0).astype(BF16), gram(sph[:3]), gram(sph[3:])]
+        return mm(a, b, TN).astype(BF16) * together
+
+    grams = [together, gram(sph[:3]), gram(sph[3:])]
 
     w_top, w_rest = halves(
         jnp.concatenate([w_rad_ref[...], w_kc_ref[...], w_kn_ref[...]], axis=0)
@@ -391,10 +393,10 @@
 
     d_sph = []
     for l, rows in ((1, sph[:3]), (2, sph[3:])):
-        pairs = jnp.where(same_center, mm(both(lhs_ref, l), both(rhs_ref, l), TN), 0.0)
+        pairs = mm(both(lhs_ref, l), both(rhs_ref, l), TN).astype(BF16) * together
         fill = [zero_row] * (8 - len(rows))
         y_top, y_rest = halves(jnp.concatenate(list(rows) + fill, axis=0))
-        got = mm(jnp.concatenate([y_top, y_rest], axis=0).astype(BF16), pairs.astype(BF16))
+        got = mm(jnp.concatenate([y_top, y_rest], axis=0).astype(BF16), pairs)
         got = got[:8, :] + got[8:, :]
         d_sph += [got[i : i + 1, :] for i in range(len(rows))]
     d1, d2, d3, d4, d5, d6, d7, d8 = d_sph

time: 48.8 us -> 48.8 us (level)
  no operation moved by 1% of the time
where the time goes in v4:
time: 48.8 us; the launch traced here: 48.5 us
  waiting for transfers between devices  17.3 us (35%)
  starting transfers between devices  15.2 us (31%)
  Pallas kernels  13.4 us (27%)
  between operations  1.51 us (3%)
  local copies, waits for them, and re-layouts  0.91 us (2%)
    ppermute x6, waiting for transfers between devices, exchange(): lax.ppermute(to_odd, axes, odd)  15.4 us
    ppermute x6, starting transfers between devices, exchange(): lax.ppermute(to_odd, axes, odd)  13.8 us
    pallas_call x6, Pallas kernels, call(): pl.pallas_call(kernel, out_shape=outs, in_specs=[outside if hbm else scal...  13.4 us
    ppermute x6, waiting for transfers between devices, exchange(): lax.ppermute(to_even, axes, even)  1.91 us
    ppermute x6, starting transfers between devices, exchange(): lax.ppermute(to_even, axes, even)  1.4 us
  transfers between devices with their start and end apart: 12, of which 9 were waited for; matrix products, arithmetic and copies ran while one was open for 2% of the time, Pallas kernels for 5%

profile of v4, /device:TPU:26, one launch (start us, length us, event | category | flops | bytes accessed | tf_op | source)
XLA Modules:
  0.0 48.5 jit_solution(9927803366889593945)
XLA Ops:
  0.6 1.7 %shard_map.166 = f32[24,128]{1,0:T(8,128)} custom-call(f32[3,1,2940]{2,1,0:T(1,128)} %bitcast.38, s32[1,2940]{1,0:T(1,128)} %bitcast.40, s32[8,64]{1,0:T(8,128)} %bitcast.43, s32[1,512]{1,0:T(1,128)} %bitcast.56), custom_call_target="tpu_custom_call" | custom-call | tf_op jit(solution)/shard_map/pallas_call | solution.py:500
  2.3 1.8 %collective-permute-start = (f32[24,128]{1,0:T(8,128)}, f32[24,128]{1,0:T(8,128)S(1)}, u32[]{:S(2)}, u32[]{:S(2)}) collective-permute-start(f32[24,128]{1,0:T(8,128)} %shard_map.166), channel_id=1, source_target_pairs={{0,1},{1,0},{2,3},{3,2},{4,5},{5,4},{6,7},{7,6},{8,9},{9,8},{10,11... | collective-permute-start | bytes 36872 | tf_op jit(solution)/shard_map/ppermute | solution.py:528
  4.1 0.3 collective-permute-start.1
  4.4 2.8 %collective-permute-done = f32[24,128]{1,0:T(8,128)S(1)} collective-permute-done((f32[24,128]{1,0:T(8,128)}, f32[24,128]{1,0:T(8,128)S(1)}, u32[]{:S(2)}, u32[]{:S(2)}) %collective-permute-start) | collective-permute-done | bytes 12320 | tf_op jit(solution)/shard_map/ppermute | solution.py:528
  7.2 0.8 %collective-permute-done.1 = f32[24,128]{1,0:T(8,128)S(1)} collective-permute-done((f32[24,128]{1,0:T(8,128)}, f32[24,128]{1,0:T(8,128)S(1)}, u32[]{:S(2)}, u32[]{:S(2)}) %collective-permute-start.1) | collective-permute-done | bytes 12320 | tf_op jit(solution)/shard_map/ppermute | solution.py:528
  8.0 0.0 copy-start.3
  8.0 0.0 copy-start.4
  8.0 4.3 %collective-permute-start.2 = (f32[3,24,128]{2,1,0:T(8,128)S(1)}, f32[3,24,128]{2,1,0:T(8,128)S(1)}, u32[]{:S(2)}, u32[]{:S(2)}) collective-permute-start(f32[3,24,128]{2,1,0:T(8,128)S(1)} %pad_maximum_fusion.1.refs_4_.refs_1_), channel_id=1, source_target_pairs={{0,32},{1,2},{2,1},{3,4},{4,3},{5,6},{6,5},{7,8},{8,7},{9,10},{10,... | collective-permute-start | bytes 110600 | tf_op jit(solution)/shard_map/ppermute | solution.py:528
  12.4 0.1 pad_add_fusion.refs_0_.where_ref
  13.2 0.0 copy-start.5
  13.2 1.1 %shard_map.167 = (f32[4,24,128]{2,1,0:T(8,128)S(1)}, f32[2,4,8,128]{3,2,1,0:T(8,128)S(1)}, s32[16,128]{1,0:T(8,128)S(1)}) custom-call(s32[2]{0:T(128)S(1)} %pad_add_fusion.refs_0_.where_ref, f32[3,1,2940]{2,1,0:T(1,128)S(1)} %bitcast.39, s32[1,2940]{1,0:T(1,128)S(1)} %bitcast.41, s32[8,64]{1,0:T(8,128)S(1)} %bitcast.44, ...), custom_call_target="tpu_custom_call" | custom-call | tf_op jit(solution)/shard_map/pallas_call | solution.py:500
  14.3 0.9 %collective-permute-done.2.refs_3_ = f32[3,24,128]{2,1,0:T(8,128)S(1)} collective-permute-done((f32[3,24,128]{2,1,0:T(8,128)S(1)}, f32[3,24,128]{2,1,0:T(8,128)S(1)}, u32[]{:S(2)}, u32[]{:S(2)}) %collective-permute-start.2) | collective-permute-done | bytes 36896 | tf_op jit(solution)/shard_map/ppermute | solution.py:528
  15.1 1.5 %shard_map.168 = (f32[3,16,128]{2,1,0:T(8,128)S(1)}, f32[3,16,128]{2,1,0:T(8,128)S(1)}, f32[3,16,128]{2,1,0:T(8,128)S(1)}, f32[16,128]{1,0:T(8,128)S(1)}, s32[40...) custom-call(s32[2]{0:T(128)S(1)} %pad_add_fusion.refs_0_.where_ref, f32[3,24,128]{2,1,0:T(8,128)S(1)} %pad_maximum_fusion.1.refs_4_.refs_1_, ...), custom_call_target="tpu_custom_call" | custom-call | tf_op jit(solution)/shard_map/pallas_call | solution.py:500
  16.6 1.3 %collective-permute-start.4 = (f32[3,16,128]{2,1,0:T(8,128)S(1)}, f32[3,16,128]{2,1,0:T(8,128)S(1)}, u32[]{:S(2)}, u32[]{:S(2)}) collective-permute-start(f32[3,16,128]{2,1,0:T(8,128)S(1)} %get-tuple-element.39), channel_id=1, source_target_pairs={{0,1},{1,0},{2,3},{3,2},{4,5},{5,4},{6,7},{7,6},{8,9},{9,8},{10,11... | collective-permute-start | bytes 73736 | tf_op jit(solution)/shard_map/ppermute | solution.py:528
  18.0 0.7 %collective-permute-start.5 = (f32[3,16,128]{2,1,0:T(8,128)S(1)}, f32[3,16,128]{2,1,0:T(8,128)S(1)}, u32[]{:S(2)}, u32[]{:S(2)}) collective-permute-start(f32[3,16,128]{2,1,0:T(8,128)S(1)} %get-tuple-element.40), channel_id=1, source_target_pairs={{0,32},{1,33},{2,34},{3,35},{4,36},{5,37},{6,38},{7,39},{8,40},{9,... | collective-permute-start | bytes 73736 | tf_op jit(solution)/shard_map/ppermute | solution.py:528
  18.8 0.1 reshape.56
  18.9 0.1 reshape.57
  18.9 2.5 %collective-permute-done.4 = f32[3,16,128]{2,1,0:T(8,128)S(1)} collective-permute-done((f32[3,16,128]{2,1,0:T(8,128)S(1)}, f32[3,16,128]{2,1,0:T(8,128)S(1)}, u32[]{:S(2)}, u32[]{:S(2)}) %collective-permute-start.4) | collective-permute-done | bytes 24608 | tf_op jit(solution)/shard_map/ppermute | solution.py:528
  21.4 0.4 collective-permute-done.5
  21.8 3.2 %collective-permute-start.6 = (f32[16,128]{1,0:T(8,128)S(1)}, f32[16,128]{1,0:T(8,128)S(1)}, u32[]{:S(2)}, u32[]{:S(2)}) collective-permute-start(f32[16,128]{1,0:T(8,128)S(1)} %get-tuple-element.57), channel_id=1, source_target_pairs={{0,32},{1,2},{2,1},{3,4},{4,3},{5,6},{6,5},{7,8},{8,7},{9,10},{10,... | collective-permute-start | bytes 24584 | tf_op jit(solution)/shard_map/ppermute | solution.py:528
  25.0 0.1 pad_maximum_fusion
  25.1 0.6 %reshape.58 = f32[3,1,1,3452]{3,2,1,0:T(1,128)} reshape(f32[3,3452]{1,0:T(4,128)S(1)} %pad_maximum_fusion) | data formatting | bytes 82848 | tf_op jit(solution)/shard_map/reshape | solution.py:633
  25.7 2.9 %collective-permute-done.6.refs_3_ = f32[16,128]{1,0:T(8,128)S(1)} collective-permute-done((f32[16,128]{1,0:T(8,128)S(1)}, f32[16,128]{1,0:T(8,128)S(1)}, u32[]{:S(2)}, u32[]{:S(2)}) %collective-permute-start.6) | collective-permute-done | bytes 8224 | tf_op jit(solution)/shard_map/ppermute | solution.py:528
  28.7 5.9 %shard_map.169 = f32[16,128]{1,0:T(8,128)S(1)} custom-call(s32[1]{0:T(128)} %bitcast.33.refs_0_, f32[3,16,128]{2,1,0:T(8,128)S(1)} %add_add_fusion.refs_1_, f32[16,128]{1,0:T(8,128)S(1)} %collective-permute-done.7.refs_2_, f32[16,128]{1,0:T(8,128)S(1)} %collective-permute-done.6.refs_3_, f32[16,128]{1,0:T(8,128)S(1)} %get-tuple-element.45.refs_4_, ...), custom_call_target="tpu_custom_call" | custom-call | tf_op jit(solution)/shard_map/pallas_call | solution.py:500
  34.6 1.8 %collective-permute-start.8 = (f32[16,128]{1,0:T(8,128)S(1)}, f32[16,128]{1,0:T(8,128)S(1)}, u32[]{:S(2)}, u32[]{:S(2)}) collective-permute-start(f32[16,128]{1,0:T(8,128)S(1)} %shard_map.169), channel_id=1, source_target_pairs={{0,1},{1,0},{2,3},{3,2},{4,5},{5,4},{6,7},{7,6},{8,9},{9,8},{10,11... | collective-permute-start | bytes 24584 | tf_op jit(solution)/shard_map/ppermute | solution.py:528
  36.3 0.3 collective-permute-start.9
  36.7 2.5 %collective-permute-done.8 = f32[16,128]{1,0:T(8,128)S(1)} collective-permute-done((f32[16,128]{1,0:T(8,128)S(1)}, f32[16,128]{1,0:T(8,128)S(1)}, u32[]{:S(2)}, u32[]{:S(2)}) %collective-permute-start.8) | collective-permute-done | bytes 8224 | tf_op jit(solution)/shard_map/ppermute | solution.py:528
  39.2 0.8 %collective-permute-done.9 = f32[16,128]{1,0:T(8,128)S(1)} collective-permute-done((f32[16,128]{1,0:T(8,128)S(1)}, f32[16,128]{1,0:T(8,128)S(1)}, u32[]{:S(2)}, u32[]{:S(2)}) %collective-permute-start.9) | collective-permute-done | bytes 8224 | tf_op jit(solution)/shard_map/ppermute | solution.py:528
  40.0 1.4 %collective-permute-start.10 = (f32[3,16,128]{2,1,0:T(8,128)S(1)}, f32[3,16,128]{2,1,0:T(8,128)S(1)}, u32[]{:S(2)}, u32[]{:S(2)}) collective-permute-start(f32[3,16,128]{2,1,0:T(8,128)S(1)} %pad_maximum_fusion.2.column_ref), channel_id=1, source_target_pairs={{0,32},{1,2},{2,1},{3,4},{4,3},{5,6},{6,5},{7,8},{8,7},{9,10},{10,... | collective-permute-start | bytes 73736 | tf_op jit(solution)/shard_map/ppermute | solution.py:528
  41.4 1.6 %shard_map.170 = (f32[3,32,128]{2,1,0:T(8,128)S(1)}, f32[1,1,3452]{2,1,0:T(1,128)}) custom-call(s32[2]{0:T(128)S(1)} %pad_add_fusion.refs_0_.where_ref, f32[3,16,128]{2,1,0:T(8,128)S(1)} %pad_maximum_fusion.2.column_ref, s32[40,128]{1,0:T(8,128)S(1)} %get-tuple-element.50.slot_ref), custom_call_target="tpu_custom_call" | custom-call | tf_op jit(solution)/shard_map/pallas_call | solution.py:500
  43.0 3.9 %collective-permute-done.10.odd_ref = f32[3,16,128]{2,1,0:T(8,128)S(1)} collective-permute-done((f32[3,16,128]{2,1,0:T(8,128)S(1)}, f32[3,16,128]{2,1,0:T(8,128)S(1)}, u32[]{:S(2)}, u32[]{:S(2)}) %collective-permute-start.10) | collective-permute-done | bytes 24608 | tf_op jit(solution)/shard_map/ppermute | solution.py:528
  46.9 1.6 %shard_map.171 = f32[3,1,3452]{2,1,0:T(1,128)} custom-call(s32[2]{0:T(128)S(1)} %pad_add_fusion.refs_0_.where_ref, f32[3,16,128]{2,1,0:T(8,128)S(1)} %collective-permute-done.11.even_ref, f32[3,16,128]{2,1,0:T(8,128)S(1)} %collective-permute-done.10.odd_ref, s32[40,128]{1,0:T(8,128)S(1)} %get-tuple-element.50.slot_ref, ...), custom_call_target="tpu_custom_call" | custom-call | tf_op jit(solution)/shard_map/pallas_call | solution.py:500
  (40 shorter events, 0.1 us)
Async XLA Ops:
  2.3 5.7 %copy-start.12 = (f32[24,128]{1,0:T(8,128)S(1)}, f32[24,128]{1,0:T(8,128)}, u32[]{:S(2)}) copy-start(f32[24,128]{1,0:T(8,128)} %shard_map.166) | copy-start | bytes 36868
  2.3 4.9 %collective-permute-start = (f32[24,128]{1,0:T(8,128)}, f32[24,128]{1,0:T(8,128)S(1)}, u32[]{:S(2)}, u32[]{:S(2)}) collective-permute-start(f32[24,128]{1,0:T(8,128)} %shard_map.166), channel_id=1, source_target_pairs={{0,1},{1,0},{2,3},{3,2},{4,5},{5,4},{6,7},{7,6},{8,9},{9,8},{10,11... | collective-permute-start | bytes 36872 | tf_op jit(solution)/shard_map/ppermute | solution.py:528
  4.1 3.9 %collective-permute-start.1 = (f32[24,128]{1,0:T(8,128)}, f32[24,128]{1,0:T(8,128)S(1)}, u32[]{:S(2)}, u32[]{:S(2)}) collective-permute-start(f32[24,128]{1,0:T(8,128)} %shard_map.166), channel_id=1, source_target_pairs={{0,32},{1,33},{2,34},{3,35},{4,36},{5,37},{6,38},{7,39},{8,40},{9,... | collective-permute-start | bytes 36872 | tf_op jit(solution)/shard_map/ppermute | solution.py:528
  8.0 5.1 %copy-start.9 = (s32[1,1,512]{2,1,0:T(1,128)S(1)}, s32[1,1,512]{2,1,0:T(1,128)}, u32[]{:S(2)}) copy-start(s32[1,1,512]{2,1,0:T(1,128)} %param.19) | copy-start | bytes 6148
  8.0 5.1 %copy-start.7 = (s32[1,1,8,64]{3,2,1,0:T(8,128)S(1)}, s32[1,1,8,64]{3,2,1,0:T(8,128)}, u32[]{:S(2)}) copy-start(s32[1,1,8,64]{3,2,1,0:T(8,128)} %param.17) | copy-start | bytes 6148
  8.0 4.5 %copy-start.13 = (bf16[256]{0:T(256)(128)(2,1)S(1)}, bf16[256]{0:T(256)(128)(2,1)}, u32[]{:S(2)}) copy-start(bf16[256]{0:T(256)(128)(2,1)} %param.29) | copy-start | bytes 1540
  8.0 5.1 %copy-start.3 = (s32[1,1,8,1260]{3,2,1,0:T(8,128)S(1)}, s32[1,1,8,1260]{3,2,1,0:T(8,128)}, u32[]{:S(2)}) copy-start(s32[1,1,8,1260]{3,2,1,0:T(8,128)} %param.18) | copy-start | bytes 120964
  8.0 5.1 %copy-start.4 = (f32[3,1,1,2940]{3,2,1,0:T(1,128)S(1)}, f32[3,1,1,2940]{3,2,1,0:T(1,128)}, u32[]{:S(2)}) copy-start(f32[3,1,1,2940]{3,2,1,0:T(1,128)} %param.15) | copy-start | bytes 105844
  8.0 5.1 %copy-start.6 = (s32[1,1,2940]{2,1,0:T(1,128)S(1)}, s32[1,1,2940]{2,1,0:T(1,128)}, u32[]{:S(2)}) copy-start(s32[1,1,2940]{2,1,0:T(1,128)} %param.16) | copy-start | bytes 35284
  8.0 7.1 %collective-permute-start.2 = (f32[3,24,128]{2,1,0:T(8,128)S(1)}, f32[3,24,128]{2,1,0:T(8,128)S(1)}, u32[]{:S(2)}, u32[]{:S(2)}) collective-permute-start(f32[3,24,128]{2,1,0:T(8,128)S(1)} %pad_maximum_fusion.1.refs_4_.refs_1_), channel_id=1, source_target_pairs={{0,32},{1,2},{2,1},{3,4},{4,3},{5,6},{6,5},{7,8},{8,7},{9,10},{10,... | collective-permute-start | bytes 110600 | tf_op jit(solution)/shard_map/ppermute | solution.py:528
  12.4 2.8 %collective-permute-start.3 = (f32[3,24,128]{2,1,0:T(8,128)S(1)}, f32[3,24,128]{2,1,0:T(8,128)S(1)}, u32[]{:S(2)}, u32[]{:S(2)}) collective-permute-start(f32[3,24,128]{2,1,0:T(8,128)S(1)} %pad_maximum_fusion.1.refs_4_.refs_1_), channel_id=1, source_target_pairs={{0,1},{1,0},{2,3},{3,2},{4,5},{5,4},{6,7},{7,6},{8,9},{9,8},{10,11... | collective-permute-start | bytes 110600 | tf_op jit(solution)/shard_map/ppermute | solution.py:528
  13.2 15.4 %copy-start.5 = (bf16[256,256]{1,0:T(8,128)(2,1)S(1)}, bf16[256,256]{1,0:T(8,128)(2,1)}, u32[]{:S(2)}) copy-start(bf16[256,256]{1,0:T(8,128)(2,1)} %refs_9_.1) | copy-start | bytes 393220
  15.1 13.5 %copy-start = (bf16[2,448,256]{2,1,0:T(8,128)(2,1)S(1)}, bf16[2,448,256]{2,1,0:T(8,128)(2,1)}, u32[]{:S(2)}) copy-start(bf16[2,448,256]{2,1,0:T(8,128)(2,1)} %refs_12_.1) | copy-start | bytes 1376260
  16.6 4.8 %collective-permute-start.4 = (f32[3,16,128]{2,1,0:T(8,128)S(1)}, f32[3,16,128]{2,1,0:T(8,128)S(1)}, u32[]{:S(2)}, u32[]{:S(2)}) collective-permute-start(f32[3,16,128]{2,1,0:T(8,128)S(1)} %get-tuple-element.39), channel_id=1, source_target_pairs={{0,1},{1,0},{2,3},{3,2},{4,5},{5,4},{6,7},{7,6},{8,9},{9,8},{10,11... | collective-permute-start | bytes 73736 | tf_op jit(solution)/shard_map/ppermute | solution.py:528
  18.0 3.8 %collective-permute-start.5 = (f32[3,16,128]{2,1,0:T(8,128)S(1)}, f32[3,16,128]{2,1,0:T(8,128)S(1)}, u32[]{:S(2)}, u32[]{:S(2)}) collective-permute-start(f32[3,16,128]{2,1,0:T(8,128)S(1)} %get-tuple-element.40), channel_id=1, source_target_pairs={{0,32},{1,33},{2,34},{3,35},{4,36},{5,37},{6,38},{7,39},{8,40},{9,... | collective-permute-start | bytes 73736 | tf_op jit(solution)/shard_map/ppermute | solution.py:528
  18.8 9.8 %copy-start.2 = (bf16[2,256,192]{1,2,0:T(8,128)(2,1)S(1)}, bf16[2,256,192]{1,2,0:T(8,128)(2,1)}, u32[]{:S(2)}) copy-start(bf16[2,256,192]{1,2,0:T(8,128)(2,1)} %param.27) | copy-start | bytes 589828
  18.9 9.8 %copy-start.1 = (bf16[2,256,192]{1,2,0:T(8,128)(2,1)S(1)}, bf16[2,256,192]{1,2,0:T(8,128)(2,1)}, u32[]{:S(2)}) copy-start(bf16[2,256,192]{1,2,0:T(8,128)(2,1)} %param.26) | copy-start | bytes 589828
  21.8 6.8 %collective-permute-start.6 = (f32[16,128]{1,0:T(8,128)S(1)}, f32[16,128]{1,0:T(8,128)S(1)}, u32[]{:S(2)}, u32[]{:S(2)}) collective-permute-start(f32[16,128]{1,0:T(8,128)S(1)} %get-tuple-element.57), channel_id=1, source_target_pairs={{0,32},{1,2},{2,1},{3,4},{4,3},{5,6},{6,5},{7,8},{8,7},{9,10},{10,... | collective-permute-start | bytes 24584 | tf_op jit(solution)/shard_map/ppermute | solution.py:528
  25.0 3.6 %collective-permute-start.7 = (f32[16,128]{1,0:T(8,128)S(1)}, f32[16,128]{1,0:T(8,128)S(1)}, u32[]{:S(2)}, u32[]{:S(2)}) collective-permute-start(f32[16,128]{1,0:T(8,128)S(1)} %get-tuple-element.56), channel_id=1, source_target_pairs={{0,1},{1,0},{2,3},{3,2},{4,5},{5,4},{6,7},{7,6},{8,9},{9,8},{10,11... | collective-permute-start | bytes 24584 | tf_op jit(solution)/shard_map/ppermute | solution.py:528
  25.1 3.5 %copy-start.8 = (f32[8,256]{1,0:T(8,128)S(1)}, f32[8,256]{1,0:T(8,128)}, u32[]{:S(2)}) copy-start(f32[8,256]{1,0:T(8,128)} %refs_6_.1) | copy-start | bytes 24580
  25.1 3.5 %copy-start.11 = (f32[4,256]{1,0:T(4,128)S(1)}, f32[4,256]{1,0:T(4,128)}, u32[]{:S(2)}) copy-start(f32[4,256]{1,0:T(4,128)} %refs_8_.1) | copy-start | bytes 12292
  25.7 2.9 %copy-start.10 = (f32[4,256]{1,0:T(4,128)S(1)}, f32[4,256]{1,0:T(4,128)}, u32[]{:S(2)}) copy-start(f32[4,256]{1,0:T(4,128)} %refs_7_.1) | copy-start | bytes 12292
  34.6 4.6 %collective-permute-start.8 = (f32[16,128]{1,0:T(8,128)S(1)}, f32[16,128]{1,0:T(8,128)S(1)}, u32[]{:S(2)}, u32[]{:S(2)}) collective-permute-start(f32[16,128]{1,0:T(8,128)S(1)} %shard_map.169), channel_id=1, source_target_pairs={{0,1},{1,0},{2,3},{3,2},{4,5},{5,4},{6,7},{7,6},{8,9},{9,8},{10,11... | collective-permute-start | bytes 24584 | tf_op jit(solution)/shard_map/ppermute | solution.py:528
  36.3 3.7 %collective-permute-start.9 = (f32[16,128]{1,0:T(8,128)S(1)}, f32[16,128]{1,0:T(8,128)S(1)}, u32[]{:S(2)}, u32[]{:S(2)}) collective-permute-start(f32[16,128]{1,0:T(8,128)S(1)} %shard_map.169), channel_id=1, source_target_pairs={{0,32},{1,33},{2,34},{3,35},{4,36},{5,37},{6,38},{7,39},{8,40},{9,... | collective-permute-start | bytes 24584 | tf_op jit(solution)/shard_map/ppermute | solution.py:528
  40.0 6.9 %collective-permute-start.10 = (f32[3,16,128]{2,1,0:T(8,128)S(1)}, f32[3,16,128]{2,1,0:T(8,128)S(1)}, u32[]{:S(2)}, u32[]{:S(2)}) collective-permute-start(f32[3,16,128]{2,1,0:T(8,128)S(1)} %pad_maximum_fusion.2.column_ref), channel_id=1, source_target_pairs={{0,32},{1,2},{2,1},{3,4},{4,3},{5,6},{6,5},{7,8},{8,7},{9,10},{10,... | collective-permute-start | bytes 73736 | tf_op jit(solution)/shard_map/ppermute | solution.py:528
  41.4 5.4 %collective-permute-start.11 = (f32[3,16,128]{2,1,0:T(8,128)S(1)}, f32[3,16,128]{2,1,0:T(8,128)S(1)}, u32[]{:S(2)}, u32[]{:S(2)}) collective-permute-start(f32[3,16,128]{2,1,0:T(8,128)S(1)} %pad_maximum_fusion.2.column_ref), channel_id=1, source_target_pairs={{0,1},{1,0},{2,3},{3,2},{4,5},{5,4},{6,7},{7,6},{8,9},{9,8},{10,11... | collective-permute-start | bytes 73736 | tf_op jit(solution)/shard_map/ppermute | solution.py:528
